TPU v7x, 128 devices: a whole 4x4x4 slice. The times are simulated.
128 devices in a mesh: dp: 16 (over x_hi, z, core), mp: 8 (over y, x_lo).
Axes of the slice: x: 4 (x_hi: 2, x_lo: 2; x = x_hi * 2 + x_lo), y: 4, z: 4, core: 2. Of those that a mesh axis runs over, the one named last changes fastest.
Arguments:
- hidden: bfloat16 [32, 1024, 1536], P('dp', 'mp'), may hold values from -6 to 6
- segments: int32 [32, 1024], P('dp'), may hold values from 0 to 4, as said below
- cotangent: bfloat16 [32, 1024, 1536], P('dp', 'mp'), may hold values from -6 to 6
- norm_gain: bfloat16 [1536], P(('dp', 'mp')), may hold values from 0.5 to 1.5
- w_z: bfloat16 [1536, 3072], P('dp', 'mp'), may hold values from -0.15625 to 0.15625
- w_x: bfloat16 [1536, 3072], P('dp', 'mp'), may hold values from -0.15625 to 0.15625
- w_dt: bfloat16 [1536, 48], P('dp', 'mp'), may hold values from -0.15625 to 0.15625
- w_bc: bfloat16 [1536, 256], P(('dp', 'mp')), may hold values from -0.15625 to 0.15625
- conv_x: bfloat16 [4, 3072], P(None, ('mp', 'dp')), may hold values from -3 to 3
- conv_x_bias: bfloat16 [3072], P(('mp', 'dp')), may hold values from -0.5 to 0.5
- conv_bc: bfloat16 [4, 256], P(None, ('dp', 'mp')), may hold values from -3 to 3
- conv_bc_bias: bfloat16 [256], P(('dp', 'mp')), may hold values from -0.5 to 0.5
- a_log: float32 [48], P('mp'), may hold values from 0 to 2.5
- d_skip: float32 [48], P('mp'), may hold values from 0.5 to 1.5
- dt_bias: float32 [48], P('mp'), may hold values from -7 to -2
- out_gain: bfloat16 [3072], P(('mp', 'dp')), may hold values from 0.5 to 1.5
- w_out: bfloat16 [3072, 1536], P('mp', 'dp'), may hold values from -0.109375 to 0.109375
Outputs:
- mixed: bfloat16 [32, 1024, 1536], P('dp', 'mp')
- grad_hidden: float32 [32, 1024, 1536], P('dp', 'mp')
- grad_norm_gain: float32 [1536], P(('dp', 'mp'))
- grad_w_z: float32 [1536, 3072], P('dp', 'mp')
- grad_w_x: float32 [1536, 3072], P('dp', 'mp')
- grad_w_dt: float32 [1536, 48], P('dp', 'mp')
- grad_w_bc: float32 [1536, 256], P(('dp', 'mp'))
- grad_conv_x: float32 [4, 3072], P(None, ('mp', 'dp'))
- grad_conv_x_bias: float32 [3072], P(('mp', 'dp'))
- grad_conv_bc: float32 [4, 256], P(None, ('dp', 'mp'))
- grad_conv_bc_bias: float32 [256], P(('dp', 'mp'))
- grad_a_log: float32 [48], P('mp')
- grad_d_skip: float32 [48], P('mp')
- grad_dt_bias: float32 [48], P('mp')
- grad_out_gain: float32 [3072], P(('mp', 'dp'))
- grad_w_out: float32 [3072, 1536], P('mp', 'dp')
Inputs may be any that keep to these rules, and one draw needn't show every extreme that they name: `segments`: within each sequence the numbers start at 0 and rise by one at the first token of each document; every document has 200 to 1024 tokens.
All inputs are finite; a program needn't handle non-finite values.
Results may differ from a plain program's by a relative error of at most 0.012.
Values may be sent and summed in bfloat16 or wider, within the bound.
A program may use at most 192 MiB of HBM per device.

v0:
```python
import jax
import jax.numpy as jnp
from jax import lax
from jax.sharding import PartitionSpec as P

BLOCK = 256


epsilon = 1e-05


def causal_conv(values, kernel, offset, seg_ids):
    length = values.shape[0]
    tap_count = kernel.shape[0]
    result = offset[None, :] + kernel[tap_count - 1][None, :] * values
    for shift_by in range(1, tap_count):
        moved = jnp.concatenate(
            [jnp.zeros((shift_by, values.shape[1]), values.dtype), values[: length - shift_by]], 0
        )
        moved_ids = jnp.concatenate(
            [jnp.full((shift_by,), -1, jnp.int32), seg_ids[: length - shift_by]], 0
        )
        keep_mask = jnp.where(moved_ids == seg_ids, 1.0, 0.0).astype(values.dtype)
        result = result + kernel[tap_count - 1 - shift_by][None, :] * moved * keep_mask[:, None]
    return result


def state_space(x_heads, step_size, log_decay, b_mat, c_mat, seg_ids):
    length, head_count, head_dim = x_heads.shape
    blocks = length // BLOCK
    highest = lax.Precision.HIGHEST

    def by_block(values):
        return values.reshape((blocks, BLOCK) + values.shape[1:])

    def one_block(carry, pieces):
        carried, last_id = carry
        x_blk, step_blk, decay_blk, b_blk, c_blk, id_blk = pieces
        cumulative = jnp.cumsum(decay_blk, axis=0)
        position = jnp.arange(BLOCK)
        same_doc = (id_blk[:, None] == id_blk[None, :]) & (position[:, None] >= position[None, :])
        decay_gaps = cumulative[:, None, :] - cumulative[None, :, :]
        decay_mat = jnp.exp(jnp.where(same_doc[:, :, None], decay_gaps, -10000.0))
        scores = jnp.dot(c_blk, b_blk.T, precision=highest)
        mix_weights = decay_mat * scores[:, :, None] * step_blk[None, :, :]
        inside = jnp.einsum("tsh,shp->thp", mix_weights, x_blk, precision=highest)
        enter_rate = (
            jnp.exp(cumulative)
            * jnp.where(id_blk == last_id, 1.0, 0.0).astype(x_heads.dtype)[:, None]
        )
        from_state = (
            jnp.einsum("tn,hpn->thp", c_blk, carried, precision=highest) * enter_rate[:, :, None]
        )
        tail_id = id_blk[BLOCK - 1]
        leave_rate = (
            jnp.exp(
                jnp.where(
                    (id_blk == tail_id)[:, None],
                    cumulative[BLOCK - 1][None, :] - cumulative,
                    -10000.0,
                )
            )
            * step_blk
        )
        keep_rate = jnp.exp(cumulative[BLOCK - 1]) * jnp.where(tail_id == last_id, 1.0, 0.0).astype(
            x_heads.dtype
        )
        carried = carried * keep_rate[:, None, None] + jnp.einsum(
            "sh,shp,sn->hpn", leave_rate, x_blk, b_blk, precision=highest
        )
        return ((carried, tail_id), inside + from_state)

    initial = (
        jnp.zeros((head_count, head_dim, b_mat.shape[1]), x_heads.dtype),
        jnp.array(-1, jnp.int32),
    )
    ignored, outputs = lax.scan(
        jax.checkpoint(one_block),
        initial,
        (
            by_block(x_heads),
            by_block(step_size),
            by_block(log_decay),
            by_block(b_mat),
            by_block(c_mat),
            by_block(seg_ids),
        ),
    )
    return outputs.reshape(length, head_count, head_dim)


def ssd_mixer(
    z_in,
    x_in,
    dt_in,
    bc_in,
    kern_x,
    bias_x,
    kern_bc,
    bias_bc,
    log_rate,
    skip_gain,
    step_bias,
    seg_ids,
):
    length = z_in.shape[0]
    head_count = dt_in.shape[1]
    x_act = jax.nn.silu(causal_conv(x_in, kern_x, bias_x, seg_ids))
    bc_act = jax.nn.silu(causal_conv(bc_in, kern_bc, bias_bc, seg_ids))
    state_size = bc_act.shape[1] // 2
    step_size = jax.nn.softplus(dt_in + step_bias)
    log_decay = -jnp.exp(log_rate) * step_size
    x_heads = x_act.reshape(length, head_count, -1)
    y_heads = (
        state_space(
            x_heads, step_size, log_decay, bc_act[:, :state_size], bc_act[:, state_size:], seg_ids
        )
        + skip_gain[None, :, None] * x_heads
    )
    return y_heads.reshape(length, -1) * jax.nn.silu(z_in)


def local(
    hidden,
    segments,
    cotangent,
    norm_gain,
    w_z,
    w_x,
    w_dt,
    w_bc,
    conv_x,
    conv_x_bias,
    conv_bc,
    conv_bc_bias,
    a_log,
    d_skip,
    dt_bias,
    out_gain,
    w_out,
):
    groups = lax.axis_size("mp")
    seq_count, own_len, model_width = hidden.shape
    length = own_len * groups
    all_rows = seq_count * length
    own_count = seq_count * own_len
    side_parts = (
        lax.all_gather(w_z, "dp", axis=0, tiled=True),
        lax.all_gather(w_x, "dp", axis=0, tiled=True),
        lax.all_gather(w_dt, "dp", axis=0, tiled=True),
        lax.all_gather(conv_x, "dp", axis=1, tiled=True),
        lax.all_gather(conv_x_bias, "dp", axis=0, tiled=True),
        lax.all_gather(out_gain, "dp", axis=0, tiled=True),
        lax.all_gather(w_out, "dp", axis=1, tiled=True),
    )
    full_z, full_x, full_dt, kernel_x, offset_x, gain_out, full_out = side_parts
    shared_parts = (
        lax.all_gather(w_bc, ("dp", "mp"), axis=0, tiled=True),
        lax.all_gather(norm_gain, ("dp", "mp"), axis=0, tiled=True),
        lax.all_gather(conv_bc, ("dp", "mp"), axis=1, tiled=True),
        lax.all_gather(conv_bc_bias, ("dp", "mp"), axis=0, tiled=True),
    )
    full_bc, gain_in, kernel_bc, offset_bc = shared_parts
    rows_own = hidden.astype(jnp.float32).reshape(own_count, model_width)
    inv_rms = lax.rsqrt(jnp.mean(rows_own * rows_own, -1, keepdims=True) + epsilon)
    gain_in_f = gain_in.astype(jnp.float32)
    normed_own = (rows_own * inv_rms * gain_in_f).astype(jnp.bfloat16)
    normed = lax.all_gather(
        normed_own.reshape(seq_count, own_len, model_width), "mp", axis=1, tiled=True
    ).reshape(all_rows, model_width)
    z_in = jnp.dot(normed, full_z, preferred_element_type=jnp.float32)
    x_in = jnp.dot(normed, full_x, preferred_element_type=jnp.float32)
    dt_in = jnp.dot(normed, full_dt, preferred_element_type=jnp.float32)
    bc_in = jnp.dot(normed, full_bc, preferred_element_type=jnp.float32)

    def local_mix(
        z_val,
        x_val,
        dt_val,
        bc_val,
        kern_x,
        bias_x,
        kern_bc,
        bias_bc,
        log_rate,
        skip_gain,
        step_bias,
    ):

        def per_seq(values):
            return values.reshape((seq_count, length) + values.shape[1:])

        gated_seq = jax.vmap(
            ssd_mixer, in_axes=(0, 0, 0, 0, None, None, None, None, None, None, None, 0)
        )(
            per_seq(z_val),
            per_seq(x_val),
            per_seq(dt_val),
            per_seq(bc_val),
            kern_x,
            bias_x,
            kern_bc,
            bias_bc,
            log_rate,
            skip_gain,
            step_bias,
            segments,
        )
        return gated_seq.reshape(all_rows, -1)

    gated, mix_back = jax.vjp(
        local_mix,
        z_in,
        x_in,
        dt_in,
        bc_in,
        kernel_x.astype(jnp.float32),
        offset_x.astype(jnp.float32),
        kernel_bc.astype(jnp.float32),
        offset_bc.astype(jnp.float32),
        a_log,
        d_skip,
        dt_bias,
    )
    sq_local = jnp.sum(gated * gated, -1)
    sq_total = lax.psum(sq_local, "mp")
    inner_total = gated.shape[1] * groups
    out_scale = lax.rsqrt(sq_total / inner_total + epsilon)
    gain_out_f = gain_out.astype(jnp.float32)
    out_normed = (gated * out_scale[:, None] * gain_out_f).astype(jnp.bfloat16)
    partial_out = jnp.dot(out_normed, full_out, preferred_element_type=jnp.float32).reshape(
        seq_count, length, model_width
    )
    out_rows = lax.psum_scatter(
        partial_out.astype(jnp.bfloat16), "mp", scatter_dimension=1, tiled=True
    ).astype(jnp.float32)
    block_out = (hidden.astype(jnp.float32) + out_rows).astype(jnp.bfloat16)
    back_z, back_x, back_dt, back_out = (
        lax.all_gather(w_z, "dp", axis=0, tiled=True),
        lax.all_gather(w_x, "dp", axis=0, tiled=True),
        lax.all_gather(w_dt, "dp", axis=0, tiled=True),
        lax.all_gather(w_out, "dp", axis=1, tiled=True),
    )
    cot_rows = lax.all_gather(cotangent, "mp", axis=1, tiled=True).reshape(all_rows, model_width)
    grad_out_normed = jnp.dot(cot_rows, back_out.T, preferred_element_type=jnp.float32)
    grad_w_out = jnp.dot(out_normed.T, cot_rows, preferred_element_type=jnp.float32)
    grad_out_gain = jnp.sum(grad_out_normed * gated * out_scale[:, None], 0)
    grad_scaled = grad_out_normed * gain_out_f
    inner_local = jnp.sum(grad_scaled * gated, -1)
    inner_all = lax.psum(inner_local, "mp")
    grad_gated = (
        out_scale[:, None] * grad_scaled
        - gated * (out_scale * out_scale * out_scale * inner_all / inner_total)[:, None]
    )
    (
        grad_z,
        grad_x,
        grad_dt,
        grad_bc_part,
        grad_kern_x,
        grad_bias_x,
        grad_kern_bc,
        grad_bias_bc,
        grad_log_rate,
        grad_skip,
        grad_step_bias,
    ) = mix_back(grad_gated)
    z_low = grad_z.astype(jnp.bfloat16)
    x_low = grad_x.astype(jnp.bfloat16)
    dt_low = grad_dt.astype(jnp.bfloat16)
    grad_w_z = jnp.dot(normed.T, z_low, preferred_element_type=jnp.float32)
    grad_w_x = jnp.dot(normed.T, x_low, preferred_element_type=jnp.float32)
    grad_w_dt = jnp.dot(normed.T, dt_low, preferred_element_type=jnp.float32)
    partial_in = jnp.dot(z_low, back_z.T, preferred_element_type=jnp.float32)
    partial_in = partial_in + jnp.dot(x_low, back_x.T, preferred_element_type=jnp.float32)
    partial_in = partial_in + jnp.dot(dt_low, back_dt.T, preferred_element_type=jnp.float32)
    rows_in = lax.psum_scatter(
        partial_in.reshape(seq_count, length, model_width), "mp", scatter_dimension=1, tiled=True
    )
    bc_part = grad_bc_part.reshape(seq_count, length, -1)
    bc_rows = lax.psum_scatter(bc_part, "mp", scatter_dimension=1, tiled=True)
    bc_low = bc_rows.reshape(own_count, -1).astype(jnp.bfloat16)
    grad_w_bc = jnp.dot(normed_own.T, bc_low, preferred_element_type=jnp.float32)
    grad_normed = rows_in.reshape(own_count, model_width) + jnp.dot(
        bc_low, full_bc.T, preferred_element_type=jnp.float32
    )
    grad_hat = grad_normed * gain_in_f
    grad_gain_in = jnp.sum(grad_normed * rows_own * inv_rms, 0)
    grad_local = inv_rms * grad_hat - rows_own * (inv_rms * inv_rms * inv_rms) * jnp.mean(
        grad_hat * rows_own, -1, keepdims=True
    )
    grad_hidden = (
        cotangent.astype(jnp.float32).reshape(own_count, model_width) + grad_local
    ).reshape(seq_count, own_len, model_width)
    side_grads = (
        lax.psum_scatter(grad_w_z, "dp", scatter_dimension=0, tiled=True),
        lax.psum_scatter(grad_w_x, "dp", scatter_dimension=0, tiled=True),
        lax.psum_scatter(grad_w_dt, "dp", scatter_dimension=0, tiled=True),
        lax.psum_scatter(grad_kern_x, "dp", scatter_dimension=1, tiled=True),
        lax.psum_scatter(grad_bias_x, "dp", scatter_dimension=0, tiled=True),
        lax.psum_scatter(grad_out_gain, "dp", scatter_dimension=0, tiled=True),
        lax.psum_scatter(grad_w_out, "dp", scatter_dimension=1, tiled=True),
    )
    shared_grads = (
        lax.psum_scatter(grad_w_bc, ("dp", "mp"), scatter_dimension=0, tiled=True),
        lax.psum_scatter(grad_gain_in, ("dp", "mp"), scatter_dimension=0, tiled=True),
        lax.psum_scatter(grad_kern_bc, ("dp", "mp"), scatter_dimension=1, tiled=True),
        lax.psum_scatter(grad_bias_bc, ("dp", "mp"), scatter_dimension=0, tiled=True),
    )
    head_grads = lax.psum((grad_log_rate, grad_skip, grad_step_bias), "dp")
    return (
        block_out,
        grad_hidden,
        shared_grads[1],
        side_grads[0],
        side_grads[1],
        side_grads[2],
        shared_grads[0],
        side_grads[3],
        side_grads[4],
        shared_grads[2],
        shared_grads[3],
        head_grads[0],
        head_grads[1],
        head_grads[2],
        side_grads[5],
        side_grads[6],
    )


def solution(mesh):
    in_specs = (
        P("dp", "mp", None),
        P("dp", None),
        P("dp", "mp", None),
        P(("dp", "mp")),
        P("dp", "mp"),
        P("dp", "mp"),
        P("dp", "mp"),
        P(("dp", "mp"), None),
        P(None, ("mp", "dp")),
        P(("mp", "dp")),
        P(None, ("dp", "mp")),
        P(("dp", "mp")),
        P("mp"),
        P("mp"),
        P("mp"),
        P(("mp", "dp")),
        P("mp", "dp"),
    )
    out_specs = (
        P("dp", "mp", None),
        P("dp", "mp", None),
        P(("dp", "mp")),
        P("dp", "mp"),
        P("dp", "mp"),
        P("dp", "mp"),
        P(("dp", "mp"), None),
        P(None, ("mp", "dp")),
        P(("mp", "dp")),
        P(None, ("dp", "mp")),
        P(("dp", "mp")),
        P("mp"),
        P("mp"),
        P("mp"),
        P(("mp", "dp")),
        P("mp", "dp"),
    )
    return jax.shard_map(local, mesh=mesh, in_specs=in_specs, out_specs=out_specs, check_vma=False)
```

profile of v0, /device:TPU:0, one launch (start us, length us, event | category | flops | bytes accessed | tf_op | source)
XLA Modules:
  0.0 2041.1 jit_solution(18413778325874971776)
XLA Ops:
  9.0 68.4 %all-reduce.41 = (bf16[1536]{0:T(1024)(128)(2,1)S(1)}, bf16[256]{0:T(256)(128)(2,1)S(1)}) all-reduce(bf16[1536]{0:T(1024)(128)(2,1)S(1)} %dynamic-update-slice, bf16[256]{0:T(256)(128)(2,1)S(1)} %dynamic-update-slice.2), channel_id=1, replica_groups=mesh['dp'=16,'mp'=8] {'dp','mp'}, use_global_device_ids=true, to_apply=%add.27 | all-reduce | flops 1792 | bytes 7168
  85.7 319.6 %all-gather.3 = bf16[128,12,256]{2,1,0:T(8,128)(2,1)S(1)} all-gather(bf16[1,12,256]{2,1,0:T(8,128)(2,1)S(1)} %bitcast.547), channel_id=1, replica_groups=mesh['dp'=16,'mp'=8] {'dp','mp'}, dimensions={0}, use_global_device_ids=true | all-gather | bytes 792576 | tf_op jit(solution)/shard_map/all_gather | solution.py:158
  405.5 309.6 %all-gather.2 = bf16[128,2,4]{2,1,0:T(2,128)(2,1)S(1)} all-gather(bf16[1,2,4]{2,1,0:T(2,128)(2,1)S(1)} %bitcast.555), channel_id=1, replica_groups=mesh['dp'=16,'mp'=8] {'dp','mp'}, dimensions={0}, use_global_device_ids=true | all-gather | bytes 2064 | tf_op jit(solution)/shard_map/all_gather | solution.py:160
  717.0 33.2 %all-reduce.42 = (bf16[384]{0:T(512)(128)(2,1)S(1)}, bf16[384]{0:T(512)(128)(2,1)S(1)}) all-reduce(bf16[384]{0:T(512)(128)(2,1)S(1)} %dynamic-update-slice.1, bf16[384]{0:T(512)(128)(2,1)S(1)} %dynamic-update-slice.3), channel_id=1, replica_groups=mesh['dp'=16,'mp'=8] {'dp'}, use_global_device_ids=true, to_apply=%add.28 | all-reduce | flops 768 | bytes 3072
  750.7 19.0 all-gather.1
  770.4 21.0 %all-gather = bf16[16,96,6]{1,2,0:T(8,128)(2,1)S(1)} all-gather(bf16[1,96,6]{1,2,0:T(8,128)(2,1)S(1)} %bitcast.553), channel_id=1, replica_groups=mesh['dp'=16,'mp'=8] {'dp'}, dimensions={0}, use_global_device_ids=true | all-gather | bytes 19584 | tf_op jit(solution)/shard_map/all_gather | solution.py:150
  804.8 5.8 fusion.118
  822.9 5.2 fusion.125
  833.4 94.1 %while.45 = (s32[]{:T(128)}, f32[2,6,64,128]{3,2,1,0:T(8,128)S(1)}, s32[2]{0:T(128)S(1)}, f32[4,2,256,6,64]{2,4,3,1,0:T(8,128)}, f32[4,2,6,64,128]{4,3,2,1,0:T(8...) while((s32[]{:T(128)}, f32[2,6,64,128]{3,2,1,0:T(8,128)S(1)}, ...), condition=%wide.region_4.5_spmd.clone, body=%wide.region_1.4_spmd.clone.sunk | while | flops 1414247936 | bytes 8913685 | solution.py:77
  842.1 4.9 fusion.226
  865.5 4.9 fusion.226
  888.9 4.9 fusion.226
  912.4 4.9 fusion.226
  927.6 6.3 copy.398
  933.9 5.2 reshape.602
  942.9 11.3 multiply_reduce_fusion.8
  954.3 8.6 copy.401
  962.9 17.6 psum.35
  980.6 9.9 fusion.99
  990.4 17.1 psum.36
  1007.6 8.1 multiply_reduce_fusion.3
  1026.5 226.3 %while.46 = (s32[]{:T(128)}, f32[2,6,64,128]{3,2,1,0:T(8,128)S(1)}, f32[4,2,256,6,64]{2,4,3,1,0:T(8,128)}, f32[4,2,256,6]{2,3,1,0:T(8,128)}, f32[4,2,256,6]{2,1,...) while((s32[]{:T(128)}, f32[2,6,64,128]{3,2,1,0:T(8,128)S(1)}, ...), condition=%wide.region_22.23_spmd.clone, body=%wide.region_10.22_spmd.clone.sunk | while | flops 3338699264 | bytes 28333604 | solution.py:77
  1048.4 6.1 fusion.248
  1060.7 15.1 reduce-window.74
  1077.5 4.8 fusion.251
  1104.9 6.1 fusion.248
  1117.2 15.1 reduce-window.74
  1161.4 6.1 fusion.248
  1173.7 15.1 reduce-window.74
  1217.9 6.1 fusion.248
  1230.2 15.1 reduce-window.74
  1262.1 5.7 convolution_bitcast_fusion.6
  1267.9 6.7 convolution_convert_fusion
  1280.2 5.6 reshape.609
  1302.5 6.6 fusion.142
  1309.1 11.4 add_add_fusion
  1321.9 7.8 convolution_bitcast_fusion.3
  1329.7 8.7 convolution_bitcast_fusion.2
  1338.5 7.6 convolution_bitcast_fusion.4
  1348.9 339.4 %fusion.2 = f32[16,256]{1,0:T(8,128)S(1)} fusion(f32[1536,256]{1,0:T(8,128)} %convolution_bitcast_fusion.5), kind=kCustom, calls=%all-reduce-scatter | all-reduce-scatter fusion | flops 524289 | bytes 1589248
  1691.8 4.9 collective-permute-start.31
  1707.7 6.2 collective-permute-start.12
  1713.9 5.1 collective-permute-start.13
  1761.5 5.5 collective-permute-start.3
  1771.7 66.5 %all-reduce.40 = (f32[4,384]{1,0:T(4,128)S(1)}, f32[384]{0:T(512)S(1)}, f32[6]{0:T(128)}, f32[6]{0:T(128)}, f32[6]{0:T(128)}, /*index=5*/f32[384]{0:T(512)S(1)}) all-reduce(f32[4,384]{1,0:T(4,128)S(1)} %pad_add_fusion, f32[384]{0:T(512)S(1)} %get-tuple-element.827, ...), channel_id=10, replica_groups=mesh['dp'=16,'mp'=8] {'dp'}, use_global_device_ids=true, to_apply=%region_36.37.clone | all-reduce | flops 2322 | bytes 18576
  1859.8 74.6 %all-reduce.39 = (f32[1536]{0:T(1024)S(1)}, f32[4,256]{1,0:T(4,128)S(1)}, f32[256]{0:T(256)S(1)}) all-reduce(f32[1536]{0:T(1024)S(1)} %get-tuple-element.829, f32[4,256]{1,0:T(4,128)S(1)} %pad_add_fusion.1, f32[256]{0:T(256)S(1)} %get-tuple-element.831), channel_id=5, replica_groups=mesh['dp'=16,'mp'=8] {'dp','mp'}, use_global_device_ids=true, to_apply=%region_27.28.clone | all-reduce | flops 2816 | bytes 22528
  1938.0 19.6 reduce-scatter.24.cloned.1.call-done
  1957.6 76.4 %reduce-scatter.20.cloned.1.call-done = f32[96,384]{1,0:T(8,128)} async-done(((f32[1536,384]{1,0:T(8,128)}), f32[96,384]{1,0:T(8,128)}) %reduce-scatter.20.cloned.1.call-update) | async-done | bytes 147472 | tf_op jit(solution)/shard_map/reduce_scatter | solution.py:296
  (884 shorter events, 387.8 us)
Async XLA Ops:
  7.2 787.9 %all-gather.10.cloned.1.call-start = ((), (), s32[]{:S(2)}) async-start(), calls=%async_computation.7 | async-start | bytes 7077888 | tf_op jit(solution)/shard_map/all_gather | solution.py:168
  82.2 688.2 %copy-start.91 = (bf16[96,6]{0,1:T(8,128)(2,1)S(1)}, bf16[96,6]{0,1:T(8,128)(2,1)}, u32[]{:S(2)}) copy-start(bf16[96,6]{0,1:T(8,128)(2,1)} %param.27) | copy-start | bytes 3460
  82.2 709.9 %copy-start.100 = (f32[6]{0:T(128)S(1)}, f32[6]{0:T(128)}, u32[]{:S(2)}) copy-start(f32[6]{0:T(128)} %param.33) | copy-start | bytes 76
  82.2 710.4 %copy-start.51 = (s32[2,1024]{1,0:T(2,128)S(1)}, s32[2,1024]{1,0:T(2,128)}, u32[]{:S(2)}) copy-start(s32[2,1024]{1,0:T(2,128)} %param.22) | copy-start | bytes 24580
  82.2 722.5 %all-gather.12.cloned.1.call-start = ((), (), s32[]{:S(2)}) async-start(), calls=%async_computation.8 | async-start | bytes 1253376 | tf_op jit(solution)/shard_map/all_gather | solution.py:149
  83.0 859.9 %all-gather.14.cloned.1.call-start = ((), (), s32[]{:S(2)}) async-start(), calls=%async_computation.9 | async-start | bytes 1253376 | tf_op jit(solution)/shard_map/all_gather | solution.py:148
  83.7 709.9 %copy-start.97 = (f32[6]{0:T(128)S(1)}, f32[6]{0:T(128)}, u32[]{:S(2)}) copy-start(f32[6]{0:T(128)} %param.34) | copy-start | bytes 76
  83.7 870.5 %all-gather.18.cloned.1.call-start = ((), (), s32[]{:S(2)}) async-start(), calls=%async_computation.12 | async-start | bytes 7077888 | tf_op jit(solution)/shard_map/all_gather | solution.py:244
  85.0 895.5 %all-gather.16.cloned.1.call-start = ((), (), s32[]{:S(2)}) async-start(), calls=%async_computation.10 | async-start | bytes 1253376 | tf_op jit(solution)/shard_map/all_gather | solution.py:154
  85.6 1260.6 %reduce-scatter.18.cloned.1.call-start = ((), (), s32[]{:S(2)}) async-start(), calls=%async_computation.14 | async-start | bytes 2359296 | tf_op jit(solution)/shard_map/reduce_scatter | solution.py:281
  1261.6 587.7 %reduce-scatter.26.cloned.1.call-start = ((), (), s32[]{:S(2)}) async-start(), calls=%async_computation.18 | async-start | bytes 835584
  1267.8 587.3 %reduce-scatter.14.cloned.1.call-start = ((), (), s32[]{:S(2)}) async-start(), calls=%async_computation.11 | async-start | bytes 7077888 | tf_op jit(solution)/shard_map/reduce_scatter | solution.py:234
  1274.6 582.8 %reduce-scatter.16.cloned.1.call-start = ((), (), s32[]{:S(2)}) async-start(), calls=%async_computation.13 | async-start | bytes 14155776 | tf_op jit(solution)/shard_map/reduce_scatter | solution.py:277
  1320.5 617.5 %reduce-scatter.22.cloned.1.call-start = ((), (), s32[]{:S(2)}) async-start(), calls=%async_computation.16 | async-start | bytes 2506752 | tf_op jit(solution)/shard_map/reduce_scatter | solution.py:297
  1329.7 627.9 %reduce-scatter.24.cloned.1.call-start = ((), (), s32[]{:S(2)}) async-start(), calls=%async_computation.17 | async-start | bytes 2506752 | tf_op jit(solution)/shard_map/reduce_scatter | solution.py:302
  1338.5 695.5 %reduce-scatter.20.cloned.1.call-start = ((), (), s32[]{:S(2)}) async-start(), calls=%async_computation.15 | async-start | bytes 2506752 | tf_op jit(solution)/shard_map/reduce_scatter | solution.py:296
  1688.4 25.5 %collective-permute-start = (f32[16,256]{1,0:T(8,128)S(1)}, f32[16,256]{1,0:T(8,128)S(1)}, u32[]{:S(2)}, u32[]{:S(2)}) collective-permute-start(f32[16,256]{1,0:T(8,128)S(1)} %fusion.2), channel_id=1, source_target_pairs={{0,1},{1,2},{2,3},{3,4},{4,5},{5,6},{6,7},{7,8},{8,9},{9,10},{10,1... | collective-permute-start | bytes 49160
  1691.8 15.9 collective-permute-start.31
  1696.7 22.3 %collective-permute-start.1 = (f32[16,256]{1,0:T(8,128)S(1)}, f32[16,256]{1,0:T(8,128)S(1)}, u32[]{:S(2)}, u32[]{:S(2)}) collective-permute-start(f32[16,256]{1,0:T(8,128)S(1)} %fusion.2), channel_id=1, source_target_pairs={{0,2},{1,3},{2,4},{3,5},{4,6},{5,7},{6,8},{7,9},{8,10},{9,11},{10,... | collective-permute-start | bytes 49160
  1700.2 21.0 %collective-permute-start.10 = (f32[16,256]{1,0:T(8,128)S(1)}, f32[16,256]{1,0:T(8,128)S(1)}, u32[]{:S(2)}, u32[]{:S(2)}) collective-permute-start(f32[16,256]{1,0:T(8,128)S(1)} %fusion.2), channel_id=1, source_target_pairs={{0,11},{1,12},{2,13},{3,14},{4,15},{5,16},{6,17},{7,18},{8,19},{9,... | collective-permute-start | bytes 49160
  1703.7 21.1 %collective-permute-start.11 = (f32[16,256]{1,0:T(8,128)S(1)}, f32[16,256]{1,0:T(8,128)S(1)}, u32[]{:S(2)}, u32[]{:S(2)}) collective-permute-start(f32[16,256]{1,0:T(8,128)S(1)} %fusion.2), channel_id=1, source_target_pairs={{0,12},{1,13},{2,14},{3,15},{4,16},{5,17},{6,18},{7,19},{8,20},{9,... | collective-permute-start | bytes 49160
  1707.7 20.5 %collective-permute-start.12 = (f32[16,256]{1,0:T(8,128)S(1)}, f32[16,256]{1,0:T(8,128)S(1)}, u32[]{:S(2)}, u32[]{:S(2)}) collective-permute-start(f32[16,256]{1,0:T(8,128)S(1)} %fusion.2), channel_id=1, source_target_pairs={{0,13},{1,14},{2,15},{3,16},{4,17},{5,18},{6,19},{7,20},{8,21},{9,... | collective-permute-start | bytes 49160
  1713.9 15.8 collective-permute-start.13
  1719.0 15.2 collective-permute-start.14
  1721.1 17.4 collective-permute-start.15
  1724.8 15.4 collective-permute-start.16
  1728.3 15.1 collective-permute-start.17
  1729.7 15.9 collective-permute-start.18
  1734.2 13.3 collective-permute-start.19
  1738.6 10.4 collective-permute-start.2
  1740.2 11.0 collective-permute-start.20
  1743.4 9.8 collective-permute-start.21
  1745.6 8.9 collective-permute-start.22
  1747.5 10.4 collective-permute-start.23
  1749.0 10.9 collective-permute-start.24
  1751.2 10.3 collective-permute-start.25
  1753.2 13.9 collective-permute-start.26
  1754.5 13.9 collective-permute-start.27
  1757.9 80.3 %collective-permute-start.28 = (f32[16,256]{1,0:T(8,128)S(1)}, f32[16,256]{1,0:T(8,128)S(1)}, u32[]{:S(2)}, u32[]{:S(2)}) collective-permute-start(f32[16,256]{1,0:T(8,128)S(1)} %fusion.2), channel_id=1, source_target_pairs={{0,29},{1,30},{2,31},{3,32},{4,33},{5,34},{6,35},{7,36},{8,37},{9,... | collective-permute-start | bytes 49160
  1759.9 81.6 %collective-permute-start.29 = (f32[16,256]{1,0:T(8,128)S(1)}, f32[16,256]{1,0:T(8,128)S(1)}, u32[]{:S(2)}, u32[]{:S(2)}) collective-permute-start(f32[16,256]{1,0:T(8,128)S(1)} %fusion.2), channel_id=1, source_target_pairs={{0,30},{1,31},{2,32},{3,33},{4,34},{5,35},{6,36},{7,37},{8,38},{9,... | collective-permute-start | bytes 49160
  1761.5 81.9 %collective-permute-start.3 = (f32[16,256]{1,0:T(8,128)S(1)}, f32[16,256]{1,0:T(8,128)S(1)}, u32[]{:S(2)}, u32[]{:S(2)}) collective-permute-start(f32[16,256]{1,0:T(8,128)S(1)} %fusion.2), channel_id=1, source_target_pairs={{0,4},{1,5},{2,6},{3,7},{4,8},{5,9},{6,10},{7,11},{8,12},{9,13},{1... | collective-permute-start | bytes 49160
  1767.1 77.7 %collective-permute-start.30 = (f32[16,256]{1,0:T(8,128)S(1)}, f32[16,256]{1,0:T(8,128)S(1)}, u32[]{:S(2)}, u32[]{:S(2)}) collective-permute-start(f32[16,256]{1,0:T(8,128)S(1)} %fusion.2), channel_id=1, source_target_pairs={{0,31},{1,32},{2,33},{3,34},{4,35},{5,36},{6,37},{7,38},{8,39},{9,... | collective-permute-start | bytes 49160
  1768.4 77.7 %collective-permute-start.4 = (f32[16,256]{1,0:T(8,128)S(1)}, f32[16,256]{1,0:T(8,128)S(1)}, u32[]{:S(2)}, u32[]{:S(2)}) collective-permute-start(f32[16,256]{1,0:T(8,128)S(1)} %fusion.2), channel_id=1, source_target_pairs={{0,5},{1,6},{2,7},{3,8},{4,9},{5,10},{6,11},{7,12},{8,13},{9,14},{... | collective-permute-start | bytes 49160
  1838.2 12.6 collective-permute-start.5
  1841.5 9.3 collective-permute-start.6
  1843.4 7.4 collective-permute-start.7
  1844.7 6.1 collective-permute-start.8
  1846.0 4.8 collective-permute-start.9
  (152 other events, 7596.3 us)
Sparse Core Ops, SparseCore 0:
  82.3 135.6 all-gather.9
  220.5 47.4 all-gather.11
  270.5 44.1 all-gather.13
  316.1 132.3 all-gather.17
  450.9 45.7 all-gather.15
  1261.8 46.9 reduce-scatter.17
  1312.6 65.3 reduce-scatter.25
  1380.5 148.6 reduce-scatter.13
  1531.7 273.9 reduce-scatter.15
  1810.7 70.4 reduce-scatter.21
  1885.8 71.7 reduce-scatter.23
  1962.6 71.4 reduce-scatter.19
where the time goes:
time: 2050 us; the launch traced here: 2040 us
  blocking collectives  1290 us (63%)
  matrix products  222 us (11%)
  local copies, waits for them, and re-layouts  163 us (8%)
  other arithmetic  161 us (8%)
  waiting for transfers between devices  98.3 us (5%)
  starting transfers between devices  90.8 us (4%)
    unnamed x5, blocking collectives  582 us
    all_gather x1, blocking collectives, local(): lax.all_gather(w_bc, ('dp', 'mp'), axis=0, tiled=True)  320 us
    all_gather x1, blocking collectives, local(): lax.all_gather(conv_bc, ('dp', 'mp'), axis=1, tiled=True)  310 us
    another operation x41, other arithmetic  91.3 us
    unnamed x33, starting transfers between devices  90.2 us
    reduce_scatter x1, waiting for transfers between devices, local(): lax.psum_scatter(grad_w_z, 'dp', scatter_dimension=0, tiled=True)  76.4 us
    dot_general x12, matrix products, one_block(): inside = jnp.einsum('tsh,shp->thp', mix_weights, x_blk, precision=highest)  63 us
  transfers between devices with their start and end apart: 44, of which 2 were waited for; matrix products, arithmetic and copies ran while one was open for 30% of the time, Pallas kernels for 0%

commit v1 on v0

v1 whole, which is shorter than its diff:
```python
import jax
import jax.numpy as jnp
from jax import lax
from jax.experimental import pallas as pl
from jax.experimental.pallas import tpu as pltpu
from jax.sharding import PartitionSpec as P

MESH = pl.DeviceIdType.MESH
EPS = 1e-05
Q = 128
HALO = 8
F32 = jnp.float32
BF16 = jnp.bfloat16
LOG2E = 1.4426950408889634
VMEM_LIMIT = 56 * 1024 * 1024

KEEP = 0
AHEAD = 4
SEG, ENTER, LEAVE, CARRY, SCALE, COEF = 8, 9, 10, 11, 12, 13
STEP_ROWS = 256

BC_TAPS, IN_GAIN, X_TAPS, HEAD_ROWS, SMALL_SHARED, SMALL_ROWS = 0, 10, 24, 60, 24, 64


def dot(a, b, dims=((1,), (0,))):
    return lax.dot_general(a, b, (dims, ((), ())), preferred_element_type=F32)


def dot_exact(a, b, dims=((1,), (0,))):
    return lax.dot_general(
        a, b, (dims, ((), ())), preferred_element_type=F32, precision=lax.Precision.HIGHEST
    )


NT = ((1,), (1,))
TN = ((0,), (0,))


def sigmoid(v):
    return 1.0 / (1.0 + jnp.exp(-v))


def softplus(v):
    return jnp.maximum(v, 0.0) + jnp.log1p(jnp.exp(-jnp.abs(v)))


def wide(small, row, count):
    return jnp.concatenate([small[row + i : row + i + 1] for i in range(count)], 1)


def columns_of(rows16):
    return jnp.concatenate([rows16, jnp.zeros((128 - rows16.shape[0], Q), F32)], 0).T


def lanes_of(tok, lane):
    return tok[:, lane : lane + 1]


def expand(values, width):
    rows = values.shape[0]
    first = lax.broadcasted_iota(jnp.int32, (rows, 128), 1) < 64
    pieces = []
    for pair in range(width // 128):
        a = jnp.broadcast_to(values[:, 2 * pair : 2 * pair + 1], (rows, 128))
        b = jnp.broadcast_to(values[:, 2 * pair + 1 : 2 * pair + 2], (rows, 128))
        pieces.append(jnp.where(first, a, b))
    return jnp.concatenate(pieces, 1)


def head_sums(values):
    width = values.shape[1]
    channel = lax.broadcasted_iota(jnp.int32, (width, 128), 0)
    lane = lax.broadcasted_iota(jnp.int32, (width, 128), 1)
    pick = jnp.where((channel >= lane * 64) & (channel < lane * 64 + 64), 1.0, 0.0).astype(BF16)
    high = values.astype(BF16)
    low = (values - high.astype(F32)).astype(BF16)
    return dot(high, pick) + dot(low, pick)


def rows8(values):
    total = values[0:8]
    for start in range(8, values.shape[0], 8):
        total = total + values[start : start + 8]
    return total


def causal():
    row = lax.broadcasted_iota(jnp.int32, (Q, Q), 0)
    col = lax.broadcasted_iota(jnp.int32, (Q, Q), 1)
    return row >= col


def pair_blocks(values):
    first = lax.broadcasted_iota(jnp.int32, values.shape, 1) < 64
    zero = jnp.zeros_like(values)
    return jnp.concatenate([jnp.where(first, values, zero), jnp.where(first, zero, values)], 0)


def decays(dt, hp, tok):
    step = softplus(dt + hp[2:3])
    rate = -jnp.exp(hp[0:1]) * step
    tri = jnp.where(causal(), 1.0, 0.0)
    cum = dot_exact(tri, rate)
    last = cum[Q - 1 : Q]
    enter = jnp.exp(cum) * lanes_of(tok, ENTER)
    leave = jnp.exp(last - cum) * lanes_of(tok, LEAVE)
    keep = jnp.exp(last) * tok[0:1, CARRY : CARRY + 1]
    cum2 = cum * LOG2E
    return step, rate, cum2, cum2.T, enter, leave, keep


def gaps(cum2, cum2_t, head):
    return jnp.exp2(jnp.minimum(cum2[:, head : head + 1] - cum2_t[head : head + 1, :], 0.0))


def place():
    dp, mp = lax.axis_index("dp"), lax.axis_index("mp")
    return {"xh": dp // 8, "z": (dp // 2) % 4, "c": dp % 2, "y": mp // 2, "xl": mp % 2}


def device(at, **other):
    at = {**at, **other}
    return (at["xh"] * 8 + at["z"] * 2 + at["c"], at["y"] * 2 + at["xl"])


def group_peers(at):
    peers = []
    for dy in range(4):
        for flip in range(2):
            if dy or flip:
                peers.append({**at, "y": (at["y"] + dy) % 4, "xl": (at["xl"] + flip) % 2})
    return peers


def x_peers(at):
    flips = [(0, 1), (1, 0), (1, 1)]
    return [{**at, "xh": (at["xh"] + a) % 2, "xl": (at["xl"] + b) % 2} for a, b in flips]


def z_peers(at):
    return [{**at, "z": (at["z"] + d) % 4} for d in range(1, 4)]


def y_peers(at):
    return [{**at, "y": (at["y"] + d) % 4} for d in range(1, 4)]


def core_peers(at):
    return [{**at, "c": 1 - at["c"]}]


def plane_peers(at):
    peers = z_peers(at)
    for x_peer in x_peers(at):
        peers += [x_peer] + z_peers(x_peer)
    return peers


def greet(peers):
    barrier = pltpu.get_barrier_semaphore()
    for peer in peers:
        pl.semaphore_signal(barrier, inc=1, device_id=device(peer), device_id_type=MESH)
    pl.semaphore_wait(barrier, len(peers))


class Sends:
    def __init__(self, send_sems, recv_sems):
        self.send_sems, self.recv_sems, self.used = send_sems, recv_sems, 0

    def make(self, source, target, peer):
        slot = self.used
        self.used += 1
        return pltpu.make_async_remote_copy(
            src_ref=source,
            dst_ref=target,
            send_sem=self.send_sems.at[slot],
            recv_sem=self.recv_sems.at[slot],
            device_id=device(peer),
            device_id_type=MESH,
        )

    def start(self, source, target, peer):
        copy = self.make(source, target, peer)
        copy.start()
        return copy


def start_all(copies):
    for copy in copies:
        copy.start()


def wait_all(copies):
    for copy in copies:
        copy.wait()


def here_copies(pairs, sems):
    copies = [pltpu.make_async_copy(a, b, sems.at[i]) for i, (a, b) in enumerate(pairs)]
    start_all(copies)
    return copies


def exchange(total, taken, peers, held, sends):
    copies = []
    for i, peer in enumerate(peers):
        copies.append(sends.start(total.at[0:taken], held.at[i, 0:taken], peer))
    wait_all(copies)
    add = total[0:taken]
    for i in range(len(peers)):
        add = add + held[i, 0:taken]
    total[0:taken] = add


class Layout:
    def __init__(self, width):
        self.width, self.half = width, width // 2
        self.part = self.half + 256
        self.total = 2 * self.part

    def x(self, v):
        return jnp.concatenate([v[:, : self.half], v[:, self.part : self.part + self.half]], 1)

    def bc(self, v):
        a, b = self.half, self.part + self.half
        return jnp.concatenate([v[:, a : a + 128], v[:, b : b + 128]], 1)

    def dt(self, v, own_heads):
        a, b = self.half + 128, self.part + self.half + 128
        return v[:, a : a + 128] + pltpu.roll(v[:, b : b + 128], own_heads, 1)

    def join(self, x, bc, dt, own_heads):
        lane = lax.broadcasted_iota(jnp.int32, dt.shape, 1)
        first = jnp.where(lane < own_heads, dt, 0.0)
        second = jnp.where(lane < own_heads, pltpu.roll(dt, 128 - own_heads, 1), 0.0)
        return jnp.concatenate(
            [x[:, : self.half], bc[:, :128], first, x[:, self.half :], bc[:, 128:], second], 1
        )


def own_heads_of(width):
    return width // 128


def chunk_rows(j):
    return pl.ds(pl.multiple_of(j * Q, Q), Q)


class RingGather:
    SEMS = 7

    def __init__(self, at, source, target, send_sems, recv_sems, local_sem):
        self.at, self.source, self.target = at, source, target
        self.sems = (send_sems, recv_sems)
        self.local_sem = local_sem
        self.up, self.down = {**at, "y": (at["y"] + 1) % 4}, {**at, "y": (at["y"] + 3) % 4}
        self.pair = {**at, "xl": 1 - at["xl"]}

    def rows(self, y, xl):
        return self.target.at[pl.ds(pl.multiple_of((y * 2 + xl) * Q, Q), Q)]

    def copies(self, stage):
        at = self.at
        y, xl, other = at["y"], at["xl"], 1 - at["xl"]
        sends = Sends(*self.sems)
        if stage == 0:
            mine = self.rows(y, xl)
            own = self.source.at[xl]
            return [sends.make(self.source.at[other], mine, self.pair)] + [
                sends.make(own, mine, p) for p in (self.up, self.down)
            ]
        if stage == 1:
            sends.used = 3
            got = self.rows(y, other)
            return [sends.make(got, got, p) for p in (self.up, self.down)]
        sends.used = 5
        low, high = self.rows((y + 3) % 4, xl), self.rows((y + 1) % 4, other)
        return [sends.make(low, low, self.up), sends.make(high, high, self.down)]

    def local(self):
        return pltpu.make_async_copy(self.source.at[self.at["xl"]], self.rows(self.at["y"], self.at["xl"]), self.local_sem)

    def begin(self):
        start_all(self.copies(0))
        self.local().start()

    def second(self):
        self.copies(0)[0].wait()
        start_all(self.copies(1))

    def third(self):
        wait_all(self.copies(0)[1:])
        wait_all(self.copies(1))
        start_all(self.copies(2))

    def finish(self):
        wait_all(self.copies(2))
        self.local().wait()


class RingScatter:
    SEMS = 7

    @staticmethod
    def scratch(width):
        return [pltpu.VMEM((12, Q, width), BF16), dma(RingScatter.SEMS), dma(RingScatter.SEMS), dma(4)]

    def __init__(self, at, part, refs):
        self.at, self.part = at, part
        self.held, self.ss, self.rs, self.ls = refs
        y = at["y"]
        self.up_y, self.down_y, self.far_y = (y + 1) % 4, (y + 3) % 4, (y + 2) % 4
        self.up, self.down = {**at, "y": self.up_y}, {**at, "y": self.down_y}
        self.pair = {**at, "xl": 1 - at["xl"]}

    def of(self, y, x):
        return self.part.at[y * 2 + x]

    def copies(self, stage):
        sends = Sends(self.ss, self.rs)
        held = self.held
        if stage == 0:
            return [
                sends.make(self.of(self.far_y, 0), held.at[0], self.up),
                sends.make(self.of(self.far_y, 1), held.at[1], self.down),
                sends.make(self.of(self.up_y, 1), held.at[2], self.up),
                sends.make(self.of(self.down_y, 0), held.at[3], self.down),
            ]
        if stage == 1:
            sends.used = 4
            return [sends.make(held.at[8], held.at[4], self.up), sends.make(held.at[9], held.at[5], self.down)]
        sends.used = 6
        return [sends.make(held.at[6], held.at[7], self.pair)]

    def locals(self):
        y = self.at["y"]
        sources = [self.of(self.up_y, 0), self.of(self.down_y, 1), self.of(y, 0), self.of(y, 1)]
        return [pltpu.make_async_copy(s, self.held.at[8 + i], self.ls.at[i]) for i, s in enumerate(sources)]

    def begin(self):
        start_all(self.copies(0))
        start_all(self.locals())

    def second(self):
        wait_all(self.locals())
        wait_all(self.copies(0)[:2])
        for i in range(2):
            self.held[8 + i] = (self.held[8 + i].astype(F32) + self.held[i].astype(F32)).astype(BF16)
        start_all(self.copies(1))

    def third(self, out):
        wait_all(self.copies(0)[2:])
        wait_all(self.copies(1))
        held, xl = self.held, self.at["xl"]
        totals = []
        for x in range(2):
            whole_part, summed = held[3 - x].astype(F32), held[4 + x].astype(F32)
            totals.append(held[10 + x].astype(F32) + whole_part + summed)
        out[xl] = jnp.where(xl == 0, totals[0], totals[1])
        held[6] = jnp.where(xl == 0, totals[1], totals[0]).astype(BF16)
        start_all(self.copies(2))

    def finish(self, out):
        wait_all(self.copies(2))
        out[1 - self.at["xl"]] = self.held[7].astype(F32)


def ring_greets(at):
    return [{**at, "y": (at["y"] + 1) % 4}, {**at, "y": (at["y"] + 3) % 4}, {**at, "xl": 1 - at["xl"]}]


class PlaneGather:
    SEMS = 13

    def __init__(self, at, source, target, send_sems, recv_sems, local_sem):
        self.at, self.source, self.target = at, source, target
        self.sems, self.local_sem = (send_sems, recv_sems), local_sem
        depth, half = source.shape[1], source.shape[2]
        self.upper, self.lower = pl.ds(0, depth // 2), pl.ds(depth // 2, depth // 2)
        self.cols = pl.ds(pl.multiple_of(at["xl"] * half, 128), half)

    def copies(self, stage):
        at, w = self.at, self.target
        xh, z, c = at["xh"], at["z"], at["c"]
        sends = Sends(*self.sems)
        if stage == 0:
            return [
                sends.make(self.source.at[:, self.upper], w.at[:, xh, z, c, self.upper, self.cols], p)
                for p in x_peers(at)
            ] + [
                sends.make(self.source.at[:, self.lower], w.at[:, xh, z, c, self.lower, self.cols], p)
                for p in z_peers(at)
            ]
        if stage == 1:
            sends.used = 6
            up, low = w.at[:, :, z, c, self.upper, :], w.at[:, xh, :, c, self.lower, self.cols]
            return [sends.make(up, up, p) for p in z_peers(at)] + [sends.make(low, low, p) for p in x_peers(at)]
        sends.used = 12
        slot = w.at[:, :, :, c]
        return [sends.make(slot, slot, core_peers(at)[0])]

    def local(self):
        at = self.at
        return pltpu.make_async_copy(
            self.source, self.target.at[:, at["xh"], at["z"], at["c"], :, self.cols], self.local_sem
        )

    def begin(self):
        start_all(self.copies(0))
        self.local().start()

    def second(self):
        self.local().wait()
        wait_all(self.copies(0))
        start_all(self.copies(1))

    def third(self):
        wait_all(self.copies(1))
        start_all(self.copies(2))

    def finish(self):
        wait_all(self.copies(2))


class Layout:
    def __init__(self, width):
        self.width, self.half = width, width // 2
        self.part = self.half + 256
        self.total = 2 * self.part

    def x(self, v):
        return jnp.concatenate([v[:, : self.half], v[:, self.part : self.part + self.half]], 1)

    def bc(self, v):
        a, b = self.half, self.part + self.half
        return jnp.concatenate([v[:, a : a + 128], v[:, b : b + 128]], 1)

    def dt(self, v, own_heads):
        a, b = self.half + 128, self.part + self.half + 128
        return v[:, a : a + 128] + pltpu.roll(v[:, b : b + 128], own_heads, 1)

    def join(self, x, bc, dt, own_heads):
        lane = lax.broadcasted_iota(jnp.int32, dt.shape, 1)
        first = jnp.where(lane < own_heads, dt, 0.0)
        second = jnp.where(lane < own_heads, pltpu.roll(dt, 128 - own_heads, 1), 0.0)
        return jnp.concatenate(
            [x[:, : self.half], bc[:, :128], first, x[:, self.half :], bc[:, 128:], second], 1
        )


def own_heads_of(width):
    return width // 128


def chunk_rows(j):
    return pl.ds(pl.multiple_of(j * Q, Q), Q)


def forward_kernel(
    tok_ref, small_ref, hid_ref, wxe_ref, cot_ref, w2_ref,
    z_ref, xe_ref, xc_ref, bcc_ref, y_ref, start_ref, gon_ref, normed_ref, cot_all_ref, w2_all_ref, stat_ref,
    state, xh, bch, cots, weights, normeds, ys, stats, held,
    cot_send, cot_recv, w_send, w_recv, stat_send, stat_recv, sems,
):
    step = pl.program_id(0)
    steps = pl.num_programs(0) // 2
    per_step = STEP_ROWS // Q
    width = z_ref.shape[1]
    lay = Layout(width)
    pairs = width // 128
    chunks = stats.shape[0] // 2
    own_heads = own_heads_of(width)
    at = place()
    ring = RingGather(at, cot_ref, cots, cot_send, cot_recv, sems.at[0])
    plane = PlaneGather(at, w2_ref, weights, w_send, w_recv, sems.at[1])

    def results():
        pairs_of = [(cots, cot_all_ref), (weights, w2_all_ref), (normeds, normed_ref)]
        return [pltpu.make_async_copy(a, b, sems.at[2 + i]) for i, (a, b) in enumerate(pairs_of)]

    @pl.when(step == 0)
    def _():
        greet(ring_greets(at) + y_peers(at)[1:2] + plane_greets(at))
        ring.begin()
        plane.begin()
        state[...] = jnp.zeros_like(state)
        xh[0:HALO] = jnp.zeros((HALO, width), F32)
        bch[0:HALO] = jnp.zeros((HALO, bch.shape[1]), F32)

    @pl.when(step == 1)
    def _():
        ring.second()
        plane.second()

    @pl.when(step == 2)
    def _():
        ring.third()

    @pl.when(step == 3)
    def _():
        plane.third()

    @pl.when(step == steps)
    def _():
        ring.finish()
        plane.finish()
        start_all(results())

    @pl.when(step < steps)
    def _():
        rows = hid_ref[...].astype(F32)
        inv_rms = lax.rsqrt(jnp.mean(rows * rows, -1, keepdims=True) + EPS)
        normed = (rows * inv_rms * wide(small_ref, IN_GAIN, 12)).astype(BF16)
        normeds[pl.ds(pl.multiple_of(step * STEP_ROWS, STEP_ROWS), STEP_ROWS)] = normed
        xe_ref[...] = dot(normed, wxe_ref[...])

        @pl.loop(0, per_step)
        def _(j):
            chunk = step * per_step + j
            here = chunk_rows(j)

            @pl.when(chunk > 0)
            def _():
                xh[0:HALO] = xh[Q : Q + HALO]
                bch[0:HALO] = bch[Q : Q + HALO]

            rows16 = tok_ref[chunk]
            tok = columns_of(rows16)
            hp = small_ref[HEAD_ROWS : HEAD_ROWS + 3]
            xe = xe_ref[here]

            def conv(held_rows, new, row, count):
                held_rows[HALO : HALO + Q] = new
                taps = [wide(small_ref, row + t * count, count) for t in range(5)]
                out = taps[4] + taps[3] * new
                for t in range(1, 4):
                    out = out + (taps[3 - t] * held_rows[HALO - t : HALO - t + Q]) * lanes_of(tok, KEEP + t)
                return out

            xc = conv(xh, lay.x(xe), X_TAPS, pairs)
            bcc = conv(bch, lay.bc(xe), BC_TAPS, 2)
            xc_ref[here] = xc
            bcc_ref[here] = bcc
            x_act = xc * sigmoid(xc)
            bc_act = bcc * sigmoid(bcc)
            n = bc_act.shape[1] // 2
            b_low = bc_act[:, :n].astype(BF16)
            c_low = bc_act[:, n:].astype(BF16)
            size, rate, cum2, cum2_t, enter, leave, keep = decays(lay.dt(xe, own_heads), hp, tok)
            same = causal() & (lanes_of(tok, SEG) == rows16[SEG : SEG + 1])
            scores = jnp.where(same, dot(c_low, b_low, NT), 0.0)
            xs = x_act * expand(size, width)
            xs_low = xs.astype(BF16)
            before = state[...]
            start_ref[j] = before
            inter = dot(c_low, before.astype(BF16)) * expand(enter, width)
            outs = []
            for pair in range(pairs):
                mixes = [(scores * gaps(cum2, cum2_t, 2 * pair + i)).astype(BF16) for i in range(2)]
                outs.append(
                    dot(jnp.concatenate(mixes, 1), pair_blocks(xs_low[:, pair * 128 : pair * 128 + 128]))
                )
            skip = expand(jnp.broadcast_to(hp[1:2], (8, 128)), width)[0:1]
            y = jnp.concatenate(outs, 1) + inter + skip * x_act
            y_ref[here] = y
            ys[chunk_rows(chunk)] = y
            moved = (xs * expand(leave, width)).astype(BF16)
            keep_all = expand(jnp.broadcast_to(keep, (8, 128)), width)[0:1]
            state[...] = before * keep_all + dot(b_low, moved, TN)

    @pl.when(step >= steps)
    def _():
        rows = pl.ds(pl.multiple_of((step - steps) * STEP_ROWS, STEP_ROWS), STEP_ROWS)
        full = weights.shape[1] * weights.shape[2] * weights.shape[3] * weights.shape[4]
        z = dot(normeds[rows], weights[0].reshape(full, width))
        gon = dot(cots[rows], weights[1].reshape(full, width))
        z_ref[...] = z
        gon_ref[...] = gon
        gated = ys[rows] * (z * sigmoid(z))
        inner = gated * (gon * wide(small_ref, X_TAPS + 5 * pairs, pairs))
        for j in range(per_step):
            chunk = (step - steps) * per_step + j
            cut = slice(j * Q, j * Q + Q)
            stats[pl.ds(chunk, 1), :] = row_sums(gated[cut] * gated[cut])
            stats[pl.ds(chunks + chunk, 1), :] = row_sums(inner[cut])

    @pl.when(step == 2 * steps - 1)
    def _():
        wait_all(results())
        exchange(stats, stats.shape[0], y_peers(at), held, Sends(stat_send, stat_recv))
        inner = width * 4
        scale = lax.rsqrt(stats[0:chunks] / inner + EPS)
        stat_ref[0:chunks] = scale
        stat_ref[chunks : 2 * chunks] = scale * scale * scale * stats[chunks : 2 * chunks] / inner


def row_sums(values):
    total = values[:, 0:128]
    for start in range(128, values.shape[1], 128):
        total = total + values[:, start : start + 128]
    return jnp.sum(total.T, axis=0, keepdims=True)


def half_of(value, xl):
    half = value.shape[-1] // 2
    return jnp.where(xl == 0, value[..., :half], value[..., half:])


class PlaneSum:
    SEMS = 13

    @staticmethod
    def scratch(count, depth, width):
        cut, half = depth // 2, width // 2
        return [
            pltpu.VMEM((count, 2, 4, depth, width), BF16),
            pltpu.VMEM((count, 2, 4, depth, width), BF16),
            pltpu.VMEM((3, count, 4, cut, half), BF16),
            pltpu.VMEM((3, count, 2, cut, width), BF16),
            pltpu.VMEM((count, 4, cut, half), BF16),
            pltpu.VMEM((count, 2, cut, width), BF16),
            pltpu.VMEM((3, count, cut, half), BF16),
            pltpu.VMEM((3, count, cut, half), BF16),
            pltpu.SemaphoreType.DMA((PlaneSum.SEMS,)),
            pltpu.SemaphoreType.DMA((PlaneSum.SEMS,)),
            pltpu.SemaphoreType.DMA((1,)),
        ]

    def __init__(self, at, source, refs):
        self.at, self.source = at, source
        (self.mine, self.got, self.a2, self.b2, self.sa, self.sb, self.a3, self.b3, self.ss, self.rs, self.ls) = refs
        self.count, self.depth, self.width = self.mine.shape[0], self.mine.shape[3], self.mine.shape[4]
        self.cut, self.half = self.depth // 2, self.width // 2

    def columns(self, xl):
        return pl.ds(pl.multiple_of(xl * self.half, 128), self.half)

    def sends(self, used):
        sends = Sends(self.ss, self.rs)
        sends.used = used
        return sends

    def local(self):
        return pltpu.make_async_copy(self.source.at[:, :, :, self.at["c"]], self.mine, self.ls.at[0])

    def first(self):
        peer = core_peers(self.at)[0]
        return [self.sends(0).make(self.source.at[:, :, :, peer["c"]], self.got, peer)]

    def second(self):
        sends = self.sends(1)
        upper, lower = pl.ds(0, self.cut), pl.ds(self.cut, self.cut)
        copies = []
        for i, p in enumerate(x_peers(self.at)):
            copies.append(
                sends.make(self.mine.at[:, p["xh"], :, upper, self.columns(p["xl"])], self.a2.at[i], p)
            )
        for i, p in enumerate(z_peers(self.at)):
            copies.append(sends.make(self.mine.at[:, :, p["z"], lower, :], self.b2.at[i], p))
        return copies

    def third(self):
        sends = self.sends(7)
        copies = []
        for i, p in enumerate(z_peers(self.at)):
            copies.append(sends.make(self.sa.at[:, p["z"]], self.a3.at[i], p))
        for i, p in enumerate(x_peers(self.at)):
            copies.append(sends.make(self.sb.at[:, p["xh"], :, self.columns(p["xl"])], self.b3.at[i], p))
        return copies

    def begin(self):
        self.local().start()
        start_all(self.first())

    def after_cores(self):
        self.local().wait()
        wait_all(self.first())
        for m in range(self.count):
            for xh in range(2):

                @pl.loop(0, 4)
                def _(z):
                    total = self.mine[m, xh, z].astype(F32) + self.got[m, xh, z].astype(F32)
                    self.mine[m, xh, z] = total.astype(BF16)

        start_all(self.second())

    def after_first_axis(self):
        wait_all(self.second())
        at, cut = self.at, self.cut
        for m in range(self.count):

            @pl.loop(0, 4)
            def _(z):
                total = half_of(self.mine[m, at["xh"], z, 0:cut], at["xl"]).astype(F32)
                for i in range(3):
                    total = total + self.a2[i, m, z].astype(F32)
                self.sa[m, z] = total.astype(BF16)

            for xh in range(2):
                total = self.mine[m, xh, at["z"], cut : 2 * cut].astype(F32)
                for i in range(3):
                    total = total + self.b2[i, m, xh].astype(F32)
                self.sb[m, xh] = total.astype(BF16)
        start_all(self.third())

    def finish(self, out):
        wait_all(self.third())
        at, cut = self.at, self.cut
        for m in range(self.count):
            total = self.sa[m, at["z"]].astype(F32)
            for i in range(3):
                total = total + self.a3[i, m].astype(F32)
            out[m, 0:cut] = total
            total = half_of(self.sb[m, at["xh"]], at["xl"]).astype(F32)
            for i in range(3):
                total = total + self.b3[i, m].astype(F32)
            out[m, cut : 2 * cut] = total


def plane_greets(at):
    return x_peers(at)[1:] + z_peers(at) + core_peers(at)


def backward_kernel(
    tok_ref, stat_ref, small_ref, z_ref, xe_ref, gon_ref, xc_ref, bcc_ref, y_ref, start_ref, part_ref, g_ref,
    xel_ref, gkx_ref, gkbc_ref, ghead_ref, out_ref, gsum_ref,
    adjoint, dh, dbh, *refs,
):
    turn = pl.program_id(0)
    turns = pl.num_programs(0)
    per_step = STEP_ROWS // Q
    width = z_ref.shape[1]
    lay = Layout(width)
    pairs = width // 128
    own_heads = own_heads_of(width)
    chunks = tok_ref.shape[0]
    at = place()
    ring = RingScatter(at, part_ref, refs[:4])
    plane = PlaneSum(at, g_ref, refs[4:])

    @pl.when(turn == 0)
    def _():
        greet(ring_greets(at) + plane_greets(at))
        ring.begin()
        plane.begin()
        adjoint[...] = jnp.zeros_like(adjoint)
        dh[...] = jnp.zeros_like(dh)
        dbh[...] = jnp.zeros_like(dbh)
        gkx_ref[...] = jnp.zeros_like(gkx_ref)
        gkbc_ref[...] = jnp.zeros_like(gkbc_ref)
        ghead_ref[...] = jnp.zeros_like(ghead_ref)

    @pl.when(turn == 1)
    def _():
        plane.after_cores()

    @pl.when(turn == 2)
    def _():
        ring.second()

    @pl.when(turn == turns - 1)
    def _():
        plane.after_first_axis()

    @pl.loop(0, per_step)
    def _(turn_in):
        j = per_step - 1 - turn_in
        chunk = (turns - 1 - turn) * per_step + j
        here = chunk_rows(j)

        @pl.when(chunk < chunks - 1)
        def _():
            dh[Q : Q + HALO] = dh[0:HALO]
            dbh[Q : Q + HALO] = dbh[0:HALO]

        rows16 = tok_ref[chunk]
        rows16 = jnp.concatenate(
            [rows16[0:SCALE], stat_ref[pl.ds(chunk, 1), :], stat_ref[pl.ds(chunks + chunk, 1), :], rows16[14:16]], 0
        )
        tok = columns_of(rows16)
        hp = small_ref[HEAD_ROWS : HEAD_ROWS + 3]
        xe = xe_ref[here]
        dt_in = lay.dt(xe, own_heads)
        xc = xc_ref[here]
        bcc = bcc_ref[here]
        x_sig = sigmoid(xc)
        x_act = xc * x_sig
        bc_sig = sigmoid(bcc)
        bc_act = bcc * bc_sig
        n = bc_act.shape[1] // 2
        b_low = bc_act[:, :n].astype(BF16)
        c_low = bc_act[:, n:].astype(BF16)
        size, rate, cum2, cum2_t, enter, leave, keep = decays(dt_in, hp, tok)
        same = causal() & (lanes_of(tok, SEG) == rows16[SEG : SEG + 1])
        scores = jnp.where(same, dot(c_low, b_low, NT), 0.0)
        step_all = expand(size, width)
        leave_all = expand(leave, width)
        xs = x_act * step_all
        xs_low = xs.astype(BF16)
        moved = (xs * leave_all).astype(BF16)

        z = z_ref[here]
        z_act = z * sigmoid(z)
        y = y_ref[here]
        gated = y * z_act
        gon = gon_ref[here]
        scale = lanes_of(tok, SCALE)
        gain = wide(small_ref, X_TAPS + 5 * pairs, pairs)
        grad_gated = scale * (gon * gain) - gated * lanes_of(tok, COEF)
        gkx_ref[5] += rows8(gon * gated * scale)
        dy = grad_gated * z_act
        dy_low = dy.astype(BF16)
        dy_in = (dy * expand(enter, width)).astype(BF16)

        skip = expand(jnp.broadcast_to(hp[1:2], (8, 128)), width)[0:1]
        before = start_ref[j]
        before_low = before.astype(BF16)
        after = adjoint[...]
        after_low = after.astype(BF16)

        from_state = dot(b_low, after_low)
        outs = []
        dscores = jnp.zeros((Q, Q), F32)
        for pair in range(pairs):
            cut = slice(pair * 128, pair * 128 + 128)
            dys = pair_blocks(dy_low[:, cut])
            inner = dot(dys, xs_low[:, cut], NT)
            mixes = []
            for i in range(2):
                gap = gaps(cum2, cum2_t, 2 * pair + i)
                mixes.append((scores * gap).astype(BF16))
                dscores = dscores + inner[i * Q : i * Q + Q] * gap
            outs.append(dot(jnp.concatenate(mixes, 0), dys, TN))
        intra = jnp.concatenate(outs, 1)
        dscores = jnp.where(same, dscores, 0.0).astype(BF16)

        dxs = intra + leave_all * from_state
        dx_act = dxs * step_all + skip * dy
        gkx_ref[6] += rows8(dy * x_act)
        plus = head_sums(dy_low.astype(F32) * (y - skip * x_act))
        through = moved.astype(F32) * from_state
        minus = head_sums(xs_low.astype(F32) * intra + through)
        direct = head_sums(dxs * x_act)
        keep_all = expand(jnp.broadcast_to(keep, (8, 128)), width)[0:1]
        at_end = rows8(through) + keep_all * rows8(after * before)
        at_end = jnp.sum(head_sums(at_end), axis=0, keepdims=True)
        last_row = lax.broadcasted_iota(jnp.int32, (Q, 128), 0) == Q - 1
        dcum = plus - minus + jnp.where(last_row, at_end, 0.0)
        tri = jnp.where(causal(), 1.0, 0.0)
        drate = dot_exact(tri, dcum, TN)
        dstep = direct - jnp.exp(hp[0:1]) * drate
        ddt = dstep * sigmoid(dt_in + hp[2:3])
        ghead_ref[0] += rows8(drate * rate)
        ghead_ref[1] += rows8(ddt)

        dc = dot(dscores, b_low) + dot(dy_in, before_low, NT)
        db = dot(dscores, c_low, TN) + dot(moved, after_low, NT)
        adjoint[...] = keep_all * after + dot(c_low, dy_in, TN)

        def conv_back(held, grad, new, row, count, out_ref):
            held[0:Q] = grad
            taps = [wide(small_ref, row + t * count, count) for t in range(4)]
            total = taps[3] * grad
            out_ref[3] += rows8(new * grad)
            out_ref[4] += rows8(grad)
            for t in range(1, 4):
                part = held[t : t + Q] * lanes_of(tok, AHEAD + t)
                total = total + taps[3 - t] * part
                out_ref[3 - t] += rows8(new * part)
            return total

        dxc = dx_act * (x_sig * (1.0 + xc * (1.0 - x_sig)))
        dx_in = conv_back(dh, dxc, lay.x(xe), X_TAPS, pairs, gkx_ref)
        dbcc = jnp.concatenate([db, dc], 1) * (bc_sig * (1.0 + bcc * (1.0 - bc_sig)))
        dbc_in = conv_back(dbh, dbcc, lay.bc(xe), BC_TAPS, 2, gkbc_ref)
        xel_ref[here] = lay.join(dx_in, dbc_in, ddt, own_heads).astype(BF16)

    @pl.when(turn == turns - 1)
    def _():
        ring.third(out_ref)
        plane.finish(gsum_ref)
        ring.finish(out_ref)


def put_wide(ref, row, value):
    for i in range(value.shape[1] // 128):
        ref[row + i : row + i + 1] = value[:, i * 128 : i * 128 + 128]


def end_kernel(
    part_ref, g_ref, gain_ref, gkx_ref, gkbc_ref, ghead_ref,
    out_ref, gsum_ref, sums_ref, bcs_ref,
    held, small_send, small_recv, bc_send, bc_recv, *refs,
):
    at = place()
    ring = RingScatter(at, part_ref, refs[:4])
    plane = PlaneSum(at, g_ref, refs[4:])
    peers = group_peers(at)
    greet(peers + plane_greets(at))
    ring.begin()
    plane.begin()
    sums_ref[...] = jnp.zeros_like(sums_ref)
    for t in range(5):
        put_wide(sums_ref, 2 * t, jnp.sum(gkbc_ref[t], axis=0, keepdims=True))
    put_wide(sums_ref, IN_GAIN, gain_ref[...])
    pairs = gkx_ref.shape[2] // 128
    for t in range(7):
        put_wide(sums_ref, X_TAPS + t * pairs, jnp.sum(gkx_ref[t], axis=0, keepdims=True))
    for t in range(2):
        put_wide(sums_ref, X_TAPS + 7 * pairs + t, jnp.sum(ghead_ref[t], axis=0, keepdims=True))
    steps = [core_peers(at), x_peers(at), z_peers(at), y_peers(at)]
    sends = Sends(small_send, small_recv)
    rows = sums_ref.shape[0]
    exchange(sums_ref, rows, steps[0], held.at[0], sends)
    plane.after_cores()
    ring.second()
    exchange(sums_ref, rows, steps[1], held.at[1], sends)
    exchange(sums_ref, rows, steps[2], held.at[2], sends)
    plane.after_first_axis()
    exchange(sums_ref, SMALL_SHARED, steps[3], held.at[3], sends)
    ring.third(out_ref)
    plane.finish(gsum_ref)
    half = gsum_ref.shape[2] - 256
    bcs_ref[at["xl"], at["y"]] = gsum_ref[0, :, half : half + 128]
    slot = bcs_ref.at[at["xl"], at["y"]]
    sends = Sends(bc_send, bc_recv)
    wait_all([sends.start(slot, slot, p) for p in peers])
    ring.finish(out_ref)


def gather_kernel(
    hid, wx_ref, wdt_ref, wbc_ref, gain_ref, kx_ref, kxb_ref, kbc_ref, kbcb_ref, og_ref, al_ref, ds_ref, db_ref,
    hid_all, wxe_all, small_all,
    wxe, bc_got, bc_rows, held, lanes,
    hid_send, hid_recv, bc_send, bc_recv, w_send, w_recv, small_send, small_recv, sems,
):
    at = place()
    peers = group_peers(at)
    core, ys = core_peers(at), y_peers(at)
    greet(peers + plane_greets(at))
    ring = RingGather(at, hid, hid_all, hid_send, hid_recv, sems.at[0])
    plane = PlaneGather(at, wxe, wxe_all, w_send, w_recv, sems.at[1])
    ring.begin()
    y, xl = at["y"], at["xl"]
    bc_got[y * 2 + xl, 0:12] = wbc_ref[...].astype(F32)
    bc_slot = bc_got.at[y * 2 + xl]
    sends = Sends(bc_send, bc_recv)
    bc_copies = [sends.start(bc_slot, bc_slot, p) for p in peers]

    depth, half = wx_ref.shape
    own_heads = wdt_ref.shape[1]
    wxe[0, :, 0:half] = wx_ref[...]
    wxe[0, :, half + 128 : half + 256] = jnp.zeros((depth, 128), BF16)
    wxe[0, :, half + 128 : half + 128 + own_heads] = wdt_ref[...]

    def placed(pieces, width, start):
        lanes[...] = jnp.zeros_like(lanes)
        row = 0
        for piece in pieces:
            count, size = piece.shape
            lanes[row : row + count, 0:size] = piece[...].astype(F32)
            row += count
        return pltpu.roll(lanes[:, 0:width], start, 1)

    dp = at["xh"] * 8 + at["z"] * 2 + at["c"]
    everyone = dp * 8 + y * 2 + xl
    small_all[...] = jnp.zeros_like(small_all)
    value = placed([kbc_ref, kbcb_ref], 256, everyone * kbc_ref.shape[1])
    for t in range(5):
        put_wide(small_all, BC_TAPS + 2 * t, value[t : t + 1])
    value = placed([gain_ref], lanes.shape[1], everyone * gain_ref.shape[1])
    put_wide(small_all, IN_GAIN, value[0:1])
    value = placed([kx_ref, kxb_ref, og_ref], 2 * half, xl * half + dp * kx_ref.shape[1])
    for t in range(6):
        put_wide(small_all, X_TAPS + t * (half // 64), value[t : t + 1])
    value = placed([al_ref, ds_ref, db_ref], 128, xl * own_heads)
    small_all[HEAD_ROWS : HEAD_ROWS + 3] = jnp.where(dp == 0, value[0:3], 0.0)
    small_sends = Sends(small_send, small_recv)
    exchange(small_all, SMALL_SHARED, ys, held.at[0], small_sends)

    wait_all(bc_copies)
    for m in range(8):
        bc_rows[12 * m : 12 * m + 12] = bc_got[m, 0:12]
    wxe[0, :, half : half + 128] = half_of(bc_rows[...], xl).astype(BF16)
    plane.begin()
    exchange(small_all, SMALL_ROWS, core, held.at[1], small_sends)
    ring.second()
    plane.second()
    exchange(small_all, SMALL_ROWS, x_peers(at), held.at[2], small_sends)
    ring.third()
    exchange(small_all, SMALL_ROWS, z_peers(at), held.at[3], small_sends)
    plane.third()
    plane.finish()
    ring.finish()


def block(rows, w, index):
    return pl.BlockSpec((rows, w), lambda i: (index(i), 0))


def whole(shape):
    return pl.BlockSpec(shape, lambda i: (0,) * len(shape), pipeline_mode=pl.Buffered(1))


def whole_out(shape):
    return pl.BlockSpec(shape, lambda i: (0,) * len(shape))


ANY = pl.BlockSpec(memory_space=pl.ANY)
IN_VMEM = pl.BlockSpec(memory_space=pltpu.VMEM)


def like(shape, dtype):
    return jax.ShapeDtypeStruct(shape, dtype)


def dma(count):
    return pltpu.SemaphoreType.DMA((count,))


def remote_params(cid):
    return pltpu.CompilerParams(collective_id=cid, has_side_effects=True, vmem_limit_bytes=VMEM_LIMIT)


def gather_call(hidden, w_x, w_dt, w_bc, small_args):
    _, rows, model = hidden.shape
    depth, half = w_x.shape
    part = half + 256
    args = [w_x, w_dt, w_bc, *small_args]
    return pl.pallas_call(
        gather_kernel,
        in_specs=[ANY] + [IN_VMEM] * len(args),
        out_specs=[ANY, ANY, IN_VMEM],
        out_shape=[
            like((8 * rows, model), BF16),
            like((1, 2, 4, 2, depth, 2 * part), BF16),
            like((SMALL_ROWS, 128), F32),
        ],
        scratch_shapes=[
            pltpu.VMEM((1, depth, part), BF16),
            pltpu.VMEM((8, 16, w_bc.shape[1]), F32),
            pltpu.VMEM((depth, w_bc.shape[1]), F32),
            pltpu.VMEM((4, 3, SMALL_ROWS, 128), F32),
            pltpu.VMEM((8, model), F32),
            dma(7), dma(7), dma(7), dma(7), dma(13), dma(13), dma(10), dma(10), dma(2),
        ],
        name="gather",
        compiler_params=remote_params(0),
    )(hidden, *args)


def forward_call(tok, small, hid_all, wxe, cotangent, w2):
    length, model = hid_all.shape
    total = wxe.shape[1]
    depth, half = w2.shape[1], w2.shape[2]
    width = 2 * half
    steps = length // STEP_ROWS
    chunks = length // Q

    def early(i):
        return jnp.minimum(i, steps - 1)

    def late(i):
        return jnp.maximum(i - steps, 0)

    return pl.pallas_call(
        forward_kernel,
        grid=(2 * steps,),
        in_specs=[whole(tok.shape), whole(small.shape), block(STEP_ROWS, model, early), whole(wxe.shape), ANY, ANY],
        out_specs=[block(STEP_ROWS, width, late), block(STEP_ROWS, total, early), block(STEP_ROWS, width, early),
                   block(STEP_ROWS, 256, early), block(STEP_ROWS, width, early),
                   pl.BlockSpec((STEP_ROWS // Q, 128, width), lambda i: (early(i), 0, 0)),
                   block(STEP_ROWS, width, late), ANY, ANY, ANY, whole_out((2 * chunks, Q))],
        out_shape=[
            like((length, width), F32), like((length, total), F32), like((length, width), F32),
            like((length, 256), F32), like((length, width), F32), like((chunks, 128, width), F32),
            like((length, width), F32), like((length, model), BF16), like((length, model), BF16),
            like((2, 2, 4, 2, depth, width), BF16), like((2 * chunks, Q), F32),
        ],
        scratch_shapes=[
            pltpu.VMEM((128, width), F32),
            pltpu.VMEM((Q + HALO, width), F32),
            pltpu.VMEM((Q + HALO, 256), F32),
            pltpu.VMEM((length, model), BF16),
            pltpu.VMEM((2, 2, 4, 2, depth, width), BF16),
            pltpu.VMEM((length, model), BF16),
            pltpu.VMEM((length, width), F32),
            pltpu.VMEM((2 * chunks, Q), F32),
            pltpu.VMEM((3, 2 * chunks, Q), F32),
            dma(7), dma(7), dma(13), dma(13), dma(3), dma(3), dma(5),
        ],
        name="mix_forward",
        compiler_params=remote_params(1),
    )(tok, small, hid_all, wxe, cotangent, w2)


def backward_call(tok, stat, small, z, xe, gon, xc, bcc, y, starts, part_out, g):
    length, width = z.shape
    total = xe.shape[1]
    steps = length // STEP_ROWS
    count, depth = g.shape[0], g.shape[4]

    def back(i):
        return steps - 1 - i

    return pl.pallas_call(
        backward_kernel,
        grid=(steps,),
        in_specs=[whole(tok.shape), whole(stat.shape), whole(small.shape),
                  block(STEP_ROWS, width, back), block(STEP_ROWS, total, back), block(STEP_ROWS, width, back),
                  block(STEP_ROWS, width, back), block(STEP_ROWS, 256, back), block(STEP_ROWS, width, back),
                  pl.BlockSpec((STEP_ROWS // Q, 128, width), lambda i: (back(i), 0, 0)), ANY, ANY],
        out_specs=[block(STEP_ROWS, total, back), whole_out((7, 8, width)), whole_out((5, 8, 256)),
                   whole_out((2, 8, 128)), whole_out((2,) + part_out.shape[1:]),
                   whole_out((count, depth, width // 2))],
        out_shape=[
            like((length, total), BF16), like((7, 8, width), F32), like((5, 8, 256), F32), like((2, 8, 128), F32),
            like((2,) + part_out.shape[1:], F32), like((count, depth, width // 2), F32),
        ],
        scratch_shapes=[
            pltpu.VMEM((128, width), F32),
            pltpu.VMEM((Q + HALO, width), F32),
            pltpu.VMEM((Q + HALO, 256), F32),
            *RingScatter.scratch(part_out.shape[2]),
            *PlaneSum.scratch(count, depth, width),
        ],
        name="mix_backward",
        compiler_params=remote_params(2),
    )(tok, stat, small, z, xe, gon, xc, bcc, y, starts, part_out, g)


def end_call(part_in, g, gain, gkx, gkbc, ghead):
    count, depth, total = g.shape[0], g.shape[4], g.shape[5]
    return pl.pallas_call(
        end_kernel,
        in_specs=[ANY, ANY, IN_VMEM, IN_VMEM, IN_VMEM, IN_VMEM],
        out_specs=[IN_VMEM] * 4,
        out_shape=[
            like((2,) + part_in.shape[1:], F32),
            like((count, depth, total // 2), F32),
            like((72, 128), F32),
            like((2, 4, depth, 128), F32),
        ],
        scratch_shapes=[
            pltpu.VMEM((4, 3, 72, 128), F32),
            dma(10), dma(10), dma(7), dma(7),
            *RingScatter.scratch(part_in.shape[2]),
            *PlaneSum.scratch(count, depth, total),
        ],
        name="end",
        compiler_params=remote_params(3),
    )(part_in, g, gain, gkx, gkbc, ghead)


def token_info(ids):
    length = ids.shape[0]
    chunks = length // Q
    seg = ids.astype(F32)
    rows = [jnp.zeros((chunks, Q), F32)] * 16
    for j in range(1, 4):
        back = jnp.concatenate([jnp.full((j,), -1.0, F32), seg[:-j]])
        ahead = jnp.concatenate([seg[j:], jnp.full((j,), -1.0, F32)])
        rows[KEEP + j] = (back == seg).astype(F32).reshape(chunks, Q)
        rows[AHEAD + j] = (ahead == seg).astype(F32).reshape(chunks, Q)
    by_chunk = seg.reshape(chunks, Q)
    tail = by_chunk[:, Q - 1 :]
    last = jnp.concatenate([jnp.full((1, 1), -1.0, F32), tail[:-1]], 0)
    rows[SEG] = by_chunk
    rows[ENTER] = (by_chunk == last).astype(F32)
    rows[LEAVE] = (by_chunk == tail).astype(F32)
    rows[CARRY] = jnp.broadcast_to((tail == last).astype(F32), by_chunk.shape)
    return jnp.stack(rows, 1)


def local(
    hidden, segments, cotangent, norm_gain, w_z, w_x, w_dt, w_bc, conv_x, conv_x_bias, conv_bc, conv_bc_bias,
    a_log, d_skip, dt_bias, out_gain, w_out,
):
    at = place()
    y, xl = at["y"], at["xl"]
    dp, mp = lax.axis_index("dp"), lax.axis_index("mp")
    _, own_len, model = hidden.shape
    depth, half = w_z.shape
    width = 2 * half
    own_heads = a_log.shape[0]
    heads = 2 * own_heads
    lay = Layout(width)

    everyone = dp * 8 + mp
    small_args = [
        norm_gain[None], conv_x, conv_x_bias[None], conv_bc, conv_bc_bias[None], out_gain[None],
        a_log[None], d_skip[None], dt_bias[None],
    ]
    hid_all, wxe_all, small = gather_call(hidden, w_x, w_dt, w_bc, small_args)
    full_xe = wxe_all.reshape(model, lay.total)
    w2 = jnp.stack([w_z, w_out.T])

    ids = lax.dynamic_index_in_dim(segments, xl, 0, keepdims=False)
    tok = token_info(ids)
    z_in, xe_in, xc, bcc, y_out, starts, gon, normed, cot_all, w2_all, stat = forward_call(
        tok, small, hid_all, full_xe, cotangent, w2
    )
    w2_all = w2_all.reshape(2, model, width)
    full_z, full_o = w2_all[0], w2_all[1]

    gain_out = small[X_TAPS + 5 * (width // 128) : X_TAPS + 6 * (width // 128)].reshape(width)
    scale, coef = stat.reshape(2, -1, 1)[0], stat.reshape(2, -1, 1)[1]
    z_sig = sigmoid(z_in)
    z_act = z_in * z_sig
    gated = y_out * z_act
    out_normed = (gated * scale * gain_out).astype(BF16)
    grad_gated = scale * (gon * gain_out) - gated * coef
    z_low = (grad_gated * y_out * (z_sig * (1.0 + z_in * (1.0 - z_sig)))).astype(BF16)
    part_out = dot(out_normed, full_o, NT).astype(BF16).reshape(8, own_len, model)
    g_z = dot(normed, z_low, TN).astype(BF16)
    g_o = dot(cot_all, out_normed, TN).astype(BF16)
    g_zo = jnp.stack([g_z, g_o]).reshape(2, 2, 4, 2, depth, width)
    xe_low, gkx, gkbc, ghead, got_out, zo_sum = backward_call(
        tok, stat, small, z_in, xe_in, gon, xc, bcc, y_out, starts, part_out, g_zo
    )
    mixed = (hidden.astype(F32) + got_out).astype(BF16)

    part_in = dot(z_low, full_z, NT) + dot(xe_low, full_xe, NT)
    rows = hid_all.astype(F32)
    inv_rms = lax.rsqrt(jnp.mean(rows * rows, -1, keepdims=True) + EPS)
    g_gain = jnp.sum(part_in * (rows * inv_rms), 0)
    g_xe = dot(normed, xe_low, TN).astype(BF16).reshape(1, 2, 4, 2, depth, lay.total)
    grad_normed, xe_sum, sums, bc_sum = end_call(
        part_in.astype(BF16).reshape(8, own_len, model), g_xe, g_gain[None], gkx, gkbc, ghead
    )
    xe_sum = xe_sum[0]
    bc_sum = jnp.sum(bc_sum, 1).transpose(1, 0, 2).reshape(8, 12, 256)
    grad_w_bc = lax.dynamic_index_in_dim(bc_sum, mp, 0, keepdims=False)
    g_kbc = lax.dynamic_index_in_dim(sums[0:10].reshape(5, 128, 2), everyone, 1, keepdims=False)
    g_gain = lax.dynamic_index_in_dim(sums[10:22].reshape(128, 12), everyone, 0, keepdims=False)
    chans = lax.dynamic_index_in_dim(sums[24:66].reshape(7, 2, half), xl, 1, keepdims=False)
    own = lax.dynamic_index_in_dim(chans.reshape(7, 16, half // 16), dp, 1, keepdims=False)
    per_head = jnp.sum(chans[6].reshape(own_heads, -1), 1)
    head_rows = lax.dynamic_index_in_dim(sums[66:68, :heads].reshape(2, 2, own_heads), xl, 1, keepdims=False)

    gain_in = small[IN_GAIN : IN_GAIN + 12].reshape(model)
    h = hidden.astype(F32)
    inv_own = lax.rsqrt(jnp.mean(h * h, -1, keepdims=True) + EPS)
    hat = grad_normed * gain_in
    grad_hidden = (
        cotangent.astype(F32)
        + inv_own * hat
        - h * (inv_own * inv_own * inv_own) * jnp.mean(hat * h, -1, keepdims=True)
    )
    return (
        mixed,
        grad_hidden,
        g_gain,
        zo_sum[0],
        xe_sum[:, :half],
        xe_sum[:, half + 128 : half + 128 + own_heads],
        grad_w_bc,
        own[0:4],
        own[4],
        g_kbc[0:4],
        g_kbc[4],
        head_rows[0],
        per_head,
        head_rows[1],
        own[5],
        zo_sum[1].T,
    )


def solution(mesh):
    in_specs = (
        P("dp", "mp", None),
        P("dp", None),
        P("dp", "mp", None),
        P(("dp", "mp")),
        P("dp", "mp"),
        P("dp", "mp"),
        P("dp", "mp"),
        P(("dp", "mp"), None),
        P(None, ("mp", "dp")),
        P(("mp", "dp")),
        P(None, ("dp", "mp")),
        P(("dp", "mp")),
        P("mp"),
        P("mp"),
        P("mp"),
        P(("mp", "dp")),
        P("mp", "dp"),
    )
    out_specs = (
        P("dp", "mp", None),
        P("dp", "mp", None),
        P(("dp", "mp")),
        P("dp", "mp"),
        P("dp", "mp"),
        P("dp", "mp"),
        P(("dp", "mp"), None),
        P(None, ("mp", "dp")),
        P(("mp", "dp")),
        P(None, ("dp", "mp")),
        P(("dp", "mp")),
        P("mp"),
        P("mp"),
        P("mp"),
        P(("mp", "dp")),
        P("mp", "dp"),
    )
    return jax.shard_map(local, mesh=mesh, in_specs=in_specs, out_specs=out_specs, check_vma=False)
```

time: 2050 us -> 255 us (0.12)
  blocking collectives: 1290 us -> 0 us
  matrix products: 222 us -> 26.2 us
  Pallas kernels: 0 us -> 193 us
  local copies, waits for them, and re-layouts: 163 us -> 17.1 us
  other arithmetic: 161 us -> 17 us
  waiting for transfers between devices: 98.3 us -> 0 us
  starting transfers between devices: 90.8 us -> 0 us
    all_gather x4 -> x0, blocking collectives: 669 us -> none  [the longest x1 320 us: local(): lax.all_gather(w_bc, ('dp', 'mp'), axis=0, tiled=True)]
    unnamed x5 -> x0, blocking collectives: 582 us -> none
    dot_general x71 -> x6, matrix products: 222 us -> 26.2 us  [dot(): return lax.dot_general(a, b, (dims, ((), ())), preferred_element_type=F32)]
    pallas_call x0 -> x4, Pallas kernels: none -> 193 us  [the longest x1 52.8 us: forward_call(): pl.pallas_call(forward_kernel, grid=(2 * steps,), in_specs=[whole(tok.sha...]
    reduce_scatter x6 -> x0, waiting for transfers between devices: 96.1 us -> none  [the longest x1 76.4 us: local(): lax.psum_scatter(grad_w_z, 'dp', scatter_dimension=0, tiled=True)]
    unnamed x33 -> x0, starting transfers between devices: 90.2 us -> none
    another operation x45 -> x3, other arithmetic: 91.4 us -> 4.49 us  [the longest x1 2.81 us: local(): g_zo = jnp.stack([g_z, g_o]).reshape(2, 2, 4, 2, depth, width)]
    psum x2 -> x0, blocking collectives: 34.7 us -> none  [the longest x1 17.6 us: local(): sq_total = lax.psum(sq_local, 'mp')]
  transfers between devices with their start and end apart: 44 -> 0, of which waited for: 2 -> 0; matrix products, arithmetic and copies ran while one was open for 30% -> 0% of each run, Pallas kernels for 0% -> 0%
where the time goes in v1:
time: 255 us; the launch traced here: 254 us
  Pallas kernels  193 us (76%)
  matrix products  26.2 us (10%)
  local copies, waits for them, and re-layouts  17.1 us (7%)
  other arithmetic  17 us (7%)
    pallas_call x1, Pallas kernels, forward_call(): pl.pallas_call(forward_kernel, grid=(2 * steps,), in_specs=[whole(tok.sha...  52.8 us
    pallas_call x1, Pallas kernels, end_call(): pl.pallas_call(end_kernel, in_specs=[ANY, ANY, IN_VMEM, IN_VMEM, IN_VMEM,...  48.5 us
    pallas_call x1, Pallas kernels, gather_call(): pl.pallas_call(gather_kernel, in_specs=[ANY] + [IN_VMEM] * len(args), out...  47.7 us
    pallas_call x1, Pallas kernels, backward_call(): pl.pallas_call(backward_kernel, grid=(steps,), in_specs=[whole(tok.shape)...  44 us
    dot_general x6, matrix products, dot(): return lax.dot_general(a, b, (dims, ((), ())), preferred_element_type=F32)  26.2 us
    unnamed x35, local copies, waits for them, and re-layouts  5.91 us

profile of v1, /device:TPU:0, one launch (start us, length us, event | category | flops | bytes accessed | tf_op | source)
XLA Modules:
  0.0 254.3 jit_solution(6060591611364970025)
XLA Ops:
  0.7 0.7 dynamic-slice_convert_fusion
  1.6 0.1 copy.52
  1.8 0.1 copy.53
  1.9 0.8 compare_convert_fusion
  3.1 0.7 fusion.38
  3.8 1.3 stack.27.tok_ref
  5.2 1.4 copy.47.wdt_ref
  6.5 1.3 copy.48.kbc_ref
  7.9 47.7 %gather.1 = (bf16[1024,1536]{1,0:T(8,128)(2,1)}, bf16[1,2,4,2,96,1280]{5,4,3,2,1,0:T(8,128)(2,1)}, f32[64,128]{1,0:T(8,128)}) custom-call(bf16[2,128,1536]{2,1,0:T(8,128)(2,1)} %hid.1, bf16[96,384]{1,0:T(8,128)(2,1)} %wx_ref.1, bf16[96,6]{1,0:T(8,128)(2,1)} %copy.47.wdt_ref, bf16[12,256]{1,0:T(8,128)(2,1)} %wbc_ref.1, bf16[1,12]{1,0:T(2,128)(2,1)} %bitcast.122, ...), custom_call_target="tpu_custom_call" | custom-call | tf_op jit(solution)/shard_map/gather/pallas_call | solution.py:1031
  55.6 1.6 pad_maximum_fusion.1.w2_ref
  57.2 52.8 %mix_forward.1 = (f32[1024,768]{1,0:T(8,128)}, f32[1024,1280]{1,0:T(8,128)}, f32[1024,768]{1,0:T(8,128)}, f32[1024,256]{1,0:T(8,128)}, f32[1024,768]{1,0:T(8,128...) custom-call(f32[8,16,128]{2,1,0:T(8,128)} %stack.27.tok_ref, ...), custom_call_target="tpu_custom_call" | custom-call | tf_op jit(solution)/shard_map/mix_forward/pallas_call | solution.py:1067
  110.0 0.7 slice_bitcast_fusion.3
  110.6 0.7 slice_bitcast_fusion.4
  111.3 5.0 %multiply_convert_fusion = (bf16[1024,768]{1,0:T(8,128)(2,1)S(1)}, bf16[1024,768]{1,0:T(8,128)(2,1)S(1)}) fusion(f32[1024,768]{1,0:T(8,128)} %get-tuple-element.44.z_ref, f32[1024,768]{1,0:T(8,128)} %get-tuple-element.49.y_ref, f32[1024,768]{1,0:T(8,128)} %get-tuple-element.46.gon_ref, f32[1024]{0:T(1024)S(1)} %get-tuple-element.126, ...), kind=kLoop, calls=%fused_computation.11 | loop fusion | flops 14942208 | bytes 12594176 | tf_op jit(solution)/shard_map/convert_element_type | solution.py:1214
  116.3 2.9 %convolution_convert_fusion.3 = bf16[1536,768]{1,0:T(8,128)(2,1)S(1)} fusion(bf16[1024,1536]{1,0:T(8,128)(2,1)S(1)} %copy-done.10, bf16[1024,768]{1,0:T(8,128)(2,1)S(1)} %get-tuple-element.114), kind=kOutput, calls=%fused_computation.10 | convolution fusion | flops 2417098752 | bytes 7077888 | tf_op jit(solution)/shard_map/dot_general | solution.py:26
  119.3 3.0 %convolution_convert_fusion.2 = bf16[1536,768]{1,0:T(8,128)(2,1)S(1)} fusion(bf16[1024,1536]{1,0:T(8,128)(2,1)S(1)} %copy-done.11, bf16[1024,768]{1,0:T(8,128)(2,1)S(1)} %get-tuple-element.115), kind=kOutput, calls=%fused_computation.9 | convolution fusion | flops 2417098752 | bytes 7077888 | tf_op jit(solution)/shard_map/dot_general | solution.py:26
  122.3 2.8 %pad_maximum_fusion.g_ref = bf16[2,2,4,2,96,768]{5,4,3,2,1,0:T(8,128)(2,1)} fusion(bf16[1,2,4,2,96,768]{5,4,3,2,1,0:T(8,128)(2,1)S(1)} %bitcast.98, bf16[1,2,4,2,96,768]{5,4,3,2,1,0:T(8,128)(2,1)S(1)} %bitcast.97), kind=kLoop, calls=%fused_computation.6 | loop fusion | flops 2359296 | bytes 9437184 | tf_op jit(solution)/shard_map/stack | solution.py:1218
  125.1 1.1 slice-done
  126.1 0.1 slice-done.1
  126.3 0.4 fusion.21
  126.7 4.1 %convolution_convert_fusion.1 = bf16[1024,1536]{1,0:T(8,128)(2,1)} fusion(bf16[1024,768]{1,0:T(8,128)(2,1)S(1)} %get-tuple-element.115, bf16[1536,768]{1,0:T(8,128)(2,1)S(1)} %bitcast.96), kind=kOutput, calls=%fused_computation.8 | convolution fusion | flops 2417491968 | bytes 7077888 | tf_op jit(solution)/shard_map/dot_general | solution.py:26
  130.8 44.0 %mix_backward.1 = (bf16[1024,1280]{1,0:T(8,128)(2,1)}, f32[7,8,768]{2,1,0:T(8,128)}, f32[5,8,256]{2,1,0:T(8,128)}, f32[2,8,128]{2,1,0:T(8,128)}, f32[2,128,1536]{2,1,0:T(8,128)}, /*index=5*/f32[2,96,384]{2,1,0:T(8,128)}) custom-call(f32[8,16,128]{2,1,0:T(8,128)} %stack.27.tok_ref, f32[16,128]{1,0:T(8,128)} %get-tuple-element.43.stat_ref, ...), custom_call_target="tpu_custom_call" | custom-call | tf_op jit(solution)/shard_map/mix_backward/pallas_call | solution.py:1107
  174.7 7.5 %convolution_convert_fusion = bf16[1536,1280]{1,0:T(8,128)(2,1)} fusion(bf16[1024,1536]{1,0:T(8,128)(2,1)S(1)} %copy-done.10, bf16[1024,1280]{1,0:T(8,128)(2,1)} %get-tuple-element.55), kind=kOutput, calls=%fused_computation.2 | convolution fusion | flops 4028497920 | bytes 9699328 | tf_op jit(solution)/shard_map/dot_general | solution.py:26
  182.3 2.6 %fusion.25 = f32[1024,1536]{1,0:T(8,128)S(1)} fusion(bf16[1024,768]{1,0:T(8,128)(2,1)S(1)} %get-tuple-element.114, bf16[1536,768]{1,0:T(8,128)(2,1)S(1)} %bitcast.95), kind=kOutput, calls=%fused_computation.76 | convolution fusion | flops 2415919104 | bytes 10223616 | tf_op jit(solution)/shard_map/dot_general | solution.py:26
  184.9 0.7 fusion
  185.6 1.1 copy-done.12
  186.8 6.1 %fusion.2 = (f32[1536]{0:T(1024)S(1)}, bf16[1024,1536]{1,0:T(8,128)(2,1)}) fusion(bf16[1024,1536]{1,0:T(8,128)(2,1)S(1)} %copy-done, f32[1024]{0:T(1024)S(1)} %add_rsqrt_fusion, f32[1024,1536]{1,0:T(8,128)S(1)} %fusion.25, bf16[1024,1280]{1,0:T(8,128)(2,1)S(1)} %copy-done.12, bf16[1536,1280]{1,0:T(8,128)(2,1)S(1)} %bitcast.91), kind=kOutput, calls=%fused_computation.5 | convolution fusion | flops 4035967488 | bytes 19146752 | tf_op jit(solution)/shard_map/dot_general | solution.py:26
  192.8 0.6 broadcast_in_dim.34.gain_ref
  193.4 48.5 %end.1 = (f32[2,128,1536]{2,1,0:T(8,128)}, f32[1,96,640]{2,1,0:T(8,128)}, f32[72,128]{1,0:T(8,128)}, f32[2,4,96,128]{3,2,1,0:T(8,128)}) custom-call(bf16[8,128,1536]{2,1,0:T(8,128)(2,1)} %bitcast.94, bf16[1,2,4,2,96,1280]{5,4,3,2,1,0:T(8,128)(2,1)} %bitcast.92, f32[1,1536]{1,0:T(1,128)} %broadcast_in_dim.34.gain_ref, ...), custom_call_target="tpu_custom_call" | custom-call | tf_op jit(solution)/shard_map/end/pallas_call | solution.py:1135
  241.9 0.8 slice_bitcast_fusion.2
  242.7 1.8 fusion.4
  244.6 2.0 fusion.6
  246.6 0.3 reshape.258
  246.9 0.6 copy.50
  247.6 0.5 fusion.16
  248.2 0.1 reshape.255
  248.3 0.6 dynamic-slice_bitcast_fusion
  249.0 0.1 reshape.257
  249.1 0.5 fusion.15
  249.6 0.6 constant_dynamic-slice_fusion.4
  250.3 0.6 reduce_sum.59
  250.9 0.1 reshape.259
  251.0 0.5 fusion.17
  251.5 0.7 slice.172
  252.2 0.1 reshape.254
  252.3 0.5 fusion.14
  252.9 0.7 copy.51
  253.5 0.7 slice_bitcast_fusion
  (55 shorter events, 1.1 us)
Async XLA Ops:
  111.3 5.0 %copy-start.10 = (bf16[1024,1536]{1,0:T(8,128)(2,1)S(1)}, bf16[1024,1536]{1,0:T(8,128)(2,1)}, u32[]{:S(2)}) copy-start(bf16[1024,1536]{1,0:T(8,128)(2,1)} %get-tuple-element.52) | copy-start | bytes 9437188
  116.3 3.0 %copy-start.11 = (bf16[1024,1536]{1,0:T(8,128)(2,1)S(1)}, bf16[1024,1536]{1,0:T(8,128)(2,1)}, u32[]{:S(2)}) copy-start(bf16[1024,1536]{1,0:T(8,128)(2,1)} %get-tuple-element.53) | copy-start | bytes 9437188
  122.3 3.9 %slice-start = ((s8[4718592]{0:T(1024)(128)(4,1)}), s8[4194304]{0:T(1024)(128)(4,1)S(1)}, s32[]{:S(2)}) async-start(s8[4718592]{0:T(1024)(128)(4,1)} %bitcast.88), calls=%async_computation | async-start | bytes 8388608
  122.3 4.0 %slice-start.1 = ((s8[4718592]{0:T(1024)(128)(4,1)}), s8[524288]{0:T(1024)(128)(4,1)S(1)}, s32[]{:S(2)}) async-start(s8[4718592]{0:T(1024)(128)(4,1)} %bitcast.88), calls=%async_computation.1 | async-start | bytes 1048576
  182.3 2.6 %copy-start = (bf16[1024,1536]{1,0:T(8,128)(2,1)S(1)}, bf16[1024,1536]{1,0:T(8,128)(2,1)}, u32[]{:S(2)}) copy-start(bf16[1024,1536]{1,0:T(8,128)(2,1)} %get-tuple-element.41.hid_ref) | copy-start | bytes 9437188
  182.3 3.4 %copy-start.3 = (bf16[1,2,4,2,96,1280]{5,4,3,2,1,0:T(8,128)(2,1)S(1)}, bf16[1,2,4,2,96,1280]{5,4,3,2,1,0:T(8,128)(2,1)}, u32[]{:S(2)}) copy-start(bf16[1,2,4,2,96,1280]{5,4,3,2,1,0:T(8,128)(2,1)} %get-tuple-element.42) | copy-start | bytes 11796484
  184.9 1.8 copy-start.12
  193.4 49.3 %copy-start.1 = (bf16[2,128,1536]{2,1,0:T(8,128)(2,1)S(1)}, bf16[2,128,1536]{2,1,0:T(8,128)(2,1)}, u32[]{:S(2)}) copy-start(bf16[2,128,1536]{2,1,0:T(8,128)(2,1)} %hid.1) | copy-start | bytes 2359300
  193.4 51.1 %copy-start.4 = (bf16[2,128,1536]{2,1,0:T(8,128)(2,1)S(1)}, bf16[2,128,1536]{2,1,0:T(8,128)(2,1)}, u32[]{:S(2)}) copy-start(bf16[2,128,1536]{2,1,0:T(8,128)(2,1)} %cot_ref.1) | copy-start | bytes 2359300
  193.4 51.1 %copy-start.5 = (f32[2,128,1536]{2,1,0:T(8,128)S(1)}, f32[2,128,1536]{2,1,0:T(8,128)}, u32[]{:S(2)}) copy-start(f32[2,128,1536]{2,1,0:T(8,128)} %get-tuple-element.54) | copy-start | bytes 4718596
  241.9 2.7 %copy-start.2 = (f32[2,128,1536]{2,1,0:T(8,128)S(1)}, f32[2,128,1536]{2,1,0:T(8,128)}, u32[]{:S(2)}) copy-start(f32[2,128,1536]{2,1,0:T(8,128)} %get-tuple-element.59) | copy-start | bytes 4718596
  244.6 2.0 copy-start.9
  244.6 3.5 %copy-start.6 = (f32[2,4,96,128]{3,2,1,0:T(8,128)S(1)}, f32[2,4,96,128]{3,2,1,0:T(8,128)}, u32[]{:S(2)}) copy-start(f32[2,4,96,128]{3,2,1,0:T(8,128)} %get-tuple-element.63) | copy-start | bytes 1179652
  244.6 6.9 %copy-start.8 = (f32[1,96,640]{2,1,0:T(8,128)S(1)}, f32[1,96,640]{2,1,0:T(8,128)}, u32[]{:S(2)}) copy-start(f32[1,96,640]{2,1,0:T(8,128)} %get-tuple-element.62) | copy-start | bytes 737284
  244.6 8.9 %copy-start.7 = (f32[2,96,384]{2,1,0:T(8,128)S(1)}, f32[2,96,384]{2,1,0:T(8,128)}, u32[]{:S(2)}) copy-start(f32[2,96,384]{2,1,0:T(8,128)} %get-tuple-element.61) | copy-start | bytes 884740

commit v2 on v1

v2 whole, which is shorter than its diff:
```python
import jax
import jax.numpy as jnp
from jax import lax
from jax.experimental import pallas as pl
from jax.experimental.pallas import tpu as pltpu
from jax.sharding import PartitionSpec as P

MESH = pl.DeviceIdType.MESH
EPS = 1e-05
Q = 128
HALO = 8
F32 = jnp.float32
BF16 = jnp.bfloat16
LOG2E = 1.4426950408889634
VMEM_LIMIT = 60 * 1024 * 1024

KEEP = 0
AHEAD = 4
SEG, ENTER, LEAVE, CARRY, SCALE, COEF = 8, 9, 10, 11, 12, 13
STEP_ROWS = 256

BC_TAPS, IN_GAIN, X_TAPS, HEAD_ROWS, SMALL_SHARED, SMALL_ROWS = 0, 10, 24, 60, 24, 64


def dot(a, b, dims=((1,), (0,))):
    return lax.dot_general(a, b, (dims, ((), ())), preferred_element_type=F32)


def dot_exact(a, b, dims=((1,), (0,))):
    return lax.dot_general(
        a, b, (dims, ((), ())), preferred_element_type=F32, precision=lax.Precision.HIGHEST
    )


NT = ((1,), (1,))
TN = ((0,), (0,))


def sigmoid(v):
    return 1.0 / (1.0 + jnp.exp(-v))


def softplus(v):
    return jnp.maximum(v, 0.0) + jnp.log1p(jnp.exp(-jnp.abs(v)))


def wide(small, row, count):
    return jnp.concatenate([small[row + i : row + i + 1] for i in range(count)], 1)


def columns_of(rows16):
    return jnp.concatenate([rows16, jnp.zeros((128 - rows16.shape[0], Q), F32)], 0).T


def lanes_of(tok, lane):
    return tok[:, lane : lane + 1]


def expand(values, width):
    rows = values.shape[0]
    first = lax.broadcasted_iota(jnp.int32, (rows, 128), 1) < 64
    pieces = []
    for pair in range(width // 128):
        a = jnp.broadcast_to(values[:, 2 * pair : 2 * pair + 1], (rows, 128))
        b = jnp.broadcast_to(values[:, 2 * pair + 1 : 2 * pair + 2], (rows, 128))
        pieces.append(jnp.where(first, a, b))
    return jnp.concatenate(pieces, 1)


def head_sums(values):
    width = values.shape[1]
    channel = lax.broadcasted_iota(jnp.int32, (width, 128), 0)
    lane = lax.broadcasted_iota(jnp.int32, (width, 128), 1)
    pick = jnp.where((channel >= lane * 64) & (channel < lane * 64 + 64), 1.0, 0.0).astype(BF16)
    high = values.astype(BF16)
    low = (values - high.astype(F32)).astype(BF16)
    return dot(high, pick) + dot(low, pick)


def rows8(values):
    total = values[0:8]
    for start in range(8, values.shape[0], 8):
        total = total + values[start : start + 8]
    return total


def causal():
    row = lax.broadcasted_iota(jnp.int32, (Q, Q), 0)
    col = lax.broadcasted_iota(jnp.int32, (Q, Q), 1)
    return row >= col


def pair_blocks(values):
    first = lax.broadcasted_iota(jnp.int32, values.shape, 1) < 64
    zero = jnp.zeros_like(values)
    return jnp.concatenate([jnp.where(first, values, zero), jnp.where(first, zero, values)], 0)


def decays(dt, hp, tok):
    step = softplus(dt + hp[2:3])
    rate = -jnp.exp(hp[0:1]) * step
    tri = jnp.where(causal(), 1.0, 0.0)
    cum = dot_exact(tri, rate)
    last = cum[Q - 1 : Q]
    enter = jnp.exp(cum) * lanes_of(tok, ENTER)
    leave = jnp.exp(last - cum) * lanes_of(tok, LEAVE)
    keep = jnp.exp(last) * tok[0:1, CARRY : CARRY + 1]
    cum2 = cum * LOG2E
    return step, rate, cum2, cum2.T, enter, leave, keep


def gaps(cum2, cum2_t, head):
    return jnp.exp2(jnp.minimum(cum2[:, head : head + 1] - cum2_t[head : head + 1, :], 0.0))


def place():
    dp, mp = lax.axis_index("dp"), lax.axis_index("mp")
    return {"xh": dp // 8, "z": (dp // 2) % 4, "c": dp % 2, "y": mp // 2, "xl": mp % 2}


def device(at, **other):
    at = {**at, **other}
    return (at["xh"] * 8 + at["z"] * 2 + at["c"], at["y"] * 2 + at["xl"])


def group_peers(at):
    peers = []
    for dy in range(4):
        for flip in range(2):
            if dy or flip:
                peers.append({**at, "y": (at["y"] + dy) % 4, "xl": (at["xl"] + flip) % 2})
    return peers


def x_peers(at):
    flips = [(0, 1), (1, 0), (1, 1)]
    return [{**at, "xh": (at["xh"] + a) % 2, "xl": (at["xl"] + b) % 2} for a, b in flips]


def z_peers(at):
    return [{**at, "z": (at["z"] + d) % 4} for d in range(1, 4)]


def y_peers(at):
    return [{**at, "y": (at["y"] + d) % 4} for d in range(1, 4)]


def core_peers(at):
    return [{**at, "c": 1 - at["c"]}]


def greet_begin(peers):
    barrier = pltpu.get_barrier_semaphore()
    for peer in peers:
        pl.semaphore_signal(barrier, inc=1, device_id=device(peer), device_id_type=MESH)


def greet_end(peers):
    pl.semaphore_wait(pltpu.get_barrier_semaphore(), len(peers))


def greet(peers):
    greet_begin(peers)
    greet_end(peers)


class Sends:
    def __init__(self, send_sems, recv_sems):
        self.send_sems, self.recv_sems, self.used = send_sems, recv_sems, 0

    def make(self, source, target, peer):
        slot = self.used
        self.used += 1
        return pltpu.make_async_remote_copy(
            src_ref=source,
            dst_ref=target,
            send_sem=self.send_sems.at[slot],
            recv_sem=self.recv_sems.at[slot],
            device_id=device(peer),
            device_id_type=MESH,
        )

    def start(self, source, target, peer):
        copy = self.make(source, target, peer)
        copy.start()
        return copy


def start_all(copies):
    for copy in copies:
        copy.start()


def wait_all(copies):
    for copy in copies:
        copy.wait()


def here_copies(pairs, sems):
    copies = [pltpu.make_async_copy(a, b, sems.at[i]) for i, (a, b) in enumerate(pairs)]
    start_all(copies)
    return copies


class Exchange:
    def __init__(self, total, taken, peers, held, sends):
        self.total, self.taken, self.held, self.count = total, taken, held, len(peers)
        rows = pl.ds(0, taken)
        self.copies = [sends.start(total.at[rows], held.at[i, rows], peer) for i, peer in enumerate(peers)]

    def finish(self):
        wait_all(self.copies)
        add = self.total[0 : self.taken]
        for i in range(self.count):
            add = add + self.held[i, 0 : self.taken]
        self.total[0 : self.taken] = add


def exchange(total, taken, peers, held, sends):
    Exchange(total, taken, peers, held, sends).finish()


class RingGather:
    SEMS = 7

    def __init__(self, at, source, target, send_sems, recv_sems, local_sem):
        self.at, self.source, self.target = at, source, target
        self.sems = (send_sems, recv_sems)
        self.local_sem = local_sem
        self.up, self.down = {**at, "y": (at["y"] + 1) % 4}, {**at, "y": (at["y"] + 3) % 4}
        self.pair = {**at, "xl": 1 - at["xl"]}

    def rows(self, y, xl):
        return self.target.at[pl.ds(pl.multiple_of((y * 2 + xl) * Q, Q), Q)]

    def copies(self, stage):
        at = self.at
        y, xl, other = at["y"], at["xl"], 1 - at["xl"]
        sends = Sends(*self.sems)
        if stage == 0:
            mine = self.rows(y, xl)
            own = self.source.at[xl]
            return [sends.make(self.source.at[other], mine, self.pair)] + [
                sends.make(own, mine, p) for p in (self.up, self.down)
            ]
        if stage == 1:
            sends.used = 3
            got = self.rows(y, other)
            return [sends.make(got, got, p) for p in (self.up, self.down)]
        sends.used = 5
        low, high = self.rows((y + 3) % 4, xl), self.rows((y + 1) % 4, other)
        return [sends.make(low, low, self.up), sends.make(high, high, self.down)]

    def local(self):
        return pltpu.make_async_copy(self.source.at[self.at["xl"]], self.rows(self.at["y"], self.at["xl"]), self.local_sem)

    def begin(self):
        start_all(self.copies(0))
        self.local().start()

    def second(self):
        self.copies(0)[0].wait()
        start_all(self.copies(1))

    def third(self):
        wait_all(self.copies(0)[1:])
        wait_all(self.copies(1))
        start_all(self.copies(2))

    def finish(self):
        wait_all(self.copies(2))
        self.local().wait()


class RingScatter:
    SEMS = 7

    @staticmethod
    def scratch(width):
        return [pltpu.VMEM((8, Q, width), BF16), dma(RingScatter.SEMS), dma(RingScatter.SEMS)]

    def __init__(self, at, part, refs):
        self.at, self.part = at, part
        self.held, self.ss, self.rs = refs
        y = at["y"]
        self.up_y, self.down_y, self.far_y = (y + 1) % 4, (y + 3) % 4, (y + 2) % 4
        self.up, self.down = {**at, "y": self.up_y}, {**at, "y": self.down_y}
        self.pair = {**at, "xl": 1 - at["xl"]}

    def copy(self, number):
        sends = Sends(self.ss, self.rs)
        sends.used = number
        if number == 6:
            return sends.make(self.held.at[6], self.held.at[7], self.pair)
        y, x = [(self.far_y, 0), (self.far_y, 1), (self.up_y, 1), (self.down_y, 0), (self.up_y, 0), (self.down_y, 1)][number]
        peer = self.down if number % 2 else self.up
        return sends.make(self.part.at[y * 2 + x], self.held.at[number], peer)

    def send_far(self):
        start_all([self.copy(0), self.copy(1)])

    def send_up(self):
        self.copy(2).start()

    def send_down(self):
        self.copy(3).start()

    def second(self):
        wait_all([self.copy(0), self.copy(1)])
        for slot, number in ((self.up_y * 2, 0), (self.down_y * 2 + 1, 1)):
            self.part[slot] = (self.part[slot].astype(F32) + self.held[number].astype(F32)).astype(BF16)
        start_all([self.copy(4), self.copy(5)])

    def third(self, out):
        wait_all([self.copy(n) for n in range(2, 6)])
        held, xl, y = self.held, self.at["xl"], self.at["y"]
        totals = []
        for x in range(2):
            totals.append(self.part[y * 2 + x].astype(F32) + held[3 - x].astype(F32) + held[4 + x].astype(F32))
        out[xl] = jnp.where(xl == 0, totals[0], totals[1]).astype(BF16)
        held[6] = jnp.where(xl == 0, totals[1], totals[0]).astype(BF16)
        self.copy(6).start()

    def finish(self, out):
        self.copy(6).wait()
        out[1 - self.at["xl"]] = self.held[7]


def ring_greets(at):
    return [{**at, "y": (at["y"] + 1) % 4}, {**at, "y": (at["y"] + 3) % 4}, {**at, "xl": 1 - at["xl"]}]


class PlaneGather:
    SEMS = 31

    def __init__(self, at, source, target, send_sems, recv_sems, local_sem, start=0, count=None):
        self.at, self.source, self.target = at, source, target
        self.sems, self.local_sem = (send_sems, recv_sems), local_sem
        depth, part = source.shape[1], source.shape[2]
        self.whole = count is None
        self.start, self.count = start, part if self.whole else count
        self.part = part
        self.upper, self.lower = pl.ds(0, depth // 2), pl.ds(depth // 2, depth // 2)
        self.lanes = pl.ds(self.start, self.count)
        self.cols = pl.ds(pl.multiple_of(at["xl"] * part + self.start, 128), self.count)
        self.both = [pl.ds(0, 2 * part)] if self.whole else [pl.ds(n * part + start, count) for n in range(2)]

    def copies(self, stage):
        at, w = self.at, self.target
        xh, z, c = at["xh"], at["z"], at["c"]
        sends = Sends(*self.sems)
        if stage == 0:
            return [
                sends.make(self.source.at[:, self.upper, self.lanes], w.at[:, xh, z, c, self.upper, self.cols], p)
                for p in x_peers(at)
            ] + [
                sends.make(self.source.at[:, self.lower, self.lanes], w.at[:, xh, z, c, self.lower, self.cols], p)
                for p in z_peers(at)
            ]
        if stage == 1:
            sends.used = 6
            copies = []
            for p in z_peers(at):
                for cols in self.both:
                    up = w.at[:, :, z, c, self.upper, cols]
                    copies.append(sends.make(up, up, p))
            low = w.at[:, xh, :, c, self.lower, self.cols]
            return copies + [sends.make(low, low, p) for p in x_peers(at)]
        sends.used = 15
        copies = []
        for cols in self.both:
            if self.count == 128:
                slots = [w.at[:, :, :, c, :, cols]]
            else:
                slots = [w.at[:, a, b, c, :, cols] for a in range(2) for b in range(4)]
            copies += [sends.make(slot, slot, core_peers(at)[0]) for slot in slots]
        return copies

    def local(self):
        at = self.at
        return pltpu.make_async_copy(
            self.source.at[:, :, self.lanes],
            self.target.at[:, at["xh"], at["z"], at["c"], :, self.cols],
            self.local_sem,
        )

    def begin(self):
        start_all(self.copies(0))
        self.local().start()

    def second(self):
        self.local().wait()
        wait_all(self.copies(0))
        start_all(self.copies(1))

    def third(self):
        wait_all(self.copies(1))
        start_all(self.copies(2))

    def finish(self):
        wait_all(self.copies(2))


class Layout:
    def __init__(self, width):
        self.width, self.half = width, width // 2
        self.part = self.half + 256
        self.total = 2 * self.part
        self.dt_at, self.bc_at = self.half, self.half + 128

    def x(self, v):
        return jnp.concatenate([v[:, : self.half], v[:, self.part : self.part + self.half]], 1)

    def bc(self, v):
        a, b = self.bc_at, self.part + self.bc_at
        return jnp.concatenate([v[:, a : a + 128], v[:, b : b + 128]], 1)

    def dt(self, v, own_heads):
        a, b = self.dt_at, self.part + self.dt_at
        return v[:, a : a + 128] + pltpu.roll(v[:, b : b + 128], own_heads, 1)

    def join(self, x, bc, dt, own_heads):
        lane = lax.broadcasted_iota(jnp.int32, dt.shape, 1)
        first = jnp.where(lane < own_heads, dt, 0.0)
        second = jnp.where(lane < own_heads, pltpu.roll(dt, 128 - own_heads, 1), 0.0)
        return jnp.concatenate(
            [x[:, : self.half], first, bc[:, :128], x[:, self.half :], second, bc[:, 128:]], 1
        )


def own_heads_of(width):
    return width // 128


def chunk_rows(j):
    return pl.ds(pl.multiple_of(j * Q, Q), Q)


def forward_kernel(
    tok_ref, small_ref, hid_ref, wxe_ref, cot_ref, w2_ref,
    zx_ref, xin_ref, bcin_ref, dt_ref, bcc_ref, y_ref, start_ref, gon_ref,
    normed_ref, cot_all_ref, w2_all_ref, stat_ref,
    state, xh, bch, xes, cots, weights, normeds, ys, stats, held,
    cot_send, cot_recv, w_send, w_recv, stat_send, stat_recv, sems,
):
    step = pl.program_id(0)
    steps = pl.num_programs(0) // 2
    per_step = STEP_ROWS // Q
    width = zx_ref.shape[2]
    lay = Layout(width)
    pairs = width // 128
    chunks = stats.shape[0] // 2
    own_heads = own_heads_of(width)
    at = place()
    ring = RingGather(at, cot_ref, cots, cot_send, cot_recv, sems.at[0])
    plane = PlaneGather(at, w2_ref, weights, w_send, w_recv, sems.at[1])

    def results():
        pairs_of = [(cots, cot_all_ref), (weights, w2_all_ref), (normeds, normed_ref)]
        return [pltpu.make_async_copy(a, b, sems.at[2 + i]) for i, (a, b) in enumerate(pairs_of)]

    @pl.when(step == 0)
    def _():
        greet(ring_greets(at) + y_peers(at)[1:2] + plane_greets(at))
        ring.begin()
        plane.begin()
        state[...] = jnp.zeros_like(state)
        xh[0:HALO] = jnp.zeros((HALO, width), F32)
        bch[0:HALO] = jnp.zeros((HALO, bch.shape[1]), F32)

    @pl.when(step == 1)
    def _():
        ring.second()
        plane.second()

    @pl.when(step == 2)
    def _():
        ring.third()

    @pl.when(step == 3)
    def _():
        plane.third()

    @pl.when(step == steps)
    def _():
        ring.finish()
        plane.finish()
        start_all(results())

    @pl.when(step < steps)
    def _():
        rows = hid_ref[...].astype(F32)
        inv_rms = lax.rsqrt(jnp.mean(rows * rows, -1, keepdims=True) + EPS)
        normed = (rows * inv_rms * wide(small_ref, IN_GAIN, 12)).astype(BF16)
        normeds[pl.ds(pl.multiple_of(step * STEP_ROWS, STEP_ROWS), STEP_ROWS)] = normed
        xes[...] = dot(normed, wxe_ref[...])

        @pl.loop(0, per_step)
        def _(j):
            chunk = step * per_step + j
            here = chunk_rows(j)

            @pl.when(chunk > 0)
            def _():
                xh[0:HALO] = xh[Q : Q + HALO]
                bch[0:HALO] = bch[Q : Q + HALO]

            rows16 = tok_ref[chunk]
            tok = columns_of(rows16)
            hp = small_ref[HEAD_ROWS : HEAD_ROWS + 3]
            xe = xes[here]
            x_in, bc_in, dt_in = lay.x(xe), lay.bc(xe), lay.dt(xe, own_heads)
            xin_ref[here] = x_in.astype(BF16)
            bcin_ref[here] = bc_in.astype(BF16)
            dt_ref[here] = dt_in

            def conv(held_rows, new, row, count):
                held_rows[HALO : HALO + Q] = new
                taps = [wide(small_ref, row + t * count, count) for t in range(5)]
                out = taps[4] + taps[3] * new
                for t in range(1, 4):
                    out = out + (taps[3 - t] * held_rows[HALO - t : HALO - t + Q]) * lanes_of(tok, KEEP + t)
                return out

            xc = conv(xh, x_in, X_TAPS, pairs)
            bcc = conv(bch, bc_in, BC_TAPS, 2)
            zx_ref[0, here] = xc
            bcc_ref[here] = bcc
            x_act = xc * sigmoid(xc)
            bc_act = bcc * sigmoid(bcc)
            n = bc_act.shape[1] // 2
            b_low = bc_act[:, :n].astype(BF16)
            c_low = bc_act[:, n:].astype(BF16)
            size, rate, cum2, cum2_t, enter, leave, keep = decays(dt_in, hp, tok)
            same = causal() & (lanes_of(tok, SEG) == rows16[SEG : SEG + 1])
            scores = jnp.where(same, dot(c_low, b_low, NT), 0.0)
            xs = x_act * expand(size, width)
            xs_low = xs.astype(BF16)
            before = state[...]
            before_low = before.astype(BF16)
            start_ref[j] = before_low
            inter = dot(c_low, before_low) * expand(enter, width)
            outs = []
            for pair in range(pairs):
                mixes = [(scores * gaps(cum2, cum2_t, 2 * pair + i)).astype(BF16) for i in range(2)]
                outs.append(
                    dot(jnp.concatenate(mixes, 1), pair_blocks(xs_low[:, pair * 128 : pair * 128 + 128]))
                )
            skip = expand(jnp.broadcast_to(hp[1:2], (8, 128)), width)[0:1]
            y = jnp.concatenate(outs, 1) + inter + skip * x_act
            y_ref[here] = y
            ys[chunk_rows(chunk)] = y
            moved = (xs * expand(leave, width)).astype(BF16)
            keep_all = expand(jnp.broadcast_to(keep, (8, 128)), width)[0:1]
            state[...] = before * keep_all + dot(b_low, moved, TN)

    @pl.when(step >= steps)
    def _():
        rows = pl.ds(pl.multiple_of((step - steps) * STEP_ROWS, STEP_ROWS), STEP_ROWS)
        full = weights.shape[1] * weights.shape[2] * weights.shape[3] * weights.shape[4]
        z = dot(normeds[rows], weights[0].reshape(full, width))
        gon = dot(cots[rows], weights[1].reshape(full, width))
        zx_ref[0] = z
        gon_ref[...] = gon.astype(BF16)
        gated = ys[rows] * (z * sigmoid(z))
        inner = gated * (gon * wide(small_ref, X_TAPS + 5 * pairs, pairs))
        for j in range(per_step):
            chunk = (step - steps) * per_step + j
            cut = slice(j * Q, j * Q + Q)
            stats[pl.ds(chunk, 1), :] = row_sums(gated[cut] * gated[cut])
            stats[pl.ds(chunks + chunk, 1), :] = row_sums(inner[cut])

    @pl.when(step == 2 * steps - 1)
    def _():
        wait_all(results())
        exchange(stats, stats.shape[0], y_peers(at), held, Sends(stat_send, stat_recv))
        inner = width * 4
        scale = lax.rsqrt(stats[0:chunks] / inner + EPS)
        stat_ref[0:chunks] = scale
        stat_ref[chunks : 2 * chunks] = scale * scale * scale * stats[chunks : 2 * chunks] / inner


def row_sums(values):
    total = values[:, 0:128]
    for start in range(128, values.shape[1], 128):
        total = total + values[:, start : start + 128]
    return jnp.sum(total.T, axis=0, keepdims=True)


def half_of(value, xl):
    half = value.shape[-1] // 2
    return jnp.where(xl == 0, value[..., :half], value[..., half:])


class PlaneSum:
    SEMS = 20

    @staticmethod
    def scratch(depth, width):
        cut, half = depth // 2, width // 2
        return [
            pltpu.VMEM((2, 4, depth, width), BF16),
            pltpu.VMEM((3, 4, cut, half), BF16),
            pltpu.VMEM((3, 2, cut, width), BF16),
            pltpu.VMEM((4, cut, half), BF16),
            pltpu.VMEM((2, cut, width), BF16),
            pltpu.VMEM((3, cut, half), BF16),
            pltpu.VMEM((3, cut, half), BF16),
            dma(PlaneSum.SEMS),
            dma(PlaneSum.SEMS),
        ]

    def __init__(self, at, source, refs):
        self.at, self.source = at, source
        (self.got, self.a2, self.b2, self.sa, self.sb, self.a3, self.b3, self.ss, self.rs) = refs
        self.depth, self.width = self.got.shape[2], self.got.shape[3]
        self.cut, self.half = self.depth // 2, self.width // 2

    def columns(self, xl):
        return pl.ds(pl.multiple_of(xl * self.half, 128), self.half)

    def sends(self, used):
        sends = Sends(self.ss, self.rs)
        sends.used = used
        return sends

    def first(self, far, z):
        peer, xh = core_peers(self.at)[0], (self.at["xh"] + far) % 2
        source = self.source.at[xh, z, peer["c"], :, pl.ds(0, self.width)]
        return self.sends((1 - far) * 4 + z).make(source, self.got.at[xh, z], peer)

    def second_x(self, number):
        p, c = x_peers(self.at)[number], self.at["c"]
        source = self.source.at[p["xh"], :, c, pl.ds(0, self.cut), self.columns(p["xl"])]
        return self.sends(8 + number).make(source, self.a2.at[number], p)

    def second_z(self, number):
        p, c = z_peers(self.at)[number], self.at["c"]
        source = self.source.at[:, p["z"], c, pl.ds(self.cut, self.cut), pl.ds(0, self.width)]
        return self.sends(11 + number).make(source, self.b2.at[number], p)

    def third(self):
        sends = self.sends(14)
        copies = []
        for i, p in enumerate(z_peers(self.at)):
            copies.append(sends.make(self.sa.at[p["z"]], self.a3.at[i], p))
        for i, p in enumerate(x_peers(self.at)):
            copies.append(sends.make(self.sb.at[p["xh"], :, self.columns(p["xl"])], self.b3.at[i], p))
        return copies

    def begin(self):
        start_all([self.first(far, z) for far in (1, 0) for z in range(4)])

    def after_cores(self):
        c = self.at["c"]
        for far in (1, 0):
            xh = (self.at["xh"] + far) % 2
            for z in range(4):
                self.first(far, z).wait()
                total = self.source[xh, z, c, :, 0 : self.width].astype(F32) + self.got[xh, z].astype(F32)
                self.source[xh, z, c, :, 0 : self.width] = total.astype(BF16)
            start_all([self.second_x(n) for n in ((1, 2) if far else (0,))])
        start_all([self.second_z(n) for n in range(3)])

    def after_first_axis(self):
        wait_all([self.second_x(n) for n in range(3)] + [self.second_z(n) for n in range(3)])
        at, cut, width = self.at, self.cut, self.width
        c = at["c"]

        @pl.loop(0, 4)
        def _(z):
            total = half_of(self.source[at["xh"], z, c, 0:cut, 0:width], at["xl"]).astype(F32)
            for i in range(3):
                total = total + self.a2[i, z].astype(F32)
            self.sa[z] = total.astype(BF16)

        for xh in range(2):
            total = self.source[xh, at["z"], c, cut : 2 * cut, 0:width].astype(F32)
            for i in range(3):
                total = total + self.b2[i, xh].astype(F32)
            self.sb[xh] = total.astype(BF16)
        start_all(self.third())

    def finish(self, out):
        wait_all(self.third())
        at, cut = self.at, self.cut
        total = self.sa[at["z"]].astype(F32)
        for i in range(3):
            total = total + self.a3[i].astype(F32)
        out[0:cut] = total
        total = half_of(self.sb[at["xh"]], at["xl"]).astype(F32)
        for i in range(3):
            total = total + self.b3[i].astype(F32)
        out[cut : 2 * cut] = total


def plane_greets(at):
    return x_peers(at)[1:] + z_peers(at) + core_peers(at)


PRE, MIX = 4, 4


def owner_block(step, y):
    return (y + jnp.where(step == 0, 2, jnp.where(step == 1, 1, jnp.where(step == 2, 3, 0)))) % 4


def block_rows(number):
    return pl.ds(pl.multiple_of(number * STEP_ROWS, STEP_ROWS), STEP_ROWS)


def backward_kernel(
    tok_ref, stat_ref, small_ref, zx_ref, gon_ref, y_ref, xin_ref, bcin_ref, dt_ref, bcc_ref, start_ref,
    cot_ref, normed_ref, w2_ref, wxe_ref,
    out_ref, back_ref, gzo_ref, gxe_ref, sums_ref, bcs_ref,
    adjoint, dh, dbh, gkx, gkbc, ghead, ggain, cots, normeds, weight, wxe, outs_low, z_low, dy_all, part, source,
    held, bc_got, small_send, small_recv, bc_send, bc_recv, sems, *refs,
):
    step = pl.program_id(0)
    per_step = STEP_ROWS // Q
    width = zx_ref.shape[2]
    pairs = width // 128
    own_heads = own_heads_of(width)
    lay = Layout(width)
    chunks = tok_ref.shape[0]
    model = cots.shape[1]
    at = place()
    ring_out = RingScatter(at, part, refs[0:3])
    ring_in = RingScatter(at, part, refs[3:6])
    plane_zo = PlaneSum(at, source, refs[6:15])
    plane_xe = PlaneSum(at, source, refs[15:24])
    peers = group_peers(at)
    loads = [
        pltpu.make_async_copy(a, b, sems.at[n])
        for n, (a, b) in enumerate(
            [(w2_ref.at[1], weight), (cot_ref, cots), (normed_ref, normeds), (wxe_ref, wxe), (w2_ref.at[0], weight)]
        )
    ]

    def put_part(owner, value):
        low = value.astype(BF16)
        for x in range(2):
            part[owner * 2 + x] = low[x * Q : x * Q + Q]

    def put_grad(values, start, half):
        for quarter in range(4):
            cut = slice(quarter * (model // 4), (quarter + 1) * (model // 4))
            value = dot(values[0][:, cut], values[1], TN).astype(BF16)
            value = value.reshape(2, 2, model // 16, value.shape[1])
            xh, z = quarter // 2, (quarter % 2) * 2
            for n in range(2):
                first = n * start[1] + start[0]
                source[xh, z : z + 2, :, :, first : first + half] = value[..., n * half : n * half + half]

    @pl.when(step == 0)
    def _():
        start_all(loads[:4])
        greet_begin(peers + plane_greets(at))
        adjoint[...] = jnp.zeros_like(adjoint)
        dh[...] = jnp.zeros_like(dh)
        dbh[...] = jnp.zeros_like(dbh)
        gkx[...] = jnp.zeros_like(gkx)
        gkbc[...] = jnp.zeros_like(gkbc)
        ghead[...] = jnp.zeros_like(ghead)
        ggain[...] = jnp.zeros_like(ggain)
        loads[0].wait()

    @pl.when(step < PRE)
    def _():
        owner = owner_block(step, at["y"])
        rows = block_rows(owner)
        columns = []
        for j in range(per_step):
            chunk = owner * per_step + j
            columns.append(
                columns_of(jnp.concatenate([stat_ref[pl.ds(chunk, 1), :], stat_ref[pl.ds(chunks + chunk, 1), :]], 0))
            )
        columns = jnp.concatenate(columns, 0)
        scale, coef = columns[:, 0:1], columns[:, 1:2]
        gain = wide(small_ref, X_TAPS + 5 * pairs, pairs)
        z, y, gon = zx_ref[0], y_ref[...], gon_ref[...].astype(F32)
        z_sig = sigmoid(z)
        z_act = z * z_sig
        gated = y * z_act
        scaled = gated * scale
        out_low = (scaled * gain).astype(BF16)
        outs_low[rows] = out_low
        gkx[5] += rows8(gon * scaled)
        grad_gated = scale * (gon * gain) - gated * coef
        dy_all[rows] = (grad_gated * z_act).astype(BF16)
        z_low[rows] = (grad_gated * y * (z_sig * (1.0 + z * (1.0 - z_sig)))).astype(BF16)
        put_part(owner, dot(out_low, weight[...], NT))

    @pl.when(step == 0)
    def _():
        greet_end(peers + plane_greets(at))
        ring_out.send_far()

    @pl.when(step == 1)
    def _():
        ring_out.send_up()

    @pl.when(step == 2)
    def _():
        ring_out.send_down()

    @pl.when(step == PRE)
    def _():
        loads[4].start()
        loads[1].wait()
        loads[2].wait()
        half = width // 2
        put_grad((cots, outs_low[...]), (half, width), half)
        put_grad((normeds, z_low[...]), (0, width), half)
        plane_zo.begin()
        ring_out.second()

    @pl.when(step == PRE + 1)
    def _():
        plane_zo.after_cores()

    @pl.when(step == PRE + 2)
    def _():
        ring_out.third(out_ref)

    @pl.when(step == PRE + MIX - 1)
    def _():
        plane_zo.after_first_axis()
        ring_out.finish(out_ref)

    @pl.when((step >= PRE) & (step < PRE + MIX))
    def _():
        @pl.loop(0, per_step)
        def _(turn_in):
            j = per_step - 1 - turn_in
            chunk = (PRE + MIX - 1 - step) * per_step + j
            here = chunk_rows(j)
            there = chunk_rows(chunk)

            @pl.when(chunk < chunks - 1)
            def _():
                dh[Q : Q + HALO] = dh[0:HALO]
                dbh[Q : Q + HALO] = dbh[0:HALO]

            rows16 = tok_ref[chunk]
            tok = columns_of(rows16)
            hp = small_ref[HEAD_ROWS : HEAD_ROWS + 3]
            dt_in = dt_ref[here]
            xc = zx_ref[0, here]
            bcc = bcc_ref[here]
            x_sig = sigmoid(xc)
            x_act = xc * x_sig
            bc_sig = sigmoid(bcc)
            bc_act = bcc * bc_sig
            n = bc_act.shape[1] // 2
            b_low = bc_act[:, :n].astype(BF16)
            c_low = bc_act[:, n:].astype(BF16)
            size, rate, cum2, cum2_t, enter, leave, keep = decays(dt_in, hp, tok)
            same = causal() & (lanes_of(tok, SEG) == rows16[SEG : SEG + 1])
            scores = jnp.where(same, dot(c_low, b_low, NT), 0.0)
            step_all = expand(size, width)
            leave_all = expand(leave, width)
            xs = x_act * step_all
            xs_low = xs.astype(BF16)
            moved = (xs * leave_all).astype(BF16)
            dy_low = dy_all[there]
            dy = dy_low.astype(F32)
            dy_in = (dy * expand(enter, width)).astype(BF16)

            skip = expand(jnp.broadcast_to(hp[1:2], (8, 128)), width)[0:1]
            before_low = start_ref[j]
            after = adjoint[...]
            after_low = after.astype(BF16)

            from_state = dot(b_low, after_low)
            outs = []
            dscores = jnp.zeros((Q, Q), F32)
            for pair in range(pairs):
                cut = slice(pair * 128, pair * 128 + 128)
                dys = pair_blocks(dy_low[:, cut])
                inner = dot(dys, xs_low[:, cut], NT)
                mixes = []
                for i in range(2):
                    gap = gaps(cum2, cum2_t, 2 * pair + i)
                    mixes.append((scores * gap).astype(BF16))
                    dscores = dscores + inner[i * Q : i * Q + Q] * gap
                outs.append(dot(jnp.concatenate(mixes, 0), dys, TN))
            intra = jnp.concatenate(outs, 1)
            dscores = jnp.where(same, dscores, 0.0).astype(BF16)

            dxs = intra + leave_all * from_state
            dx_act = dxs * step_all + skip * dy
            gkx[6] += rows8(dy * x_act)
            plus = head_sums(dy * (y_ref[here] - skip * x_act))
            through = moved.astype(F32) * from_state
            minus = head_sums(xs_low.astype(F32) * intra + through)
            direct = head_sums(dxs * x_act)
            keep_all = expand(jnp.broadcast_to(keep, (8, 128)), width)[0:1]
            at_end = rows8(through) + keep_all * rows8(after * before_low.astype(F32))
            at_end = jnp.sum(head_sums(at_end), axis=0, keepdims=True)
            last_row = lax.broadcasted_iota(jnp.int32, (Q, 128), 0) == Q - 1
            dcum = plus - minus + jnp.where(last_row, at_end, 0.0)
            tri = jnp.where(causal(), 1.0, 0.0)
            drate = dot_exact(tri, dcum, TN)
            dstep = direct - jnp.exp(hp[0:1]) * drate
            ddt = dstep * sigmoid(dt_in + hp[2:3])
            ghead[0] += rows8(drate * rate)
            ghead[1] += rows8(ddt)

            dc = dot(dscores, b_low) + dot(dy_in, before_low, NT)
            db = dot(dscores, c_low, TN) + dot(moved, after_low, NT)
            adjoint[...] = keep_all * after + dot(c_low, dy_in, TN)

            def conv_back(held_rows, grad, new, row, count, out):
                held_rows[0:Q] = grad
                taps = [wide(small_ref, row + t * count, count) for t in range(4)]
                total = taps[3] * grad
                out[3] += rows8(new * grad)
                out[4] += rows8(grad)
                for t in range(1, 4):
                    piece = held_rows[t : t + Q] * lanes_of(tok, AHEAD + t)
                    total = total + taps[3 - t] * piece
                    out[3 - t] += rows8(new * piece)
                return total

            dxc = dx_act * (x_sig * (1.0 + xc * (1.0 - x_sig)))
            dx_in = conv_back(dh, dxc, xin_ref[here].astype(F32), X_TAPS, pairs, gkx)
            dbcc = jnp.concatenate([db, dc], 1) * (bc_sig * (1.0 + bcc * (1.0 - bc_sig)))
            dbc_in = conv_back(dbh, dbcc, bcin_ref[here].astype(F32), BC_TAPS, 2, gkbc)
            cots[there, 0 : lay.total] = lay.join(dx_in, dbc_in, ddt, own_heads).astype(BF16)

    @pl.when(step == PRE + MIX)
    def _():
        plane_zo.finish(gzo_ref)
        loads[3].wait()
        loads[4].wait()

        def part_in(number):
            owner = (at["y"] + number) % 4
            rows = block_rows(owner)
            value = dot(z_low[rows], weight[...], NT) + dot(cots[rows, 0 : lay.total], wxe[...], NT)
            ggain[...] += rows8(value * normeds[rows].astype(F32))
            put_part(owner, value)

        part_in(2)
        ring_in.send_far()
        put_grad((normeds, cots[:, 0 : lay.total]), (0, lay.part), lay.part)
        plane_xe.begin()
        part_in(1)
        ring_in.send_up()
        part_in(3)
        ring_in.send_down()
        ring_in.second()
        plane_xe.after_cores()
        part_in(0)

        sums_ref[...] = jnp.zeros_like(sums_ref)
        for t in range(5):
            put_wide(sums_ref, 2 * t, jnp.sum(gkbc[t], axis=0, keepdims=True))
        put_wide(sums_ref, IN_GAIN, jnp.sum(ggain[...], axis=0, keepdims=True) / wide(small_ref, IN_GAIN, model // 128))
        for t in range(7):
            put_wide(sums_ref, X_TAPS + t * pairs, jnp.sum(gkx[t], axis=0, keepdims=True))
        for t in range(2):
            put_wide(sums_ref, X_TAPS + 7 * pairs + t, jnp.sum(ghead[t], axis=0, keepdims=True))
        steps = [core_peers(at), x_peers(at), z_peers(at), y_peers(at)]
        sends = Sends(small_send, small_recv)
        rows = sums_ref.shape[0]
        exchange(sums_ref, rows, steps[0], held.at[0], sends)
        exchange(sums_ref, rows, steps[1], held.at[1], sends)
        plane_xe.after_first_axis()
        exchange(sums_ref, rows, steps[2], held.at[2], sends)
        ring_in.third(back_ref)
        exchange(sums_ref, SMALL_SHARED, steps[3], held.at[3], sends)
        plane_xe.finish(gxe_ref)
        bc_got[at["xl"], at["y"]] = gxe_ref[:, lay.bc_at : lay.bc_at + 128]
        slot = bc_got.at[at["xl"], at["y"]]
        sends = Sends(bc_send, bc_recv)
        wait_all([sends.start(slot, slot, p) for p in peers])
        for n in range(2):
            bcs_ref[n] = jnp.sum(bc_got[n], axis=0)
        ring_in.finish(back_ref)


def put_wide(ref, row, value):
    for i in range(value.shape[1] // 128):
        ref[row + i : row + i + 1] = value[:, i * 128 : i * 128 + 128]


def gather_kernel(
    hid, ids_ref, wx_ref, wdt_ref, wbc_ref, gain_ref, kx_ref, kxb_ref, kbc_ref, kbcb_ref, og_ref, al_ref, ds_ref, db_ref,
    hid_all, wxe_all, small_all, tok_all,
    wxe, bc_got, bc_rows, held, lanes,
    hid_send, hid_recv, bc_send, bc_recv, w_send, w_recv, wbc_send, wbc_recv, small_send, small_recv, sems,
):
    at = place()
    peers = group_peers(at)
    y, xl = at["y"], at["xl"]
    depth, half = wx_ref.shape
    own_heads = wdt_ref.shape[0]
    ring = RingGather(at, hid, hid_all, hid_send, hid_recv, sems.at[0])
    plane = PlaneGather(at, wxe, wxe_all, w_send, w_recv, sems.at[1], 0, half + 128)
    plane_bc = PlaneGather(at, wxe, wxe_all, wbc_send, wbc_recv, sems.at[2], half + 128, 128)

    wxe[0, :, 0:half] = wx_ref[...]
    lanes[...] = jnp.zeros_like(lanes)
    lanes[0:own_heads, 0:depth] = wdt_ref[...].astype(F32)
    wxe[0, :, half : half + 128] = columns_of(lanes[:, 0:128])[0:depth].astype(BF16)
    lanes[...] = jnp.zeros_like(lanes)
    lanes[0:2, 0:4] = kbc_ref[...].astype(F32)
    taps_bc = columns_of(lanes[:, 0:128])[0:4, 0:2]
    bc_slot = bc_got.at[y * 2 + xl]
    bc_got[y * 2 + xl, 0:12] = wbc_ref[...].astype(F32)

    def placed(pieces, width, start):
        lanes[...] = jnp.zeros_like(lanes)
        row = 0
        for piece in pieces:
            count, size = piece.shape
            lanes[row : row + count, 0:size] = piece[...].astype(F32)
            row += count
        return pltpu.roll(lanes[:, 0:width], start, 1)

    dp = at["xh"] * 8 + at["z"] * 2 + at["c"]
    everyone = dp * 8 + y * 2 + xl
    small_all[...] = jnp.zeros_like(small_all)
    value = placed([taps_bc, kbcb_ref], 256, everyone * kbc_ref.shape[0])
    for t in range(5):
        put_wide(small_all, BC_TAPS + 2 * t, value[t : t + 1])
    value = placed([gain_ref], lanes.shape[1], everyone * gain_ref.shape[1])
    put_wide(small_all, IN_GAIN, value[0:1])
    value = placed([kx_ref, kxb_ref, og_ref], 2 * half, xl * half + dp * kx_ref.shape[1])
    for t in range(6):
        put_wide(small_all, X_TAPS + t * (half // 64), value[t : t + 1])
    value = placed([al_ref, ds_ref, db_ref], 128, xl * own_heads)
    small_all[HEAD_ROWS : HEAD_ROWS + 3] = jnp.where(dp == 0, value[0:3], 0.0)

    greet_begin(peers + plane_greets(at))
    token_info(ids_ref[xl], tok_all)
    greet_end(peers + plane_greets(at))
    sends = Sends(bc_send, bc_recv)
    bc_copies = [sends.start(bc_slot, bc_slot, p) for p in peers]
    small_sends = Sends(small_send, small_recv)
    small = Exchange(small_all, SMALL_SHARED, y_peers(at), held.at[0], small_sends)
    plane.begin()
    ring.begin()

    wait_all(bc_copies)
    for m in range(8):
        bc_rows[12 * m : 12 * m + 12] = bc_got[m, 0:12]
    wxe[0, :, half + 128 : half + 256] = half_of(bc_rows[...], xl).astype(BF16)
    plane_bc.begin()
    small.finish()
    small = Exchange(small_all, SMALL_ROWS, core_peers(at), held.at[1], small_sends)
    plane.second()
    small.finish()
    small = Exchange(small_all, SMALL_ROWS, x_peers(at), held.at[2], small_sends)
    plane_bc.second()
    ring.second()
    small.finish()
    small = Exchange(small_all, SMALL_ROWS, z_peers(at), held.at[3], small_sends)
    plane.third()
    plane_bc.third()
    ring.third()
    small.finish()
    plane.finish()
    plane_bc.finish()
    ring.finish()


def block(rows, w, index):
    return pl.BlockSpec((rows, w), lambda i: (index(i), 0))


def whole(shape):
    return pl.BlockSpec(shape, lambda i: (0,) * len(shape), pipeline_mode=pl.Buffered(1))


def whole_out(shape):
    return pl.BlockSpec(shape, lambda i: (0,) * len(shape))


ANY = pl.BlockSpec(memory_space=pl.ANY)
IN_VMEM = pl.BlockSpec(memory_space=pltpu.VMEM)


def like(shape, dtype):
    return jax.ShapeDtypeStruct(shape, dtype)


def dma(count):
    return pltpu.SemaphoreType.DMA((count,))


def remote_params(cid):
    return pltpu.CompilerParams(collective_id=cid, has_side_effects=True, vmem_limit_bytes=VMEM_LIMIT)


def gather_call(hidden, ids, w_x, w_dt, w_bc, small_args):
    _, rows, model = hidden.shape
    depth, half = w_x.shape
    part = half + 256
    args = [ids, w_x, w_dt, w_bc, *small_args]
    return pl.pallas_call(
        gather_kernel,
        in_specs=[ANY] + [IN_VMEM] * len(args),
        out_specs=[ANY, ANY, IN_VMEM, IN_VMEM],
        out_shape=[
            like((8 * rows, model), BF16),
            like((1, 2, 4, 2, depth, 2 * part), BF16),
            like((SMALL_ROWS, 128), F32),
            like((ids.shape[1], 16, Q), F32),
        ],
        scratch_shapes=[
            pltpu.VMEM((1, depth, part), BF16),
            pltpu.VMEM((8, 16, w_bc.shape[1]), F32),
            pltpu.VMEM((depth, w_bc.shape[1]), F32),
            pltpu.VMEM((4, 3, SMALL_ROWS, 128), F32),
            pltpu.VMEM((8, model), F32),
            dma(7), dma(7), dma(7), dma(7), dma(31), dma(31), dma(31), dma(31), dma(10), dma(10), dma(3),
        ],
        name="gather",
        compiler_params=remote_params(0),
    )(hidden, *args)


def forward_call(tok, small, hid_all, wxe, cotangent, w2):
    length, model = hid_all.shape
    total = wxe.shape[1]
    depth, half = w2.shape[1], w2.shape[2]
    width = 2 * half
    steps = length // STEP_ROWS
    chunks = length // Q

    def early(i):
        return jnp.minimum(i, steps - 1)

    def late(i):
        return jnp.maximum(i - steps, 0)

    return pl.pallas_call(
        forward_kernel,
        grid=(2 * steps,),
        in_specs=[whole(tok.shape), whole(small.shape), block(STEP_ROWS, model, early), whole(wxe.shape), ANY, ANY],
        out_specs=[pl.BlockSpec((1, STEP_ROWS, width), lambda i: (i // steps, i % steps, 0)),
                   block(STEP_ROWS, width, early), block(STEP_ROWS, 256, early),
                   block(STEP_ROWS, 128, early), block(STEP_ROWS, 256, early), block(STEP_ROWS, width, early),
                   pl.BlockSpec((STEP_ROWS // Q, 128, width), lambda i: (early(i), 0, 0)),
                   block(STEP_ROWS, width, late), ANY, ANY, ANY, whole_out((2 * chunks, Q))],
        out_shape=[
            like((2, length, width), F32), like((length, width), BF16), like((length, 256), BF16),
            like((length, 128), F32),
            like((length, 256), F32), like((length, width), F32), like((chunks, 128, width), BF16),
            like((length, width), BF16), like((length, model), BF16), like((length, model), BF16),
            like((2, 2, 4, 2, depth, width), BF16), like((2 * chunks, Q), F32),
        ],
        scratch_shapes=[
            pltpu.VMEM((128, width), F32),
            pltpu.VMEM((Q + HALO, width), F32),
            pltpu.VMEM((Q + HALO, 256), F32),
            pltpu.VMEM((STEP_ROWS, total), F32),
            pltpu.VMEM((length, model), BF16),
            pltpu.VMEM((2, 2, 4, 2, depth, width), BF16),
            pltpu.VMEM((length, model), BF16),
            pltpu.VMEM((length, width), F32),
            pltpu.VMEM((2 * chunks, Q), F32),
            pltpu.VMEM((3, 2 * chunks, Q), F32),
            dma(7), dma(7), dma(31), dma(31), dma(3), dma(3), dma(5),
        ],
        name="mix_forward",
        compiler_params=remote_params(1),
    )(tok, small, hid_all, wxe, cotangent, w2)


def backward_call(tok, stat, small, zx, gon, y, xin, bcin, dt, bcc, starts, cots, normed, w2, wxe):
    length, width = y.shape
    model, total = wxe.shape
    depth = model // 16
    steps = length // STEP_ROWS

    def both(i):
        first = owner_block(i, lax.axis_index("mp") // 2)
        return jnp.where(i < PRE, first, jnp.maximum(PRE + MIX - 1 - i, 0))

    def mix(i):
        return jnp.clip(PRE + MIX - 1 - i, 0, steps - 1)

    def pre(i):
        return owner_block(jnp.minimum(i, PRE - 1), lax.axis_index("mp") // 2)

    return pl.pallas_call(
        backward_kernel,
        grid=(PRE + MIX + 1,),
        in_specs=[whole(tok.shape), whole(stat.shape), whole(small.shape),
                  pl.BlockSpec((1, STEP_ROWS, width), lambda i: (jnp.where(i < PRE, 1, 0), both(i), 0)),
                  block(STEP_ROWS, width, pre), block(STEP_ROWS, width, both),
                  block(STEP_ROWS, width, mix), block(STEP_ROWS, 256, mix), block(STEP_ROWS, 128, mix),
                  block(STEP_ROWS, 256, mix),
                  pl.BlockSpec((STEP_ROWS // Q, 128, width), lambda i: (mix(i), 0, 0)), ANY, ANY, ANY, ANY],
        out_specs=[whole((2, Q, model)), whole((2, Q, model)), whole((depth, width)), whole((depth, total // 2)),
                   whole((72, 128)), whole((2, depth, 128))],
        out_shape=[
            like((2, Q, model), BF16), like((2, Q, model), BF16), like((depth, width), F32),
            like((depth, total // 2), F32), like((72, 128), F32), like((2, depth, 128), F32),
        ],
        scratch_shapes=[
            pltpu.VMEM((128, width), F32),
            pltpu.VMEM((Q + HALO, width), F32),
            pltpu.VMEM((Q + HALO, 256), F32),
            pltpu.VMEM((7, 8, width), F32),
            pltpu.VMEM((5, 8, 256), F32),
            pltpu.VMEM((2, 8, 128), F32),
            pltpu.VMEM((8, model), F32),
            pltpu.VMEM((length, model), BF16),
            pltpu.VMEM((length, model), BF16),
            pltpu.VMEM((model, width), BF16),
            pltpu.VMEM((model, total), BF16),
            pltpu.VMEM((length, width), BF16),
            pltpu.VMEM((length, width), BF16),
            pltpu.VMEM((length, width), BF16),
            pltpu.VMEM((8, Q, model), BF16),
            pltpu.VMEM((2, 4, 2, depth, 2 * width), BF16),
            pltpu.VMEM((4, 3, 72, 128), F32),
            pltpu.VMEM((2, 4, depth, 128), F32),
            dma(10), dma(10), dma(7), dma(7), dma(5),
            *RingScatter.scratch(model),
            *RingScatter.scratch(model),
            *PlaneSum.scratch(depth, 2 * width),
            *PlaneSum.scratch(depth, total),
        ],
        name="mix_backward",
        compiler_params=remote_params(2),
    )(tok, stat, small, zx, gon, y, xin, bcin, dt, bcc, starts, cots, normed, w2, wxe)


def token_info(ids, out):
    chunks = ids.shape[0]
    seg = ids.astype(F32)
    lane = lax.broadcasted_iota(jnp.int32, seg.shape, 1)
    row = lax.broadcasted_iota(jnp.int32, seg.shape, 0)

    def chunk_back(v):
        return jnp.where(row == 0, -1.0, pltpu.roll(v, 1, 0))

    def chunk_ahead(v):
        return jnp.where(row == chunks - 1, -1.0, pltpu.roll(v, chunks - 1, 0))

    def flag(mask):
        return jnp.where(mask, 1.0, 0.0)

    tail = jnp.broadcast_to(seg[:, Q - 1 :], seg.shape)
    last = chunk_back(tail)
    rows = {SEG: seg, ENTER: flag(seg == last), LEAVE: flag(seg == tail), CARRY: flag(tail == last)}
    for j in range(1, 4):
        turned = pltpu.roll(seg, j, 1)
        rows[KEEP + j] = flag(jnp.where(lane < j, chunk_back(turned), turned) == seg)
        turned = pltpu.roll(seg, Q - j, 1)
        rows[AHEAD + j] = flag(jnp.where(lane >= Q - j, chunk_ahead(turned), turned) == seg)
    out[...] = jnp.zeros_like(out)
    for number, value in rows.items():
        for chunk in range(chunks):
            out[chunk, number : number + 1] = value[chunk : chunk + 1]


def finish_kernel(
    hid, cot, got, back, small, gzo, gxe, sums, bcs,
    mixed, g_hid, g_gain, g_wz, g_wx, g_wdt, g_wbc, g_kx, g_kxb, g_kbc, g_kbcb, g_al, g_ds, g_db, g_og, g_wo,
):
    at = place()
    xl, mp = at["xl"], at["y"] * 2 + at["xl"]
    dp = at["xh"] * 8 + at["z"] * 2 + at["c"]
    everyone = dp * 8 + mp
    depth, half = g_wz.shape
    model = hid.shape[2]
    own_heads = g_al.shape[1]
    gain_in = wide(small, IN_GAIN, model // 128)
    for s in range(hid.shape[0]):
        h = hid[s].astype(F32)
        mixed[s] = (h + got[s].astype(F32)).astype(BF16)
        inv = lax.rsqrt(jnp.mean(h * h, -1, keepdims=True) + EPS)
        hat = back[s].astype(F32) * gain_in
        g_hid[s] = (
            cot[s].astype(F32) + inv * hat - h * ((inv * inv * inv) * jnp.mean(hat * h, -1, keepdims=True))
        )
    g_wz[...] = gzo[:, 0:half]
    g_wo[...] = gzo[:, half : 2 * half].T
    g_wx[...] = gxe[:, 0:half]
    g_wdt[...] = gxe[:, half : half + 128].T[0:own_heads]

    def cut(values, start, count):
        width = values.shape[1]
        return pltpu.roll(values, lax.rem(width - start, width), 1)[:, 0:count]

    def tall(row, count):
        return jnp.broadcast_to(wide(sums, row, count), (8, count * 128))

    pairs = half // 64
    g_gain[...] = cut(tall(IN_GAIN, model // 128), everyone * g_gain.shape[1], g_gain.shape[1])[0:1]
    rows = jnp.concatenate([wide(sums, X_TAPS + t * pairs, pairs) for t in range(7)] + [jnp.zeros((1, 2 * half), F32)], 0)
    own = cut(rows, xl * half + dp * g_kx.shape[1], g_kx.shape[1])
    g_kx[...] = own[0:4]
    g_kxb[...] = own[4:5]
    g_og[...] = own[5:6]
    per_head = head_sums(rows)
    g_ds[...] = cut(per_head, xl * own_heads, own_heads)[6:7]
    per_head = jnp.concatenate([sums[64:72]], 0)
    per_head = cut(per_head, xl * own_heads, own_heads)
    first = X_TAPS + 7 * pairs - 64
    g_al[...] = per_head[first : first + 1]
    g_db[...] = per_head[first + 1 : first + 2]
    rows = jnp.concatenate([wide(sums, BC_TAPS + 2 * t, 2) for t in range(5)] + [jnp.zeros((3, 256), F32)], 0)
    own = cut(rows, everyone * 2, 128)
    g_kbc[...] = jnp.concatenate([own, jnp.zeros((120, 128), F32)], 0).T[0:2, 0:4]
    g_kbcb[...] = own[4:5, 0:2]
    total = jnp.concatenate([bcs[0], bcs[1]], 1)
    g_wbc[...] = pltpu.roll(total, lax.rem(depth - mp * 12, depth), 0)[0:12]


def finish_call(hidden, cotangent, got, back, small, gzo, gxe, sums, bcs, own_heads):
    depth, half = gzo.shape[0], gzo.shape[1] // 2
    shapes = [
        (hidden.shape, BF16), (hidden.shape, F32), ((1, hidden.shape[2] // 128), F32), ((depth, half), F32),
        ((depth, half), F32), ((own_heads, depth), F32), ((12, 256), F32), ((4, half // 16), F32),
        ((1, half // 16), F32), ((2, 4), F32), ((1, 2), F32), ((1, own_heads), F32), ((1, own_heads), F32),
        ((1, own_heads), F32), ((1, half // 16), F32), ((half, depth), F32),
    ]
    return pl.pallas_call(
        finish_kernel,
        in_specs=[IN_VMEM] * 9,
        out_specs=[IN_VMEM] * len(shapes),
        out_shape=[like(*shape) for shape in shapes],
        name="finish",
        compiler_params=pltpu.CompilerParams(vmem_limit_bytes=VMEM_LIMIT),
    )(hidden, cotangent, got, back, small, gzo, gxe, sums, bcs)


def local(
    hidden, segments, cotangent, norm_gain, w_z, w_x, w_dt, w_bc, conv_x, conv_x_bias, conv_bc, conv_bc_bias,
    a_log, d_skip, dt_bias, out_gain, w_out,
):
    _, _, model = hidden.shape
    depth, half = w_z.shape
    width = 2 * half
    own_heads = a_log.shape[0]
    lay = Layout(width)

    small_args = [
        norm_gain[None], conv_x, conv_x_bias[None], conv_bc.T, conv_bc_bias[None], out_gain[None],
        a_log[None], d_skip[None], dt_bias[None],
    ]
    ids = segments.reshape(segments.shape[0], -1, Q)
    hid_all, wxe_all, small, tok = gather_call(hidden, ids, w_x, w_dt.T, w_bc, small_args)
    full_xe = wxe_all.reshape(model, lay.total)
    w2 = jnp.stack([w_z, w_out.T])
    zx, xin, bcin, dt, bcc, y_out, starts, gon, normed, cot_all, w2_all, stat = forward_call(
        tok, small, hid_all, full_xe, cotangent, w2
    )
    got_out, grad_normed, zo_sum, xe_sum, sums, bc_sum = backward_call(
        tok, stat, small, zx, gon, y_out, xin, bcin, dt, bcc, starts, cot_all, normed,
        w2_all.reshape(2, model, width), full_xe,
    )
    (
        mixed, g_hid, g_gain, g_wz, g_wx, g_wdt, g_wbc, g_kx, g_kxb, g_kbc, g_kbcb, g_al, g_ds, g_db, g_og, g_wo,
    ) = finish_call(hidden, cotangent, got_out, grad_normed, small, zo_sum, xe_sum, sums, bc_sum, own_heads)
    return (
        mixed, g_hid, g_gain[0], g_wz, g_wx, g_wdt.T, g_wbc, g_kx, g_kxb[0], g_kbc.T, g_kbcb[0], g_al[0], g_ds[0],
        g_db[0], g_og[0], g_wo,
    )


def solution(mesh):
    in_specs = (
        P("dp", "mp", None),
        P("dp", None),
        P("dp", "mp", None),
        P(("dp", "mp")),
        P("dp", "mp"),
        P("dp", "mp"),
        P("dp", "mp"),
        P(("dp", "mp"), None),
        P(None, ("mp", "dp")),
        P(("mp", "dp")),
        P(None, ("dp", "mp")),
        P(("dp", "mp")),
        P("mp"),
        P("mp"),
        P("mp"),
        P(("mp", "dp")),
        P("mp", "dp"),
    )
    out_specs = (
        P("dp", "mp", None),
        P("dp", "mp", None),
        P(("dp", "mp")),
        P("dp", "mp"),
        P("dp", "mp"),
        P("dp", "mp"),
        P(("dp", "mp"), None),
        P(None, ("mp", "dp")),
        P(("mp", "dp")),
        P(None, ("dp", "mp")),
        P(("dp", "mp")),
        P("mp"),
        P("mp"),
        P("mp"),
        P(("mp", "dp")),
        P("mp", "dp"),
    )
    return jax.shard_map(local, mesh=mesh, in_specs=in_specs, out_specs=out_specs, check_vma=False)
```

time: 255 us -> 204 us (0.80)
  matrix products: 26.2 us -> 0 us
  other arithmetic: 17 us -> 1.6 us
  local copies, waits for them, and re-layouts: 17.1 us -> 3.01 us
  Pallas kernels: 193 us -> 199 us
    dot_general x6 -> x0, matrix products: 26.2 us -> none  [dot(): return lax.dot_general(a, b, (dims, ((), ())), preferred_element_type=F32)]
    pallas_call x2, Pallas kernels: 92.4 us -> 102 us  [the longest x1 97.6 us: backward_call(): pl.pallas_call(backward_kernel, grid=(PRE + MIX + 1,), in_specs=[whole(to...]
    convert_element_type x5 -> x0, other arithmetic: 7.25 us -> none  [the longest x1 4.96 us: local(): (grad_gated * y_out * (z_sig * (1.0 + z_in * (1.0 - z_sig)))).astype(BF16)]
    reduce_sum x4 -> x0, other arithmetic: 3.13 us -> none  [the longest x1 1.8 us: local(): inv_own = lax.rsqrt(jnp.mean(h * h, -1, keepdims=True) + EPS)]
    pallas_call x1, Pallas kernels: 52.8 us -> 49.7 us  [forward_call(): pl.pallas_call(forward_kernel, grid=(2 * steps,), in_specs=[whole(tok.sha...]
    unnamed x35 -> x2, local copies, waits for them, and re-layouts: 5.91 us -> 3.01 us
    another operation x2 -> x0, other arithmetic: 2.88 us -> none  [the longest x1 2.81 us: local(): g_zo = jnp.stack([g_z, g_o]).reshape(2, 2, 4, 2, depth, width)]
    slice x16 -> x0, local copies, waits for them, and re-layouts: 2.73 us -> none  [the longest x1 0.67 us: local(): xe_sum[:, :half]]
where the time goes in v2:
time: 204 us
  Pallas kernels  199 us (98%)
  local copies, waits for them, and re-layouts  3.01 us (1%)
    pallas_call x1, Pallas kernels, backward_call(): pl.pallas_call(backward_kernel, grid=(PRE + MIX + 1,), in_specs=[whole(to...  97.6 us
    pallas_call x1, Pallas kernels, forward_call(): pl.pallas_call(forward_kernel, grid=(2 * steps,), in_specs=[whole(tok.sha...  49.7 us
    pallas_call x1, Pallas kernels, gather_call(): pl.pallas_call(gather_kernel, in_specs=[ANY] + [IN_VMEM] * len(args), out...  46.9 us
    pallas_call x1, Pallas kernels, finish_call(): pl.pallas_call(finish_kernel, in_specs=[IN_VMEM] * 9, out_specs=[IN_VMEM]...  4.56 us

profile of v2, /device:TPU:0, one launch (start us, length us, event | category | flops | bytes accessed | tf_op | source)
XLA Modules:
  0.0 204.0 jit_solution(7352371467028747295)
XLA Ops:
  0.6 1.3 copy.36
  1.9 1.6 pad_maximum_fusion.w2_ref
  3.5 46.9 %gather.1 = (bf16[1024,1536]{1,0:T(8,128)(2,1)}, bf16[1,2,4,2,96,1280]{5,4,3,2,1,0:T(8,128)(2,1)}, f32[64,128]{1,0:T(8,128)}, f32[8,16,128]{2,1,0:T(8,128)}) custom-call(bf16[2,128,1536]{2,1,0:T(8,128)(2,1)} %hid.3, s32[2,8,128]{2,1,0:T(8,128)} %bitcast.33, bf16[96,384]{1,0:T(8,128)(2,1)} %wx_ref.1, bf16[6,96]{1,0:T(8,128)(2,1)} %bitcast.35, ...), custom_call_target="tpu_custom_call" | custom-call | tf_op jit(solution)/shard_map/gather/pallas_call | solution.py:1103
  50.4 49.7 %mix_forward.1 = (f32[2,1024,768]{2,1,0:T(8,128)}, bf16[1024,768]{1,0:T(8,128)(2,1)}, bf16[1024,256]{1,0:T(8,128)(2,1)}, f32[1024,128]{1,0:T(8,128)}, f32[1024,2...) custom-call(f32[8,16,128]{2,1,0:T(8,128)} %get-tuple-element.54.tok_, ...), custom_call_target="tpu_custom_call" | custom-call | tf_op jit(solution)/shard_map/mix_forward/pallas_call | solution.py:1140
  100.1 97.6 %mix_backward.1 = (bf16[2,128,1536]{2,1,0:T(8,128)(2,1)}, bf16[2,128,1536]{2,1,0:T(8,128)(2,1)}, f32[96,768]{1,0:T(8,128)}, f32[96,640]{1,0:T(8,128)}, f32[72,128]{1,0:T(8,128)}, /*index=5*/f32[2,96,128]{2,1,0:T(8,128)}) custom-call(f32[8,16,128]{2,1,0:T(8,128)} %get-tuple-element.54.tok_ref, f32[16,128]{1,0:T(8,128)} %get-tuple-element.58.stat_ref, ...), custom_call_target="tpu_custom_call" | custom-call | tf_op jit(solution)/shard_map/mix_backward/pallas_call | solution.py:1190
  197.7 4.6 %finish.1 = (bf16[2,128,1536]{2,1,0:T(8,128)(2,1)}, f32[2,128,1536]{2,1,0:T(8,128)}, f32[1,12]{1,0:T(1,128)}, f32[96,384]{1,0:T(8,128)}, f32[96,384]{1,0:T(8,128...) custom-call(bf16[2,128,1536]{2,1,0:T(8,128)(2,1)} %hid.3, ...), custom_call_target="tpu_custom_call" | custom-call | tf_op jit(solution)/shard_map/finish/pallas_call | solution.py:1326
  202.3 1.7 copy.33

commit v3 on v2

--- a/solution.py
+++ b/solution.py
@@ -37,7 +37,7 @@
 
 
 def sigmoid(v):
-    return 1.0 / (1.0 + jnp.exp(-v))
+    return 0.5 + 0.5 * jnp.tanh(0.5 * v)
 
 
 def softplus(v):
@@ -56,24 +56,24 @@
     return tok[:, lane : lane + 1]
 
 
-def expand(values, width):
-    rows = values.shape[0]
-    first = lax.broadcasted_iota(jnp.int32, (rows, 128), 1) < 64
-    pieces = []
-    for pair in range(width // 128):
-        a = jnp.broadcast_to(values[:, 2 * pair : 2 * pair + 1], (rows, 128))
-        b = jnp.broadcast_to(values[:, 2 * pair + 1 : 2 * pair + 2], (rows, 128))
-        pieces.append(jnp.where(first, a, b))
-    return jnp.concatenate(pieces, 1)
-
-
-def head_sums(values):
-    width = values.shape[1]
+def head_pick(width):
     channel = lax.broadcasted_iota(jnp.int32, (width, 128), 0)
     lane = lax.broadcasted_iota(jnp.int32, (width, 128), 1)
-    pick = jnp.where((channel >= lane * 64) & (channel < lane * 64 + 64), 1.0, 0.0).astype(BF16)
+    return jnp.where((channel >= lane * 64) & (channel < lane * 64 + 64), 1.0, 0.0).astype(BF16)
+
+
+def two_parts(values):
     high = values.astype(BF16)
-    low = (values - high.astype(F32)).astype(BF16)
+    return high, (values - high.astype(F32)).astype(BF16)
+
+
+def expand(values, pick):
+    high, low = two_parts(values)
+    return dot(high, pick, NT) + dot(low, pick, NT)
+
+
+def head_sums(values, pick):
+    high, low = two_parts(values)
     return dot(high, pick) + dot(low, pick)
 
 
@@ -145,6 +145,10 @@
     return [{**at, "y": (at["y"] + d) % 4} for d in range(1, 4)]
 
 
+def y_core_peers(at):
+    return core_peers(at) + [{**p, "c": (at["c"] + flip) % 2} for flip in range(2) for p in y_peers(at)]
+
+
 def core_peers(at):
     return [{**at, "c": 1 - at["c"]}]
 
@@ -220,8 +224,31 @@
     Exchange(total, taken, peers, held, sends).finish()
 
 
+PIECES = 2
+
+
+def pieces():
+    rows = Q // PIECES
+    return [pl.ds(i * rows, rows) for i in range(PIECES)]
+
+
+class YCoreExchange:
+    def __init__(self, at, total, held, sends):
+        self.total, self.held = total, held
+        self.copies = [sends.start(total, held.at[i], peer) for i, peer in enumerate(y_core_peers(at))]
+
+    def finish(self):
+        wait_all(self.copies)
+        shared = self.total[0:SMALL_SHARED]
+        for i in range(len(self.copies)):
+            shared = shared + self.held[i, 0:SMALL_SHARED]
+        rows = slice(SMALL_SHARED, self.total.shape[0])
+        self.total[rows] = self.total[rows] + self.held[0, rows]
+        self.total[0:SMALL_SHARED] = shared
+
+
 class RingGather:
-    SEMS = 7
+    SEMS = 7 * PIECES
 
     def __init__(self, at, source, target, send_sems, recv_sems, local_sem):
         self.at, self.source, self.target = at, source, target
@@ -230,50 +257,71 @@
         self.up, self.down = {**at, "y": (at["y"] + 1) % 4}, {**at, "y": (at["y"] + 3) % 4}
         self.pair = {**at, "xl": 1 - at["xl"]}
 
-    def rows(self, y, xl):
-        return self.target.at[pl.ds(pl.multiple_of((y * 2 + xl) * Q, Q), Q)]
-
-    def copies(self, stage):
+    def rows(self, y, xl, piece):
+        rows = Q // PIECES
+        return self.target.at[pl.ds(pl.multiple_of((y * 2 + xl) * Q + piece * rows, rows), rows)]
+
+    def make(self, kind, piece, source, target, peer):
+        sends = Sends(*self.sems)
+        sends.used = kind * PIECES + piece
+        return sends.make(source, target, peer)
+
+    def pair_copy(self, i):
         at = self.at
-        y, xl, other = at["y"], at["xl"], 1 - at["xl"]
-        sends = Sends(*self.sems)
-        if stage == 0:
-            mine = self.rows(y, xl)
-            own = self.source.at[xl]
-            return [sends.make(self.source.at[other], mine, self.pair)] + [
-                sends.make(own, mine, p) for p in (self.up, self.down)
-            ]
-        if stage == 1:
-            sends.used = 3
-            got = self.rows(y, other)
-            return [sends.make(got, got, p) for p in (self.up, self.down)]
-        sends.used = 5
-        low, high = self.rows((y + 3) % 4, xl), self.rows((y + 1) % 4, other)
-        return [sends.make(low, low, self.up), sends.make(high, high, self.down)]
+        return self.make(0, i, self.source.at[1 - at["xl"], pieces()[i]], self.rows(at["y"], at["xl"], i), self.pair)
+
+    def own_copy(self, i, down):
+        at = self.at
+        source, target = self.source.at[at["xl"], pieces()[i]], self.rows(at["y"], at["xl"], i)
+        return self.make(1 + down, i, source, target, self.down if down else self.up)
+
+    def pair_on(self, i, down):
+        got = self.rows(self.at["y"], 1 - self.at["xl"], i)
+        return self.make(3 + down, i, got, got, self.down if down else self.up)
+
+    def pass_on(self, i, down):
+        at = self.at
+        if down:
+            got = self.rows((at["y"] + 1) % 4, 1 - at["xl"], i)
+        else:
+            got = self.rows((at["y"] + 3) % 4, at["xl"], i)
+        return self.make(5 + down, i, got, got, self.down if down else self.up)
 
     def local(self):
-        return pltpu.make_async_copy(self.source.at[self.at["xl"]], self.rows(self.at["y"], self.at["xl"]), self.local_sem)
-
-    def begin(self):
-        start_all(self.copies(0))
-        self.local().start()
-
-    def second(self):
-        self.copies(0)[0].wait()
-        start_all(self.copies(1))
+        at = self.at
+        target = self.target.at[pl.ds(pl.multiple_of((at["y"] * 2 + at["xl"]) * Q, Q), Q)]
+        return pltpu.make_async_copy(self.source.at[at["xl"]], target, self.local_sem)
+
+    def begin(self, which=range(PIECES)):
+        for i in which:
+            self.pair_copy(i).start()
+            start_all([self.own_copy(i, down) for down in range(2)])
+
+    def second(self, which=range(PIECES)):
+        for i in which:
+            self.pair_copy(i).wait()
+            start_all([self.pair_on(i, down) for down in range(2)])
+
+    def pass_low(self):
+        for i in range(PIECES):
+            self.own_copy(i, 0).wait()
+            self.pass_on(i, 0).start()
 
     def third(self):
-        wait_all(self.copies(0)[1:])
-        wait_all(self.copies(1))
-        start_all(self.copies(2))
+        self.local().wait()
+        for i in range(PIECES):
+            self.pair_on(i, 1).wait()
+            self.pass_on(i, 1).start()
+        for i in range(PIECES):
+            self.own_copy(i, 1).wait()
+            self.pair_on(i, 0).wait()
 
     def finish(self):
-        wait_all(self.copies(2))
-        self.local().wait()
+        wait_all([self.pass_on(i, down) for i in range(PIECES) for down in range(2)])
 
 
 class RingScatter:
-    SEMS = 7
+    SEMS = 7 * PIECES
 
     @staticmethod
     def scratch(width):
@@ -287,42 +335,47 @@
         self.up, self.down = {**at, "y": self.up_y}, {**at, "y": self.down_y}
         self.pair = {**at, "xl": 1 - at["xl"]}
 
-    def copy(self, number):
+    def copy(self, number, i):
         sends = Sends(self.ss, self.rs)
-        sends.used = number
+        sends.used = number * PIECES + i
+        piece = pieces()[i]
         if number == 6:
-            return sends.make(self.held.at[6], self.held.at[7], self.pair)
+            return sends.make(self.held.at[6, piece], self.held.at[7, piece], self.pair)
         y, x = [(self.far_y, 0), (self.far_y, 1), (self.up_y, 1), (self.down_y, 0), (self.up_y, 0), (self.down_y, 1)][number]
         peer = self.down if number % 2 else self.up
-        return sends.make(self.part.at[y * 2 + x], self.held.at[number], peer)
+        return sends.make(self.part.at[y * 2 + x, piece], self.held.at[number, piece], peer)
 
     def send_far(self):
-        start_all([self.copy(0), self.copy(1)])
+        start_all([self.copy(n, i) for i in range(PIECES) for n in range(2)])
 
     def send_up(self):
-        self.copy(2).start()
+        start_all([self.copy(2, i) for i in range(PIECES)])
 
     def send_down(self):
-        self.copy(3).start()
+        start_all([self.copy(3, i) for i in range(PIECES)])
 
     def second(self):
-        wait_all([self.copy(0), self.copy(1)])
-        for slot, number in ((self.up_y * 2, 0), (self.down_y * 2 + 1, 1)):
-            self.part[slot] = (self.part[slot].astype(F32) + self.held[number].astype(F32)).astype(BF16)
-        start_all([self.copy(4), self.copy(5)])
+        for i, piece in enumerate(pieces()):
+            for slot, number in ((self.up_y * 2, 0), (self.down_y * 2 + 1, 1)):
+                self.copy(number, i).wait()
+                total = self.part[slot, piece].astype(F32) + self.held[number, piece].astype(F32)
+                self.part[slot, piece] = total.astype(BF16)
+                self.copy(4 + number, i).start()
 
     def third(self, out):
-        wait_all([self.copy(n) for n in range(2, 6)])
         held, xl, y = self.held, self.at["xl"], self.at["y"]
-        totals = []
-        for x in range(2):
-            totals.append(self.part[y * 2 + x].astype(F32) + held[3 - x].astype(F32) + held[4 + x].astype(F32))
-        out[xl] = jnp.where(xl == 0, totals[0], totals[1]).astype(BF16)
-        held[6] = jnp.where(xl == 0, totals[1], totals[0]).astype(BF16)
-        self.copy(6).start()
+        for i, piece in enumerate(pieces()):
+            wait_all([self.copy(n, i) for n in range(2, 6)])
+            totals = []
+            for x in range(2):
+                total = self.part[y * 2 + x, piece].astype(F32) + held[3 - x, piece].astype(F32)
+                totals.append(total + held[4 + x, piece].astype(F32))
+            out[xl, piece] = jnp.where(xl == 0, totals[0], totals[1]).astype(BF16)
+            held[6, piece] = jnp.where(xl == 0, totals[1], totals[0]).astype(BF16)
+            self.copy(6, i).start()
 
     def finish(self, out):
-        self.copy(6).wait()
+        wait_all([self.copy(6, i) for i in range(PIECES)])
         out[1 - self.at["xl"]] = self.held[7]
 
 
@@ -437,67 +490,142 @@
 
 
 def forward_kernel(
-    tok_ref, small_ref, hid_ref, wxe_ref, cot_ref, w2_ref,
+    hid, cot_ref, w2_ref,
+    ids_ref, wx_ref, wdt_ref, wbc_ref, gain_ref, kx_ref, kxb_ref, kbc_ref, kbcb_ref, og_ref, al_ref, ds_ref, db_ref,
     zx_ref, xin_ref, bcin_ref, dt_ref, bcc_ref, y_ref, start_ref, gon_ref,
-    normed_ref, cot_all_ref, w2_all_ref, stat_ref,
-    state, xh, bch, xes, cots, weights, normeds, ys, stats, held,
-    cot_send, cot_recv, w_send, w_recv, stat_send, stat_recv, sems,
+    normed_ref, cot_all_ref, w2_all_ref, wxe_all_ref, stat_ref, small_all, tok_all,
+    wxe, bc_got, bc_rows, held, lanes,
+    pick_ref, state, xh, bch, hids, wxes, xes, cots, weights, normeds, ys, stats, stat_held,
+    hid_send, hid_recv, bc_send, bc_recv, w_send, w_recv, wbc_send, wbc_recv, small_send, small_recv,
+    cot_send, cot_recv, w2_send, w2_recv, stat_send, stat_recv, sems,
 ):
     step = pl.program_id(0)
-    steps = pl.num_programs(0) // 2
+    steps = (pl.num_programs(0) - 1) // 2
     per_step = STEP_ROWS // Q
     width = zx_ref.shape[2]
     lay = Layout(width)
     pairs = width // 128
     chunks = stats.shape[0] // 2
-    own_heads = own_heads_of(width)
+    own_heads = wdt_ref.shape[0]
+    depth, half = wx_ref.shape
     at = place()
-    ring = RingGather(at, cot_ref, cots, cot_send, cot_recv, sems.at[0])
-    plane = PlaneGather(at, w2_ref, weights, w_send, w_recv, sems.at[1])
+    y, xl = at["y"], at["xl"]
+    peers = group_peers(at)
+    ring = RingGather(at, hid, hids, hid_send, hid_recv, sems.at[0])
+    ring_cot = RingGather(at, cot_ref, cots, cot_send, cot_recv, sems.at[1])
+    plane = PlaneGather(at, wxe, wxes, w_send, w_recv, sems.at[2], 0, half + 128)
+    plane_bc = PlaneGather(at, wxe, wxes, wbc_send, wbc_recv, sems.at[3], half + 128, 128)
+    plane_w2 = PlaneGather(at, w2_ref, weights, w2_send, w2_recv, sems.at[4])
+    small_ref, tok_ref = small_all, tok_all
 
     def results():
-        pairs_of = [(cots, cot_all_ref), (weights, w2_all_ref), (normeds, normed_ref)]
-        return [pltpu.make_async_copy(a, b, sems.at[2 + i]) for i, (a, b) in enumerate(pairs_of)]
+        pairs_of = [(wxes, wxe_all_ref), (normeds, normed_ref), (cots, cot_all_ref), (weights, w2_all_ref)]
+        return [pltpu.make_async_copy(a, b, sems.at[5 + i]) for i, (a, b) in enumerate(pairs_of)]
 
     @pl.when(step == 0)
     def _():
-        greet(ring_greets(at) + y_peers(at)[1:2] + plane_greets(at))
-        ring.begin()
+        greets = peers + plane_greets(at) + y_core_peers(at)[4:]
+        greet_begin(greets)
+        bc_slot = bc_got.at[y * 2 + xl]
+        wxe[0, :, 0:half] = wx_ref[...]
+        lanes[...] = jnp.zeros_like(lanes)
+        lanes[0:own_heads, 0:depth] = wdt_ref[...].astype(F32)
+        wxe[0, :, half : half + 128] = columns_of(lanes[:, 0:128])[0:depth].astype(BF16)
+        lanes[...] = jnp.zeros_like(lanes)
+        lanes[0:2, 0:4] = kbc_ref[...].astype(F32)
+        taps_bc = columns_of(lanes[:, 0:128])[0:4, 0:2]
+        bc_got[y * 2 + xl, 0:12] = wbc_ref[...].astype(F32)
+
+        def placed(pieces, width, start):
+            lanes[...] = jnp.zeros_like(lanes)
+            row = 0
+            for piece in pieces:
+                count, size = piece.shape
+                lanes[row : row + count, 0:size] = piece[...].astype(F32)
+                row += count
+            return pltpu.roll(lanes[:, 0:width], start, 1)
+
+        dp = at["xh"] * 8 + at["z"] * 2 + at["c"]
+        everyone = dp * 8 + y * 2 + xl
+        small_all[...] = jnp.zeros_like(small_all)
+        value = placed([taps_bc, kbcb_ref], 256, everyone * kbc_ref.shape[0])
+        for t in range(5):
+            put_wide(small_all, BC_TAPS + 2 * t, value[t : t + 1])
+        value = placed([gain_ref], lanes.shape[1], everyone * gain_ref.shape[1])
+        put_wide(small_all, IN_GAIN, value[0:1])
+        value = placed([kx_ref, kxb_ref, og_ref], 2 * half, xl * half + dp * kx_ref.shape[1])
+        for t in range(6):
+            put_wide(small_all, X_TAPS + t * (half // 64), value[t : t + 1])
+        value = placed([al_ref, ds_ref, db_ref], 128, xl * own_heads)
+        small_all[HEAD_ROWS : HEAD_ROWS + 3] = jnp.where(dp == 0, value[0:3], 0.0)
+        greet_end(greets)
+        sends = Sends(bc_send, bc_recv)
+        bc_copies = [sends.start(bc_slot, bc_slot, p) for p in peers]
+        small_sends = Sends(small_send, small_recv)
+        small = YCoreExchange(at, small_all, held, small_sends)
+        ring.local().start()
+        ring_cot.local().start()
+        ring.begin(range(0, 1))
         plane.begin()
+        ids = ids_ref[pl.ds(xl, 1), :]
+        token_info(jnp.concatenate([ids[:, n * Q : n * Q + Q] for n in range(chunks)], 0), tok_all)
+        pick_ref[...] = head_pick(width)
         state[...] = jnp.zeros_like(state)
         xh[0:HALO] = jnp.zeros((HALO, width), F32)
         bch[0:HALO] = jnp.zeros((HALO, bch.shape[1]), F32)
 
-    @pl.when(step == 1)
-    def _():
-        ring.second()
+        wait_all(bc_copies)
+        for m in range(8):
+            bc_rows[12 * m : 12 * m + 12] = bc_got[m, 0:12]
+        wxe[0, :, half + 128 : half + 256] = half_of(bc_rows[...], xl).astype(BF16)
+        small.finish()
+        small = Exchange(small_all, SMALL_ROWS, x_peers(at), held.at[7:10], small_sends)
+        plane_bc.begin()
+        ring.begin(range(1, 2))
+        ring.second(range(0, 1))
+        small.finish()
+        small = Exchange(small_all, SMALL_ROWS, z_peers(at), held.at[10:13], small_sends)
         plane.second()
-
-    @pl.when(step == 2)
-    def _():
+        plane_bc.second()
+        ring.second(range(1, 2))
+        ring.pass_low()
+        small.finish()
         ring.third()
+        ring_cot.begin()
+        plane.third()
+        plane_bc.third()
+        plane_w2.begin()
+        plane.finish()
+        plane_bc.finish()
+
+        def project(number):
+            rows = block_rows((y + number) % 4)
+            value = hids[rows].astype(F32)
+            inv_rms = lax.rsqrt(jnp.mean(value * value, -1, keepdims=True) + EPS)
+            normed = (value * inv_rms * wide(small_ref, IN_GAIN, 12)).astype(BF16)
+            normeds[rows] = normed
+            xes[rows] = dot(normed, wxes[0].reshape(hids.shape[1], lay.total))
+
+        @pl.loop(0, 3)
+        def _(n):
+            project(n + n // 2)
+
+        ring_cot.second()
+        plane_w2.second()
+        ring.finish()
+        project(2)
+        ring_cot.pass_low()
+        start_all(results()[:2])
 
     @pl.when(step == 3)
     def _():
-        plane.third()
-
-    @pl.when(step == steps)
-    def _():
-        ring.finish()
-        plane.finish()
-        start_all(results())
-
-    @pl.when(step < steps)
-    def _():
-        rows = hid_ref[...].astype(F32)
-        inv_rms = lax.rsqrt(jnp.mean(rows * rows, -1, keepdims=True) + EPS)
-        normed = (rows * inv_rms * wide(small_ref, IN_GAIN, 12)).astype(BF16)
-        normeds[pl.ds(pl.multiple_of(step * STEP_ROWS, STEP_ROWS), STEP_ROWS)] = normed
-        xes[...] = dot(normed, wxe_ref[...])
-
+        ring_cot.third()
+
+    @pl.when((step >= 1) & (step <= steps))
+    def _():
         @pl.loop(0, per_step)
         def _(j):
-            chunk = step * per_step + j
+            chunk = (step - 1) * per_step + j
             here = chunk_rows(j)
 
             @pl.when(chunk > 0)
@@ -505,10 +633,15 @@
                 xh[0:HALO] = xh[Q : Q + HALO]
                 bch[0:HALO] = bch[Q : Q + HALO]
 
+            @pl.when(chunk == 5)
+            def _():
+                plane_w2.third()
+
             rows16 = tok_ref[chunk]
             tok = columns_of(rows16)
             hp = small_ref[HEAD_ROWS : HEAD_ROWS + 3]
-            xe = xes[here]
+            pick = pick_ref[...]
+            xe = xes[chunk_rows(chunk)]
             x_in, bc_in, dt_in = lay.x(xe), lay.bc(xe), lay.dt(xe, own_heads)
             xin_ref[here] = x_in.astype(BF16)
             bcin_ref[here] = bc_in.astype(BF16)
@@ -534,46 +667,66 @@
             size, rate, cum2, cum2_t, enter, leave, keep = decays(dt_in, hp, tok)
             same = causal() & (lanes_of(tok, SEG) == rows16[SEG : SEG + 1])
             scores = jnp.where(same, dot(c_low, b_low, NT), 0.0)
-            xs = x_act * expand(size, width)
+            xs = x_act * expand(size, pick)
             xs_low = xs.astype(BF16)
             before = state[...]
             before_low = before.astype(BF16)
             start_ref[j] = before_low
-            inter = dot(c_low, before_low) * expand(enter, width)
+            inter = dot(c_low, before_low) * expand(enter, pick)
             outs = []
             for pair in range(pairs):
                 mixes = [(scores * gaps(cum2, cum2_t, 2 * pair + i)).astype(BF16) for i in range(2)]
                 outs.append(
                     dot(jnp.concatenate(mixes, 1), pair_blocks(xs_low[:, pair * 128 : pair * 128 + 128]))
                 )
-            skip = expand(jnp.broadcast_to(hp[1:2], (8, 128)), width)[0:1]
+            skip = expand(jnp.broadcast_to(hp[1:2], (8, 128)), pick)[0:1]
             y = jnp.concatenate(outs, 1) + inter + skip * x_act
             y_ref[here] = y
             ys[chunk_rows(chunk)] = y
-            moved = (xs * expand(leave, width)).astype(BF16)
-            keep_all = expand(jnp.broadcast_to(keep, (8, 128)), width)[0:1]
+            moved = (xs * expand(leave, pick)).astype(BF16)
+            keep_all = expand(jnp.broadcast_to(keep, (8, 128)), pick)[0:1]
             state[...] = before * keep_all + dot(b_low, moved, TN)
 
-    @pl.when(step >= steps)
-    def _():
-        rows = pl.ds(pl.multiple_of((step - steps) * STEP_ROWS, STEP_ROWS), STEP_ROWS)
-        full = weights.shape[1] * weights.shape[2] * weights.shape[3] * weights.shape[4]
-        z = dot(normeds[rows], weights[0].reshape(full, width))
+    full = hids.shape[1]
+
+    @pl.when(step == steps + 1)
+    def _():
+        plane_w2.finish()
+
+        @pl.loop(0, steps)
+        def _(number):
+            rows = block_rows(number)
+            z = dot(normeds[rows], weights[0].reshape(full, width))
+            xes[rows, 0:width] = z
+            gated = ys[rows] * (z * sigmoid(z))
+            ys[rows] = gated
+            for j in range(per_step):
+                value = gated[j * Q : j * Q + Q]
+                stats[pl.ds(number * per_step + j, 1), :] = row_sums(value * value)
+
+        results()[3].start()
+
+    @pl.when(step == 2 * steps)
+    def _():
+        ring_cot.finish()
+        results()[2].start()
+
+    @pl.when(step > steps)
+    def _():
+        number = arrival_block(step - steps - 1, y)
+        rows = block_rows(number)
+        zx_ref[0] = xes[rows, 0:width]
         gon = dot(cots[rows], weights[1].reshape(full, width))
-        zx_ref[0] = z
         gon_ref[...] = gon.astype(BF16)
-        gated = ys[rows] * (z * sigmoid(z))
-        inner = gated * (gon * wide(small_ref, X_TAPS + 5 * pairs, pairs))
+        inner = ys[rows] * (gon * wide(small_ref, X_TAPS + 5 * pairs, pairs))
         for j in range(per_step):
-            chunk = (step - steps) * per_step + j
-            cut = slice(j * Q, j * Q + Q)
-            stats[pl.ds(chunk, 1), :] = row_sums(gated[cut] * gated[cut])
-            stats[pl.ds(chunks + chunk, 1), :] = row_sums(inner[cut])
-
-    @pl.when(step == 2 * steps - 1)
-    def _():
+            stats[pl.ds(chunks + number * per_step + j, 1), :] = row_sums(inner[j * Q : j * Q + Q])
+
+    @pl.when(step == 2 * steps)
+    def _():
+        sums = Exchange(stats, stats.shape[0], y_peers(at), stat_held, Sends(stat_send, stat_recv))
         wait_all(results())
-        exchange(stats, stats.shape[0], y_peers(at), held, Sends(stat_send, stat_recv))
+        sums.finish()
         inner = width * 4
         scale = lax.rsqrt(stats[0:chunks] / inner + EPS)
         stat_ref[0:chunks] = scale
@@ -624,10 +777,10 @@
         sends.used = used
         return sends
 
-    def first(self, far, z):
-        peer, xh = core_peers(self.at)[0], (self.at["xh"] + far) % 2
+    def first(self, xh, z):
+        peer = core_peers(self.at)[0]
         source = self.source.at[xh, z, peer["c"], :, pl.ds(0, self.width)]
-        return self.sends((1 - far) * 4 + z).make(source, self.got.at[xh, z], peer)
+        return self.sends(xh * 4 + z).make(source, self.got.at[xh, z], peer)
 
     def second_x(self, number):
         p, c = x_peers(self.at)[number], self.at["c"]
@@ -648,15 +801,12 @@
             copies.append(sends.make(self.sb.at[p["xh"], :, self.columns(p["xl"])], self.b3.at[i], p))
         return copies
 
-    def begin(self):
-        start_all([self.first(far, z) for far in (1, 0) for z in range(4)])
-
     def after_cores(self):
         c = self.at["c"]
         for far in (1, 0):
             xh = (self.at["xh"] + far) % 2
             for z in range(4):
-                self.first(far, z).wait()
+                self.first(xh, z).wait()
                 total = self.source[xh, z, c, :, 0 : self.width].astype(F32) + self.got[xh, z].astype(F32)
                 self.source[xh, z, c, :, 0 : self.width] = total.astype(BF16)
             start_all([self.second_x(n) for n in ((1, 2) if far else (0,))])
@@ -701,6 +851,10 @@
 PRE, MIX = 4, 4
 
 
+def arrival_block(step, y):
+    return (y + step + jnp.where(step == 2, 1, jnp.where(step == 3, 3, 0))) % 4
+
+
 def owner_block(step, y):
     return (y + jnp.where(step == 0, 2, jnp.where(step == 1, 1, jnp.where(step == 2, 3, 0)))) % 4
 
@@ -713,7 +867,7 @@
     tok_ref, stat_ref, small_ref, zx_ref, gon_ref, y_ref, xin_ref, bcin_ref, dt_ref, bcc_ref, start_ref,
     cot_ref, normed_ref, w2_ref, wxe_ref,
     out_ref, back_ref, gzo_ref, gxe_ref, sums_ref, bcs_ref,
-    adjoint, dh, dbh, gkx, gkbc, ghead, ggain, cots, normeds, weight, wxe, outs_low, z_low, dy_all, part, source,
+    pick_ref, adjoint, dh, dbh, gkx, gkbc, ghead, cots, normeds, weight, wxe, outs_low, z_low, dy_all, part, source,
     held, bc_got, small_send, small_recv, bc_send, bc_recv, sems, *refs,
 ):
     step = pl.program_id(0)
@@ -724,6 +878,7 @@
     lay = Layout(width)
     chunks = tok_ref.shape[0]
     model = cots.shape[1]
+    depth = model // 16
     at = place()
     ring_out = RingScatter(at, part, refs[0:3])
     ring_in = RingScatter(at, part, refs[3:6])
@@ -742,27 +897,30 @@
         for x in range(2):
             part[owner * 2 + x] = low[x * Q : x * Q + Q]
 
-    def put_grad(values, start, half):
+    def put_grads(plane, terms):
         for quarter in range(4):
             cut = slice(quarter * (model // 4), (quarter + 1) * (model // 4))
-            value = dot(values[0][:, cut], values[1], TN).astype(BF16)
-            value = value.reshape(2, 2, model // 16, value.shape[1])
             xh, z = quarter // 2, (quarter % 2) * 2
-            for n in range(2):
-                first = n * start[1] + start[0]
-                source[xh, z : z + 2, :, :, first : first + half] = value[..., n * half : n * half + half]
+            for left, right, start, part in terms:
+                value = dot(left[:, cut], right, TN).astype(BF16)
+                half = value.shape[1] // 2
+                value = value.reshape(2, 2, model // 16, 2 * half)
+                for n in range(2):
+                    first = n * part + start
+                    source[xh, z : z + 2, :, :, first : first + half] = value[..., n * half : n * half + half]
+            start_all([plane.first(xh, z), plane.first(xh, z + 1)])
 
     @pl.when(step == 0)
     def _():
         start_all(loads[:4])
-        greet_begin(peers + plane_greets(at))
+        greet_begin(peers + plane_greets(at) + y_core_peers(at)[4:])
+        pick_ref[...] = head_pick(width)
         adjoint[...] = jnp.zeros_like(adjoint)
         dh[...] = jnp.zeros_like(dh)
         dbh[...] = jnp.zeros_like(dbh)
         gkx[...] = jnp.zeros_like(gkx)
         gkbc[...] = jnp.zeros_like(gkbc)
         ghead[...] = jnp.zeros_like(ghead)
-        ggain[...] = jnp.zeros_like(ggain)
         loads[0].wait()
 
     @pl.when(step < PRE)
@@ -793,7 +951,7 @@
 
     @pl.when(step == 0)
     def _():
-        greet_end(peers + plane_greets(at))
+        greet_end(peers + plane_greets(at) + y_core_peers(at)[4:])
         ring_out.send_far()
 
     @pl.when(step == 1)
@@ -809,24 +967,18 @@
         loads[4].start()
         loads[1].wait()
         loads[2].wait()
-        half = width // 2
-        put_grad((cots, outs_low[...]), (half, width), half)
-        put_grad((normeds, z_low[...]), (0, width), half)
-        plane_zo.begin()
+        put_grads(
+            plane_zo, [(cots, outs_low[...], width // 2, width), (normeds, z_low[...], 0, width)]
+        )
         ring_out.second()
 
     @pl.when(step == PRE + 1)
     def _():
         plane_zo.after_cores()
 
-    @pl.when(step == PRE + 2)
+    @pl.when(step == PRE + 3)
     def _():
         ring_out.third(out_ref)
-
-    @pl.when(step == PRE + MIX - 1)
-    def _():
-        plane_zo.after_first_axis()
-        ring_out.finish(out_ref)
 
     @pl.when((step >= PRE) & (step < PRE + MIX))
     def _():
@@ -842,9 +994,14 @@
                 dh[Q : Q + HALO] = dh[0:HALO]
                 dbh[Q : Q + HALO] = dbh[0:HALO]
 
+            @pl.when(chunk == 0)
+            def _():
+                plane_zo.after_first_axis()
+
             rows16 = tok_ref[chunk]
             tok = columns_of(rows16)
             hp = small_ref[HEAD_ROWS : HEAD_ROWS + 3]
+            pick = pick_ref[...]
             dt_in = dt_ref[here]
             xc = zx_ref[0, here]
             bcc = bcc_ref[here]
@@ -858,16 +1015,16 @@
             size, rate, cum2, cum2_t, enter, leave, keep = decays(dt_in, hp, tok)
             same = causal() & (lanes_of(tok, SEG) == rows16[SEG : SEG + 1])
             scores = jnp.where(same, dot(c_low, b_low, NT), 0.0)
-            step_all = expand(size, width)
-            leave_all = expand(leave, width)
+            step_all = expand(size, pick)
+            leave_all = expand(leave, pick)
             xs = x_act * step_all
             xs_low = xs.astype(BF16)
             moved = (xs * leave_all).astype(BF16)
             dy_low = dy_all[there]
             dy = dy_low.astype(F32)
-            dy_in = (dy * expand(enter, width)).astype(BF16)
-
-            skip = expand(jnp.broadcast_to(hp[1:2], (8, 128)), width)[0:1]
+            dy_in = (dy * expand(enter, pick)).astype(BF16)
+
+            skip = expand(jnp.broadcast_to(hp[1:2], (8, 128)), pick)[0:1]
             before_low = start_ref[j]
             after = adjoint[...]
             after_low = after.astype(BF16)
@@ -891,13 +1048,13 @@
             dxs = intra + leave_all * from_state
             dx_act = dxs * step_all + skip * dy
             gkx[6] += rows8(dy * x_act)
-            plus = head_sums(dy * (y_ref[here] - skip * x_act))
+            plus = head_sums(dy * (y_ref[here] - skip * x_act), pick)
             through = moved.astype(F32) * from_state
-            minus = head_sums(xs_low.astype(F32) * intra + through)
-            direct = head_sums(dxs * x_act)
-            keep_all = expand(jnp.broadcast_to(keep, (8, 128)), width)[0:1]
+            minus = head_sums(xs_low.astype(F32) * intra + through, pick)
+            direct = head_sums(dxs * x_act, pick)
+            keep_all = expand(jnp.broadcast_to(keep, (8, 128)), pick)[0:1]
             at_end = rows8(through) + keep_all * rows8(after * before_low.astype(F32))
-            at_end = jnp.sum(head_sums(at_end), axis=0, keepdims=True)
+            at_end = jnp.sum(head_sums(at_end, pick), axis=0, keepdims=True)
             last_row = lax.broadcasted_iota(jnp.int32, (Q, 128), 0) == Q - 1
             dcum = plus - minus + jnp.where(last_row, at_end, 0.0)
             tri = jnp.where(causal(), 1.0, 0.0)
@@ -931,54 +1088,61 @@
 
     @pl.when(step == PRE + MIX)
     def _():
-        plane_zo.finish(gzo_ref)
+        sums_ref[...] = jnp.zeros_like(sums_ref)
+        for t in range(5):
+            put_wide(sums_ref, 2 * t, jnp.sum(gkbc[t], axis=0, keepdims=True))
+        for t in range(7):
+            put_wide(sums_ref, X_TAPS + t * pairs, jnp.sum(gkx[t], axis=0, keepdims=True))
+        for t in range(2):
+            put_wide(sums_ref, X_TAPS + 7 * pairs + t, jnp.sum(ghead[t], axis=0, keepdims=True))
+        small_sends = Sends(small_send, small_recv)
+        small = YCoreExchange(at, sums_ref, held, small_sends)
         loads[3].wait()
         loads[4].wait()
 
         def part_in(number):
             owner = (at["y"] + number) % 4
             rows = block_rows(owner)
-            value = dot(z_low[rows], weight[...], NT) + dot(cots[rows, 0 : lay.total], wxe[...], NT)
-            ggain[...] += rows8(value * normeds[rows].astype(F32))
-            put_part(owner, value)
-
+            put_part(owner, dot(z_low[rows], weight[...], NT) + dot(cots[rows, 0 : lay.total], wxe[...], NT))
+
+        put_grads(plane_xe, [(normeds, cots[:, 0 : lay.total], 0, lay.part)])
+        small.finish()
+        small = Exchange(sums_ref, sums_ref.shape[0], x_peers(at), held.at[7:10], small_sends)
         part_in(2)
         ring_in.send_far()
-        put_grad((normeds, cots[:, 0 : lay.total]), (0, lay.part), lay.part)
-        plane_xe.begin()
+        small.finish()
+        small = Exchange(sums_ref, sums_ref.shape[0], z_peers(at), held.at[10:13], small_sends)
+        plane_xe.after_cores()
         part_in(1)
         ring_in.send_up()
         part_in(3)
         ring_in.send_down()
+        part_in(0)
         ring_in.second()
-        plane_xe.after_cores()
-        part_in(0)
-
-        sums_ref[...] = jnp.zeros_like(sums_ref)
-        for t in range(5):
-            put_wide(sums_ref, 2 * t, jnp.sum(gkbc[t], axis=0, keepdims=True))
-        put_wide(sums_ref, IN_GAIN, jnp.sum(ggain[...], axis=0, keepdims=True) / wide(small_ref, IN_GAIN, model // 128))
-        for t in range(7):
-            put_wide(sums_ref, X_TAPS + t * pairs, jnp.sum(gkx[t], axis=0, keepdims=True))
-        for t in range(2):
-            put_wide(sums_ref, X_TAPS + 7 * pairs + t, jnp.sum(ghead[t], axis=0, keepdims=True))
-        steps = [core_peers(at), x_peers(at), z_peers(at), y_peers(at)]
-        sends = Sends(small_send, small_recv)
-        rows = sums_ref.shape[0]
-        exchange(sums_ref, rows, steps[0], held.at[0], sends)
-        exchange(sums_ref, rows, steps[1], held.at[1], sends)
+        small.finish()
+        ring_out.finish(out_ref)
+        plane_zo.finish(gzo_ref)
         plane_xe.after_first_axis()
-        exchange(sums_ref, rows, steps[2], held.at[2], sends)
         ring_in.third(back_ref)
-        exchange(sums_ref, SMALL_SHARED, steps[3], held.at[3], sends)
         plane_xe.finish(gxe_ref)
-        bc_got[at["xl"], at["y"]] = gxe_ref[:, lay.bc_at : lay.bc_at + 128]
+
+        dp = at["xh"] * 8 + at["z"] * 2 + at["c"]
+        own = pl.ds(pl.multiple_of(dp * depth, 16), depth)
+        terms = half_of(weight[own], at["xl"]).astype(F32) * gzo_ref[:, 0 : lay.half]
+        total = terms[:, 0:128] + terms[:, 128:256] + terms[:, 256:384]
+        terms = half_of(wxe[own], at["xl"]).astype(F32) * gxe_ref[...]
+        for n in range(lay.part // 128):
+            total = total + terms[:, n * 128 : n * 128 + 128]
+        total = jnp.concatenate([total, jnp.zeros((128 - depth, 128), F32)], 0)
+        bc_got[at["xl"], at["y"], 0:depth] = gxe_ref[:, lay.bc_at : lay.bc_at + 128]
+        bc_got[at["xl"], at["y"], depth : depth + 8] = jnp.broadcast_to(jnp.sum(total.T, axis=0, keepdims=True), (8, 128))
         slot = bc_got.at[at["xl"], at["y"]]
         sends = Sends(bc_send, bc_recv)
-        wait_all([sends.start(slot, slot, p) for p in peers])
+        bc_copies = [sends.start(slot, slot, p) for p in peers]
+        ring_in.finish(back_ref)
+        wait_all(bc_copies)
         for n in range(2):
             bcs_ref[n] = jnp.sum(bc_got[n], axis=0)
-        ring_in.finish(back_ref)
 
 
 def put_wide(ref, row, value):
@@ -986,87 +1150,6 @@
         ref[row + i : row + i + 1] = value[:, i * 128 : i * 128 + 128]
 
 
-def gather_kernel(
-    hid, ids_ref, wx_ref, wdt_ref, wbc_ref, gain_ref, kx_ref, kxb_ref, kbc_ref, kbcb_ref, og_ref, al_ref, ds_ref, db_ref,
-    hid_all, wxe_all, small_all, tok_all,
-    wxe, bc_got, bc_rows, held, lanes,
-    hid_send, hid_recv, bc_send, bc_recv, w_send, w_recv, wbc_send, wbc_recv, small_send, small_recv, sems,
-):
-    at = place()
-    peers = group_peers(at)
-    y, xl = at["y"], at["xl"]
-    depth, half = wx_ref.shape
-    own_heads = wdt_ref.shape[0]
-    ring = RingGather(at, hid, hid_all, hid_send, hid_recv, sems.at[0])
-    plane = PlaneGather(at, wxe, wxe_all, w_send, w_recv, sems.at[1], 0, half + 128)
-    plane_bc = PlaneGather(at, wxe, wxe_all, wbc_send, wbc_recv, sems.at[2], half + 128, 128)
-
-    wxe[0, :, 0:half] = wx_ref[...]
-    lanes[...] = jnp.zeros_like(lanes)
-    lanes[0:own_heads, 0:depth] = wdt_ref[...].astype(F32)
-    wxe[0, :, half : half + 128] = columns_of(lanes[:, 0:128])[0:depth].astype(BF16)
-    lanes[...] = jnp.zeros_like(lanes)
-    lanes[0:2, 0:4] = kbc_ref[...].astype(F32)
-    taps_bc = columns_of(lanes[:, 0:128])[0:4, 0:2]
-    bc_slot = bc_got.at[y * 2 + xl]
-    bc_got[y * 2 + xl, 0:12] = wbc_ref[...].astype(F32)
-
-    def placed(pieces, width, start):
-        lanes[...] = jnp.zeros_like(lanes)
-        row = 0
-        for piece in pieces:
-            count, size = piece.shape
-            lanes[row : row + count, 0:size] = piece[...].astype(F32)
-            row += count
-        return pltpu.roll(lanes[:, 0:width], start, 1)
-
-    dp = at["xh"] * 8 + at["z"] * 2 + at["c"]
-    everyone = dp * 8 + y * 2 + xl
-    small_all[...] = jnp.zeros_like(small_all)
-    value = placed([taps_bc, kbcb_ref], 256, everyone * kbc_ref.shape[0])
-    for t in range(5):
-        put_wide(small_all, BC_TAPS + 2 * t, value[t : t + 1])
-    value = placed([gain_ref], lanes.shape[1], everyone * gain_ref.shape[1])
-    put_wide(small_all, IN_GAIN, value[0:1])
-    value = placed([kx_ref, kxb_ref, og_ref], 2 * half, xl * half + dp * kx_ref.shape[1])
-    for t in range(6):
-        put_wide(small_all, X_TAPS + t * (half // 64), value[t : t + 1])
-    value = placed([al_ref, ds_ref, db_ref], 128, xl * own_heads)
-    small_all[HEAD_ROWS : HEAD_ROWS + 3] = jnp.where(dp == 0, value[0:3], 0.0)
-
-    greet_begin(peers + plane_greets(at))
-    token_info(ids_ref[xl], tok_all)
-    greet_end(peers + plane_greets(at))
-    sends = Sends(bc_send, bc_recv)
-    bc_copies = [sends.start(bc_slot, bc_slot, p) for p in peers]
-    small_sends = Sends(small_send, small_recv)
-    small = Exchange(small_all, SMALL_SHARED, y_peers(at), held.at[0], small_sends)
-    plane.begin()
-    ring.begin()
-
-    wait_all(bc_copies)
-    for m in range(8):
-        bc_rows[12 * m : 12 * m + 12] = bc_got[m, 0:12]
-    wxe[0, :, half + 128 : half + 256] = half_of(bc_rows[...], xl).astype(BF16)
-    plane_bc.begin()
-    small.finish()
-    small = Exchange(small_all, SMALL_ROWS, core_peers(at), held.at[1], small_sends)
-    plane.second()
-    small.finish()
-    small = Exchange(small_all, SMALL_ROWS, x_peers(at), held.at[2], small_sends)
-    plane_bc.second()
-    ring.second()
-    small.finish()
-    small = Exchange(small_all, SMALL_ROWS, z_peers(at), held.at[3], small_sends)
-    plane.third()
-    plane_bc.third()
-    ring.third()
-    small.finish()
-    plane.finish()
-    plane_bc.finish()
-    ring.finish()
-
-
 def block(rows, w, index):
     return pl.BlockSpec((rows, w), lambda i: (index(i), 0))
 
@@ -1095,80 +1178,64 @@
     return pltpu.CompilerParams(collective_id=cid, has_side_effects=True, vmem_limit_bytes=VMEM_LIMIT)
 
 
-def gather_call(hidden, ids, w_x, w_dt, w_bc, small_args):
+def forward_call(hidden, cotangent, w2, ids, w_x, w_dt, w_bc, small_args):
     _, rows, model = hidden.shape
-    depth, half = w_x.shape
-    part = half + 256
+    _, depth, half = w2.shape
+    width, part = 2 * half, half + 256
+    length = 8 * rows
+    steps = length // STEP_ROWS
+    chunks = length // Q
     args = [ids, w_x, w_dt, w_bc, *small_args]
+
+    def early(i):
+        return jnp.clip(i - 1, 0, steps - 1)
+
+    def late(i):
+        return arrival_block(jnp.maximum(i - steps - 1, 0), lax.axis_index("mp") // 2)
+
     return pl.pallas_call(
-        gather_kernel,
-        in_specs=[ANY] + [IN_VMEM] * len(args),
-        out_specs=[ANY, ANY, IN_VMEM, IN_VMEM],
+        forward_kernel,
+        grid=(2 * steps + 1,),
+        in_specs=[ANY, ANY, ANY] + [whole(arg.shape) for arg in args],
+        out_specs=[pl.BlockSpec((1, STEP_ROWS, width), lambda i: (jnp.where(i > steps, 1, 0), jnp.where(i > steps, late(i), early(i)), 0)),
+                   block(STEP_ROWS, width, early), block(STEP_ROWS, 256, early),
+                   block(STEP_ROWS, 128, early), block(STEP_ROWS, 256, early), block(STEP_ROWS, width, early),
+                   pl.BlockSpec((STEP_ROWS // Q, 128, width), lambda i: (early(i), 0, 0)),
+                   block(STEP_ROWS, width, late), ANY, ANY, ANY, ANY,
+                   whole_out((2 * chunks, Q)), whole_out((SMALL_ROWS, 128)), whole_out((chunks, 16, Q))],
         out_shape=[
-            like((8 * rows, model), BF16),
-            like((1, 2, 4, 2, depth, 2 * part), BF16),
-            like((SMALL_ROWS, 128), F32),
-            like((ids.shape[1], 16, Q), F32),
+            like((2, length, width), F32), like((length, width), BF16), like((length, 256), BF16),
+            like((length, 128), F32),
+            like((length, 256), F32), like((length, width), F32), like((chunks, 128, width), BF16),
+            like((length, width), BF16), like((length, model), BF16), like((length, model), BF16),
+            like((2, 2, 4, 2, depth, width), BF16), like((1, 2, 4, 2, depth, 2 * part), BF16),
+            like((2 * chunks, Q), F32), like((SMALL_ROWS, 128), F32), like((chunks, 16, Q), F32),
         ],
         scratch_shapes=[
             pltpu.VMEM((1, depth, part), BF16),
             pltpu.VMEM((8, 16, w_bc.shape[1]), F32),
             pltpu.VMEM((depth, w_bc.shape[1]), F32),
-            pltpu.VMEM((4, 3, SMALL_ROWS, 128), F32),
+            pltpu.VMEM((13, SMALL_ROWS, 128), F32),
             pltpu.VMEM((8, model), F32),
-            dma(7), dma(7), dma(7), dma(7), dma(31), dma(31), dma(31), dma(31), dma(10), dma(10), dma(3),
-        ],
-        name="gather",
-        compiler_params=remote_params(0),
-    )(hidden, *args)
-
-
-def forward_call(tok, small, hid_all, wxe, cotangent, w2):
-    length, model = hid_all.shape
-    total = wxe.shape[1]
-    depth, half = w2.shape[1], w2.shape[2]
-    width = 2 * half
-    steps = length // STEP_ROWS
-    chunks = length // Q
-
-    def early(i):
-        return jnp.minimum(i, steps - 1)
-
-    def late(i):
-        return jnp.maximum(i - steps, 0)
-
-    return pl.pallas_call(
-        forward_kernel,
-        grid=(2 * steps,),
-        in_specs=[whole(tok.shape), whole(small.shape), block(STEP_ROWS, model, early), whole(wxe.shape), ANY, ANY],
-        out_specs=[pl.BlockSpec((1, STEP_ROWS, width), lambda i: (i // steps, i % steps, 0)),
-                   block(STEP_ROWS, width, early), block(STEP_ROWS, 256, early),
-                   block(STEP_ROWS, 128, early), block(STEP_ROWS, 256, early), block(STEP_ROWS, width, early),
-                   pl.BlockSpec((STEP_ROWS // Q, 128, width), lambda i: (early(i), 0, 0)),
-                   block(STEP_ROWS, width, late), ANY, ANY, ANY, whole_out((2 * chunks, Q))],
-        out_shape=[
-            like((2, length, width), F32), like((length, width), BF16), like((length, 256), BF16),
-            like((length, 128), F32),
-            like((length, 256), F32), like((length, width), F32), like((chunks, 128, width), BF16),
-            like((length, width), BF16), like((length, model), BF16), like((length, model), BF16),
-            like((2, 2, 4, 2, depth, width), BF16), like((2 * chunks, Q), F32),
-        ],
-        scratch_shapes=[
+            pltpu.VMEM((width, 128), BF16),
             pltpu.VMEM((128, width), F32),
             pltpu.VMEM((Q + HALO, width), F32),
             pltpu.VMEM((Q + HALO, 256), F32),
-            pltpu.VMEM((STEP_ROWS, total), F32),
+            pltpu.VMEM((length, model), BF16),
+            pltpu.VMEM((1, 2, 4, 2, depth, 2 * part), BF16),
+            pltpu.VMEM((length, 2 * part), F32),
             pltpu.VMEM((length, model), BF16),
             pltpu.VMEM((2, 2, 4, 2, depth, width), BF16),
             pltpu.VMEM((length, model), BF16),
             pltpu.VMEM((length, width), F32),
             pltpu.VMEM((2 * chunks, Q), F32),
             pltpu.VMEM((3, 2 * chunks, Q), F32),
-            dma(7), dma(7), dma(31), dma(31), dma(3), dma(3), dma(5),
+            dma(RingGather.SEMS), dma(RingGather.SEMS), dma(7), dma(7), dma(31), dma(31), dma(31), dma(31), dma(13), dma(13),
+            dma(RingGather.SEMS), dma(RingGather.SEMS), dma(31), dma(31), dma(3), dma(3), dma(9),
         ],
         name="mix_forward",
         compiler_params=remote_params(1),
-    )(tok, small, hid_all, wxe, cotangent, w2)
+    )(hidden, cotangent, w2, *args)
 
 
 def backward_call(tok, stat, small, zx, gon, y, xin, bcin, dt, bcc, starts, cots, normed, w2, wxe):
@@ -1197,19 +1264,19 @@
                   block(STEP_ROWS, 256, mix),
                   pl.BlockSpec((STEP_ROWS // Q, 128, width), lambda i: (mix(i), 0, 0)), ANY, ANY, ANY, ANY],
         out_specs=[whole((2, Q, model)), whole((2, Q, model)), whole((depth, width)), whole((depth, total // 2)),
-                   whole((72, 128)), whole((2, depth, 128))],
+                   whole((72, 128)), whole((2, depth + 8, 128))],
         out_shape=[
             like((2, Q, model), BF16), like((2, Q, model), BF16), like((depth, width), F32),
-            like((depth, total // 2), F32), like((72, 128), F32), like((2, depth, 128), F32),
+            like((depth, total // 2), F32), like((72, 128), F32), like((2, depth + 8, 128), F32),
         ],
         scratch_shapes=[
+            pltpu.VMEM((width, 128), BF16),
             pltpu.VMEM((128, width), F32),
             pltpu.VMEM((Q + HALO, width), F32),
             pltpu.VMEM((Q + HALO, 256), F32),
             pltpu.VMEM((7, 8, width), F32),
             pltpu.VMEM((5, 8, 256), F32),
             pltpu.VMEM((2, 8, 128), F32),
-            pltpu.VMEM((8, model), F32),
             pltpu.VMEM((length, model), BF16),
             pltpu.VMEM((length, model), BF16),
             pltpu.VMEM((model, width), BF16),
@@ -1219,9 +1286,9 @@
             pltpu.VMEM((length, width), BF16),
             pltpu.VMEM((8, Q, model), BF16),
             pltpu.VMEM((2, 4, 2, depth, 2 * width), BF16),
-            pltpu.VMEM((4, 3, 72, 128), F32),
-            pltpu.VMEM((2, 4, depth, 128), F32),
-            dma(10), dma(10), dma(7), dma(7), dma(5),
+            pltpu.VMEM((13, 72, 128), F32),
+            pltpu.VMEM((2, 4, depth + 8, 128), F32),
+            dma(13), dma(13), dma(7), dma(7), dma(5),
             *RingScatter.scratch(model),
             *RingScatter.scratch(model),
             *PlaneSum.scratch(depth, 2 * width),
@@ -1262,7 +1329,7 @@
 
 
 def finish_kernel(
-    hid, cot, got, back, small, gzo, gxe, sums, bcs,
+    hid, cot, got, back, small, gain, gzo, gxe, sums, bcs,
     mixed, g_hid, g_gain, g_wz, g_wx, g_wdt, g_wbc, g_kx, g_kxb, g_kbc, g_kbcb, g_al, g_ds, g_db, g_og, g_wo,
 ):
     at = place()
@@ -1282,7 +1349,7 @@
             cot[s].astype(F32) + inv * hat - h * ((inv * inv * inv) * jnp.mean(hat * h, -1, keepdims=True))
         )
     g_wz[...] = gzo[:, 0:half]
-    g_wo[...] = gzo[:, half : 2 * half].T
+    g_wo[...] = gzo[:, half : 2 * half]
     g_wx[...] = gxe[:, 0:half]
     g_wdt[...] = gxe[:, half : half + 128].T[0:own_heads]
 
@@ -1290,17 +1357,15 @@
         width = values.shape[1]
         return pltpu.roll(values, lax.rem(width - start, width), 1)[:, 0:count]
 
-    def tall(row, count):
-        return jnp.broadcast_to(wide(sums, row, count), (8, count * 128))
-
     pairs = half // 64
-    g_gain[...] = cut(tall(IN_GAIN, model // 128), everyone * g_gain.shape[1], g_gain.shape[1])[0:1]
+    own = cut(bcs[0, depth : depth + 8] + bcs[1, depth : depth + 8], mp * g_gain.shape[1], g_gain.shape[1])
+    g_gain[...] = own[0:1] / gain[...].astype(F32)
     rows = jnp.concatenate([wide(sums, X_TAPS + t * pairs, pairs) for t in range(7)] + [jnp.zeros((1, 2 * half), F32)], 0)
     own = cut(rows, xl * half + dp * g_kx.shape[1], g_kx.shape[1])
     g_kx[...] = own[0:4]
     g_kxb[...] = own[4:5]
     g_og[...] = own[5:6]
-    per_head = head_sums(rows)
+    per_head = head_sums(rows, head_pick(2 * half))
     g_ds[...] = cut(per_head, xl * own_heads, own_heads)[6:7]
     per_head = jnp.concatenate([sums[64:72]], 0)
     per_head = cut(per_head, xl * own_heads, own_heads)
@@ -1311,26 +1376,26 @@
     own = cut(rows, everyone * 2, 128)
     g_kbc[...] = jnp.concatenate([own, jnp.zeros((120, 128), F32)], 0).T[0:2, 0:4]
     g_kbcb[...] = own[4:5, 0:2]
-    total = jnp.concatenate([bcs[0], bcs[1]], 1)
+    total = jnp.concatenate([bcs[0, 0:depth], bcs[1, 0:depth]], 1)
     g_wbc[...] = pltpu.roll(total, lax.rem(depth - mp * 12, depth), 0)[0:12]
 
 
-def finish_call(hidden, cotangent, got, back, small, gzo, gxe, sums, bcs, own_heads):
+def finish_call(hidden, cotangent, got, back, small, gain, gzo, gxe, sums, bcs, own_heads):
     depth, half = gzo.shape[0], gzo.shape[1] // 2
     shapes = [
         (hidden.shape, BF16), (hidden.shape, F32), ((1, hidden.shape[2] // 128), F32), ((depth, half), F32),
         ((depth, half), F32), ((own_heads, depth), F32), ((12, 256), F32), ((4, half // 16), F32),
         ((1, half // 16), F32), ((2, 4), F32), ((1, 2), F32), ((1, own_heads), F32), ((1, own_heads), F32),
-        ((1, own_heads), F32), ((1, half // 16), F32), ((half, depth), F32),
+        ((1, own_heads), F32), ((1, half // 16), F32), ((depth, half), F32),
     ]
     return pl.pallas_call(
         finish_kernel,
-        in_specs=[IN_VMEM] * 9,
+        in_specs=[IN_VMEM] * 10,
         out_specs=[IN_VMEM] * len(shapes),
         out_shape=[like(*shape) for shape in shapes],
         name="finish",
         compiler_params=pltpu.CompilerParams(vmem_limit_bytes=VMEM_LIMIT),
-    )(hidden, cotangent, got, back, small, gzo, gxe, sums, bcs)
+    )(hidden, cotangent, got, back, small, gain, gzo, gxe, sums, bcs)
 
 
 def local(
@@ -1347,23 +1412,23 @@
         norm_gain[None], conv_x, conv_x_bias[None], conv_bc.T, conv_bc_bias[None], out_gain[None],
         a_log[None], d_skip[None], dt_bias[None],
     ]
-    ids = segments.reshape(segments.shape[0], -1, Q)
-    hid_all, wxe_all, small, tok = gather_call(hidden, ids, w_x, w_dt.T, w_bc, small_args)
+    w2 = jnp.stack([w_z, w_out.T])
+    zx, xin, bcin, dt, bcc, y_out, starts, gon, normed, cot_all, w2_all, wxe_all, stat, small, tok = forward_call(
+        hidden, cotangent, w2, segments, w_x, w_dt.T, w_bc, small_args
+    )
     full_xe = wxe_all.reshape(model, lay.total)
-    w2 = jnp.stack([w_z, w_out.T])
-    zx, xin, bcin, dt, bcc, y_out, starts, gon, normed, cot_all, w2_all, stat = forward_call(
-        tok, small, hid_all, full_xe, cotangent, w2
-    )
     got_out, grad_normed, zo_sum, xe_sum, sums, bc_sum = backward_call(
         tok, stat, small, zx, gon, y_out, xin, bcin, dt, bcc, starts, cot_all, normed,
         w2_all.reshape(2, model, width), full_xe,
     )
     (
         mixed, g_hid, g_gain, g_wz, g_wx, g_wdt, g_wbc, g_kx, g_kxb, g_kbc, g_kbcb, g_al, g_ds, g_db, g_og, g_wo,
-    ) = finish_call(hidden, cotangent, got_out, grad_normed, small, zo_sum, xe_sum, sums, bc_sum, own_heads)
+    ) = finish_call(
+        hidden, cotangent, got_out, grad_normed, small, norm_gain[None], zo_sum, xe_sum, sums, bc_sum, own_heads
+    )
     return (
         mixed, g_hid, g_gain[0], g_wz, g_wx, g_wdt.T, g_wbc, g_kx, g_kxb[0], g_kbc.T, g_kbcb[0], g_al[0], g_ds[0],
-        g_db[0], g_og[0], g_wo,
+        g_db[0], g_og[0], g_wo.T,
     )
 
 

time: 204 us -> 181 us (0.89)
  Pallas kernels: 199 us -> 178 us
  local copies, waits for them, and re-layouts: 3.01 us -> 0 us
    pallas_call x3 -> x2, Pallas kernels: 101 us -> 86.3 us  [the longest x1 81.8 us: forward_call(): pl.pallas_call(forward_kernel, grid=(2 * steps + 1,), in_specs=[ANY, ANY,...]
    pallas_call x1, Pallas kernels: 97.6 us -> 91.8 us  [backward_call(): pl.pallas_call(backward_kernel, grid=(PRE + MIX + 1,), in_specs=[whole(to...]
    unnamed x2 -> x0, local copies, waits for them, and re-layouts: 3.01 us -> none
where the time goes in v3:
time: 181 us
  Pallas kernels  178 us (98%)
    pallas_call x1, Pallas kernels, backward_call(): pl.pallas_call(backward_kernel, grid=(PRE + MIX + 1,), in_specs=[whole(to...  91.8 us
    pallas_call x1, Pallas kernels, forward_call(): pl.pallas_call(forward_kernel, grid=(2 * steps + 1,), in_specs=[ANY, ANY,...  81.8 us
    pallas_call x1, Pallas kernels, finish_call(): pl.pallas_call(finish_kernel, in_specs=[IN_VMEM] * 10, out_specs=[IN_VMEM...  4.53 us

profile of v3, /device:TPU:0, one launch (start us, length us, event | category | flops | bytes accessed | tf_op | source)
XLA Modules:
  0.0 180.5 jit_solution(11087796479557634213)
XLA Ops:
  0.6 1.6 pad_maximum_fusion.w2_ref
  2.2 81.8 %mix_forward.1 = (f32[2,1024,768]{2,1,0:T(8,128)}, bf16[1024,768]{1,0:T(8,128)(2,1)}, bf16[1024,256]{1,0:T(8,128)(2,1)}, f32[1024,128]{1,0:T(8,128)}, f32[1024,2...) custom-call(bf16[2,128,1536]{2,1,0:T(8,128)(2,1)} %hid.3, ...), custom_call_target="tpu_custom_call" | custom-call | tf_op jit(solution)/shard_map/mix_forward/pallas_call | solution.py:1196
  84.0 91.8 %mix_backward.1 = (bf16[2,128,1536]{2,1,0:T(8,128)(2,1)}, bf16[2,128,1536]{2,1,0:T(8,128)(2,1)}, f32[96,768]{1,0:T(8,128)}, f32[96,640]{1,0:T(8,128)}, f32[72,128]{1,0:T(8,128)}, /*index=5*/f32[2,104,128]{2,1,0:T(8,128)}) custom-call(f32[8,16,128]{2,1,0:T(8,128)} %get-tuple-element.53.tok_ref, f32[16,128]{1,0:T(8,128)} %get-tuple-element.54.stat_ref, ...), custom_call_target="tpu_custom_call" | custom-call | tf_op jit(solution)/shard_map/mix_backward/pallas_call | solution.py:1257
  175.8 4.5 %finish.1 = (bf16[2,128,1536]{2,1,0:T(8,128)(2,1)}, f32[2,128,1536]{2,1,0:T(8,128)}, f32[1,12]{1,0:T(1,128)}, f32[96,384]{1,0:T(8,128)}, f32[96,384]{1,0:T(8,128...) custom-call(bf16[2,128,1536]{2,1,0:T(8,128)(2,1)} %hid.3, ...), custom_call_target="tpu_custom_call" | custom-call | tf_op jit(solution)/shard_map/finish/pallas_call | solution.py:1391
